TPU v7x, 32 devices: a whole 2x2x4 slice. The times are simulated.
32 devices in a mesh: phase: 2 (over x), shard: 16 (over z, y, core).
Axes of the slice: x: 2, y: 2, z: 4, core: 2. Of those that a mesh axis runs over, the one named last changes fastest.
Arguments:
- grid_fields: bfloat16 [2, 128, 128, 512], P(None, 'shard', 'phase'), may hold values from -6 to 6
- encode_weight: bfloat16 [512, 512], replicated, may hold values from -0.25 to 0.25
- encode_send: int32 [16, 16, 3], P('shard'), may hold values from 0 to 7
- encode_count: int32 [16, 16], P('shard'), may hold values from 0 to 3, as said below
- encode_target: int32 [16, 16, 3, 128], P('shard'), may hold values from -1 to 255, as said below
- edge_weight: bfloat16 [2, 512, 1024], P('phase'), may hold values from -0.25 to 0.25
- node_weight: bfloat16 [2, 1024, 512], P('phase'), may hold values from -0.1875 to 0.1875
- node_gain: float32 [2, 512], P('phase'), may hold values from 0.25 to 1.75
- mesh_send: int32 [16, 16, 4], P('shard'), may hold values from 0 to 255
- mesh_neighbour: int32 [4096, 8], P('shard'), may hold values from -1 to 319, as said below
- decode_weight: bfloat16 [512, 512], P(None, 'phase'), may hold values from -0.25 to 0.25
- decode_send: int32 [16, 16, 1], P('shard'), may hold values from 0 to 1
- decode_source: int32 [3, 16384], P(None, 'shard'), may hold values from 0 to 2047
- output_weight: bfloat16 [512, 227], P('phase'), may hold values from -0.25 to 0.25
- skip_weight: bfloat16 [512, 227], replicated, may hold values from -0.25 to 0.25
Outputs:
- forecast: float32 [2, 128, 128, 227], P(None, 'shard', 'phase')
Inputs may be any that keep to these rules, and one draw needn't show every extreme that they name: `encode_count`: slots at or past the count hold arbitrary blocks; such slots carry nothing. `encode_target`: -1 marks a row that feeds no node of that owner; entries of slots past the count are arbitrary. `mesh_neighbour`: entries below 256 name the owner's own nodes, larger ones a slot of the node rows received from another owner, -1 no edge.
All inputs are finite; a program needn't handle non-finite values.
Results may differ from a plain program's by a relative error of at most 0.012.
Values may be sent and summed in bfloat16 or wider, within the bound.
A program may use at most 64 MiB of HBM per device.

v0:
```python
import math

import jax
import jax.numpy as jnp
from jax import lax
from jax.sharding import PartitionSpec as P


def from_behind(value, axis, by):
    length = lax.axis_size(axis)
    pairs = [(i, i + by) for i in range(length) if 0 <= i + by < length]
    return lax.ppermute(value, axis, pairs)


def broadcast(block, axis, source):
    block = jnp.where(lax.axis_index(axis) == source, block, jnp.zeros_like(block))
    return lax.psum(block, axis)


def layer_norm(values):
    average = jnp.mean(values, axis=-1, keepdims=True)
    centred = values - average
    variance = jnp.mean(centred * centred, axis=-1, keepdims=True)
    return centred * lax.rsqrt(variance + 1e-05)


def add_by_target(values, targets, node_count):
    row_count, columns = values.shape
    block_rows = math.gcd(row_count, 2048)
    value_blocks = values.reshape(row_count // block_rows, block_rows, columns)
    target_blocks = targets.reshape(row_count // block_rows, block_rows)
    node_ids = jnp.arange(node_count, dtype=jnp.int32)

    def accumulate(running, pieces):
        onehot = (pieces[1][None, :] == node_ids[:, None]).astype(jnp.bfloat16)
        return (running + jnp.dot(onehot, pieces[0], preferred_element_type=jnp.float32), None)

    running, unused = lax.scan(
        accumulate, jnp.zeros((node_count, columns), jnp.float32), (value_blocks, target_blocks)
    )
    return running


def encode_sums(messages, send_blocks, slot_live, targets, node_count):
    picked = messages[send_blocks]
    picked = jnp.where(slot_live[:, :, None, None, None], picked, jnp.zeros_like(picked))
    arrived = lax.all_to_all(picked, "shard", split_axis=0, concat_axis=0, tiled=True)
    peer_count, capacity, part_rows, batches, columns = arrived.shape
    node_ids = jnp.where(targets >= 0, targets, node_count).reshape(-1)
    summed = add_by_target(
        arrived.reshape(peer_count * capacity * part_rows, batches * columns), node_ids, node_count
    )
    return jnp.transpose(summed.reshape(node_count, batches, columns), (1, 0, 2))


def on_device(
    grid_fields,
    encode_weight,
    encode_send,
    encode_count,
    encode_target,
    edge_weight,
    node_weight,
    node_gain,
    mesh_send,
    mesh_neighbour,
    decode_weight,
    decode_send,
    decode_source,
    output_weight,
    skip_weight,
):
    phases = lax.axis_size("phase")
    phase_index = lax.axis_index("phase")
    batches, blocks, part_rows, features = grid_fields.shape
    node_count = mesh_neighbour.shape[0]
    block_size = encode_target.shape[3]
    send_blocks = encode_send[0]
    capacity = send_blocks.shape[1]
    slot_live = jnp.arange(capacity, dtype=jnp.int32)[None, :] < encode_count[0][:, None]
    messages = jax.nn.silu(
        jnp.einsum("mgrd,dc->grmc", grid_fields, encode_weight, preferred_element_type=jnp.float32)
    ).astype(jnp.bfloat16)
    own_targets = lax.dynamic_slice_in_dim(encode_target[0], phase_index * part_rows, part_rows, 2)
    partial_sums = encode_sums(messages, send_blocks, slot_live, own_targets, node_count)
    encoded = lax.psum(partial_sums, "phase")
    initial = layer_norm(encoded).astype(jnp.bfloat16)
    my_edge = edge_weight[0]
    my_node = node_weight[0]
    my_gain = node_gain[0]
    send_nodes = mesh_send[0]
    edge_live = mesh_neighbour >= 0
    safe_index = jnp.where(edge_live, mesh_neighbour, 0)
    slot_count = mesh_neighbour.shape[1]

    def process(mesh_state):
        both_parts = jnp.dot(mesh_state, my_edge, preferred_element_type=jnp.float32)
        source_part = both_parts[:, :features].astype(jnp.bfloat16)
        dest_part = both_parts[:, features:]
        incoming = lax.all_to_all(
            source_part[send_nodes], "shard", split_axis=0, concat_axis=0, tiled=True
        )
        lookup_table = jnp.concatenate([source_part, incoming.reshape(-1, features)], axis=0)
        running = jnp.zeros((node_count, features), jnp.float32)
        for slot_index in range(slot_count):
            gathered = lookup_table[safe_index[:, slot_index]].astype(jnp.float32)
            running = running + jnp.where(
                edge_live[:, slot_index][:, None], jax.nn.silu(gathered + dest_part), 0.0
            )
        summary = running.astype(jnp.bfloat16)
        mixed = jnp.dot(mesh_state, my_node[:features], preferred_element_type=jnp.float32)
        mixed = mixed + jnp.dot(summary, my_node[features:], preferred_element_type=jnp.float32)
        return (mesh_state.astype(jnp.float32) + my_gain * layer_norm(jax.nn.silu(mixed))).astype(
            jnp.bfloat16
        )

    tick_count = batches + phases - 1

    def advance(carried, tick_index):
        current, finished = carried
        entering = lax.dynamic_index_in_dim(
            initial, jnp.minimum(tick_index, batches - 1), 0, keepdims=False
        )
        inputs = jnp.where(phase_index == 0, entering, current)
        result = process(inputs)
        leaving = tick_index - (phases - 1)
        updated = lax.dynamic_update_index_in_dim(finished, result, jnp.maximum(leaving, 0), 0)
        finished = jnp.where((phase_index == phases - 1) & (leaving >= 0), updated, finished)
        current = from_behind(result, "phase", 1)
        return ((current, finished), None)

    carried, unused = lax.scan(
        advance,
        (jnp.zeros_like(initial[0]), jnp.zeros_like(initial)),
        jnp.arange(tick_count, dtype=jnp.int32),
    )
    finished = carried[1]
    final_states = broadcast(finished, "phase", phases - 1)
    mapped = jnp.einsum(
        "mnd,dc->nmc", final_states, decode_weight, preferred_element_type=jnp.float32
    ).astype(jnp.bfloat16)
    columns = mapped.shape[2]
    node_blocks = mapped.reshape(node_count // block_size, block_size, batches, columns)
    outgoing = node_blocks[decode_send[0]]
    arrived = lax.all_to_all(outgoing, "shard", split_axis=0, concat_axis=0, tiled=True)
    arrived = arrived.reshape(-1, batches, columns)
    summed = arrived[decode_source[0]].astype(jnp.float32)
    summed = summed + arrived[decode_source[1]].astype(jnp.float32)
    summed = summed + arrived[decode_source[2]].astype(jnp.float32)
    hidden = jax.nn.silu(summed).astype(jnp.bfloat16)
    skipped = jnp.einsum(
        "mgrd,do->mgro", grid_fields, skip_weight, preferred_element_type=jnp.float32
    )
    output_terms = jnp.einsum(
        "rmc,co->mro", hidden, output_weight, preferred_element_type=jnp.float32
    )
    output_terms = output_terms.reshape(batches, blocks, block_size, output_terms.shape[2])
    shared = lax.psum_scatter(output_terms, "phase", scatter_dimension=2, tiled=True)
    return shared + skipped


def solution(mesh):
    return jax.shard_map(
        on_device,
        mesh=mesh,
        in_specs=(
            P(None, "shard", "phase", None),
            P(),
            P("shard", None, None),
            P("shard", None),
            P("shard", None, None, None),
            P("phase", None, None),
            P("phase", None, None),
            P("phase", None),
            P("shard", None, None),
            P("shard", None),
            P(None, "phase"),
            P("shard", None, None),
            P(None, "shard"),
            P("phase", None),
            P(),
        ),
        out_specs=P(None, "shard", "phase", None),
        check_vma=False,
    )
```

profile of v0, /device:TPU:10, one launch (start us, length us, event | category | flops | bytes accessed | tf_op | source)
XLA Modules:
  0.0 538.5 jit_solution(3840892488353764927)
XLA Ops:
  8.2 2.0 fusion.19
  10.3 4.9 gather_fusion.9
  15.2 5.9 %broadcast_select_fusion = bf16[16,3,64,2,512]{4,2,3,1,0:T(8,128)(2,1)} fusion(bf16[16,3,64,2,512]{4,2,3,1,0:T(8,128)(2,1)} %bitcast.145, pred[16,3]{1,0:T(8,128)(4,1)S(1)} %iota_compare_fusion.2), kind=kLoop, calls=%fused_computation.66 | loop fusion | flops 3145728 | bytes 12582960 | tf_op jit(solution)/shard_map/jit(_where)/select_n | solution.py:46
  21.1 6.4 %all-to-all-start.1 = ((bf16[16,3,64,2,512]{4,2,3,1,0:T(8,128)(2,1)}), bf16[16,3,64,2,512]{4,2,3,1,0:T(8,128)(2,1)}, u32[]{:S(2)}, u32[]{:S(2)}) async-start(bf16[16,3,64,2,512]{4,2,3,1,0:T(8,128)(2,1)} %broadcast_select_fusion), calls=%async_computation.1 | async-start | bytes 12582912 | tf_op jit(solution)/shard_map/all_to_all | solution.py:47
  27.8 135.5 %all-to-all-done.1 = bf16[16,3,64,2,512]{4,2,3,1,0:T(8,128)(2,1)} async-done(((bf16[16,3,64,2,512]{4,2,3,1,0:T(8,128)(2,1)}), bf16[16,3,64,2,512]{4,2,3,1,0:T(8,128)(2,1)}, u32[]{:S(2)}, u32[]{:S(2)}) %all-to-all-start.1) | async-done | bytes 6291488 | tf_op jit(solution)/shard_map/all_to_all | solution.py:47
  163.3 12.7 %copy.60 = bf16[16,3,64,2,512]{4,3,2,1,0:T(2,128)(2,1)} copy(bf16[16,3,64,2,512]{4,2,3,1,0:T(8,128)(2,1)} %all-to-all-done.1) | data formatting | bytes 12582912 | tf_op jit(solution)/shard_map/all_to_all | solution.py:47
  176.0 11.0 %reshape_reshape.4 = bf16[3,1024,1024]{2,1,0:T(8,128)(2,1)} reshape(bf16[16,3,64,2,512]{4,3,2,1,0:T(2,128)(2,1)} %copy.60) | data formatting | bytes 12582912 | tf_op jit(solution)/shard_map/reshape;reshape | solution.py:30
  187.0 7.8 %while.26 = (s32[]{:T(128)}, f32[256,1024]{1,0:T(8,128)S(1)}, s32[3,1024]{1,0:T(4,128)S(1)}, bf16[3,1024,1024]{2,1,0:T(8,128)(2,1)}, s32[]{:T(128)}, /*index=5*/s32[]{:T(128)}) while((s32[]{:T(128)}, f32[256,1024]{1,0:T(8,128)S(1)}, s32[3,1024]{1,0:T(4,128)S(1)}, bf16[3,1024,1024]{2,1,0:T(8,128)(2,1)}, s32[]{:T(128)}, ...), condition=%wide.region_1.2_spmd.clone, body=%wide.region_0.1_spmd.clone.sunk | while | flops 537657344 | bytes 4207187 | solution.py:38
  187.0 2.6 fusion.53
  189.6 2.6 fusion.53
  192.2 2.6 fusion.53
  196.2 40.4 %all-reduce.3.cloned.1.call-done = f32[2,256,512]{2,1,0:T(8,128)} async-done(((f32[2,256,512]{2,1,0:T(8,128)}), f32[2,256,512]{2,1,0:T(8,128)}) %all-reduce.3.cloned.1.call-update) | async-done | bytes 1048592 | tf_op jit(solution)/shard_map/psum | solution.py:86
  236.6 1.5 reduce_sum.42
  238.1 1.5 multiply_reduce_fusion.1
  241.4 128.4 %while.25 = (s32[]{:T(128)}, bf16[256,512]{1,0:T(8,128)(2,1)S(1)}, bf16[2,256,512]{2,1,0:T(8,128)(2,1)}, pred[]{:T(512)}, s32[3]{0:T(128)S(1)}, /*index=5*/bf16[...) while((s32[]{:T(128)}, bf16[256,512]{1,0:T(8,128)(2,1)S(1)}, ...), condition=%wide.region_8.9_spmd, body=%wide.region_5.8_spmd.sunk | while | flops 548158912 | bytes 26240440 | solution.py:132
  245.6 6.1 %all-to-all-start = ((bf16[16,4,512]{2,1,0:T(4,128)(2,1)}), bf16[16,4,512]{2,1,0:T(4,128)(2,1)S(1)}, u32[]{:S(2)}, u32[]{:S(2)}) async-start(bf16[16,4,512]{2,1,0:T(4,128)(2,1)} %reshape.418), calls=%async_computation | async-start | bytes 131072 | tf_op jit(solution)/shard_map/while/body/eval_jaxpr/all_to_all | solution.py:100
  251.8 2.2 fusion.48
  254.6 2.2 all-to-all-done
  259.1 1.9 gather_fusion.3
  261.0 1.9 gather_fusion.4
  262.9 1.9 gather_fusion.5
  264.7 1.9 gather_fusion.6
  266.6 1.9 gather_fusion.7
  268.5 1.9 gather_fusion.8
  270.3 3.4 fusion.50
  275.0 1.3 collective-permute-start
  276.3 8.9 %collective-permute-done = bf16[256,512]{1,0:T(8,128)(2,1)S(1)} collective-permute-done((bf16[256,512]{1,0:T(8,128)(2,1)S(1)}, bf16[256,512]{1,0:T(8,128)(2,1)S(1)}, u32[]{:S(2)}, u32[]{:S(2)}) %collective-permute-start) | collective-permute-done | bytes 262176 | tf_op jit(solution)/shard_map/while/body/eval_jaxpr/ppermute | solution.py:12
  289.3 4.6 all-to-all-start
  294.1 2.2 fusion.48
  296.9 2.3 all-to-all-done
  301.5 1.9 gather_fusion.3
  303.4 1.9 gather_fusion.4
  305.2 1.9 gather_fusion.5
  307.1 1.9 gather_fusion.6
  308.9 1.9 gather_fusion.7
  310.8 1.9 gather_fusion.8
  312.7 3.4 fusion.50
  317.3 1.3 collective-permute-start
  318.6 8.9 %collective-permute-done = bf16[256,512]{1,0:T(8,128)(2,1)S(1)} collective-permute-done((bf16[256,512]{1,0:T(8,128)(2,1)S(1)}, bf16[256,512]{1,0:T(8,128)(2,1)S(1)}, u32[]{:S(2)}, u32[]{:S(2)}) %collective-permute-start) | collective-permute-done | bytes 262176 | tf_op jit(solution)/shard_map/while/body/eval_jaxpr/ppermute | solution.py:12
  331.7 4.6 all-to-all-start
  336.4 2.2 fusion.48
  339.2 2.3 all-to-all-done
  343.8 1.9 gather_fusion.3
  345.7 1.9 gather_fusion.4
  347.6 1.9 gather_fusion.5
  349.4 1.9 gather_fusion.6
  351.3 1.9 gather_fusion.7
  353.2 1.9 gather_fusion.8
  355.0 3.4 fusion.50
  361.0 8.9 %collective-permute-done = bf16[256,512]{1,0:T(8,128)(2,1)S(1)} collective-permute-done((bf16[256,512]{1,0:T(8,128)(2,1)S(1)}, bf16[256,512]{1,0:T(8,128)(2,1)S(1)}, u32[]{:S(2)}, u32[]{:S(2)}) %collective-permute-start) | collective-permute-done | bytes 262176 | tf_op jit(solution)/shard_map/while/body/eval_jaxpr/ppermute | solution.py:12
  369.9 1.9 broadcast_select_fusion.1
  371.8 26.5 %all-reduce.5.cloned.1.call-done = bf16[2,256,512]{2,1,0:T(8,128)(2,1)} async-done(((bf16[2,256,512]{2,1,0:T(8,128)(2,1)}), bf16[2,256,512]{2,1,0:T(8,128)(2,1)}) %all-reduce.5.cloned.1.call-update) | async-done | bytes 524304 | tf_op jit(solution)/shard_map/psum | solution.py:17
  398.3 1.4 convolution_convert_fusion
  399.8 2.0 gather_fusion.10
  401.8 6.2 %all-to-all-start.2 = ((bf16[16,1,128,2,256]{4,2,3,1,0:T(8,128)(2,1)}), bf16[16,1,128,2,256]{4,2,3,1,0:T(8,128)(2,1)S(1)}, u32[]{:S(2)}, u32[]{:S(2)}) async-start(bf16[16,1,128,2,256]{4,2,3,1,0:T(8,128)(2,1)} %bitcast.146), calls=%async_computation.2 | async-start | bytes 4194304 | tf_op jit(solution)/shard_map/all_to_all | solution.py:145
  408.3 45.5 %all-to-all-done.2 = bf16[16,1,128,2,256]{4,2,3,1,0:T(8,128)(2,1)S(1)} async-done(((bf16[16,1,128,2,256]{4,2,3,1,0:T(8,128)(2,1)}), bf16[16,1,128,2,256]{4,2,3,1,0:T(8,128)(2,1)S(1)}, u32[]{:S(2)}, u32[]{:S(2)}) %all-to-all-start.2) | async-done | bytes 2097184 | tf_op jit(solution)/shard_map/all_to_all | solution.py:145
  454.0 12.8 %copy.65 = bf16[2048,2,256]{2,1,0:T(2,128)(2,1)S(1)} copy(bf16[2048,2,256]{2,0,1:T(8,128)(2,1)S(1)} %bitcast.148) | data formatting | bytes 4194304 | tf_op jit(solution)/shard_map/reshape | solution.py:146
  466.8 8.5 %gather_fusion.11 = bf16[1024,2,256]{2,1,0:T(2,128)(2,1)} fusion(bf16[2048,2,256]{2,1,0:T(2,128)(2,1)S(1)} %copy.65, s32[1024]{0:T(1024)S(1)} %broadcast_clamp_fusion.2), kind=kCustom, calls=%fused_computation.11 | custom fusion | bytes 2101248 | tf_op jit(solution)/shard_map/gather | solution.py:147
  475.3 8.5 %gather_fusion.12 = bf16[1024,2,256]{2,1,0:T(2,128)(2,1)} fusion(bf16[2048,2,256]{2,1,0:T(2,128)(2,1)S(1)} %copy.65, s32[1024]{0:T(1024)S(1)} %broadcast_clamp_fusion.1), kind=kCustom, calls=%fused_computation.12 | custom fusion | bytes 2101248 | tf_op jit(solution)/shard_map/gather | solution.py:148
  483.8 8.5 %gather_fusion.13 = bf16[1024,2,256]{2,1,0:T(2,128)(2,1)} fusion(bf16[2048,2,256]{2,1,0:T(2,128)(2,1)S(1)} %copy.65, s32[1024]{0:T(1024)S(1)} %broadcast_clamp_fusion), kind=kCustom, calls=%fused_computation.13 | custom fusion | bytes 2101248 | tf_op jit(solution)/shard_map/gather | solution.py:149
  492.3 2.7 convolution_bitcast_fusion
  495.0 1.9 copy.74
  496.9 32.4 %reduce-scatter.2.cloned.1.call-done = f32[2,8,64,227]{3,2,1,0:T(8,128)} async-done(((f32[2,8,128,227]{3,2,1,0:T(8,128)}), f32[2,8,64,227]{3,2,1,0:T(8,128)}) %reduce-scatter.2.cloned.1.call-update) | async-done | bytes 929808 | tf_op jit(solution)/shard_map/reduce_scatter | solution.py:158
  529.3 2.7 convolution_add_fusion.1
  (161 shorter events, 28.6 us)
Async XLA Ops:
  6.5 1.7 copy-start
  21.1 6.5 %copy-start.10 = (s32[1,16,3,128]{3,1,2,0:T(8,128)S(1)}, s32[1,16,3,128]{3,1,2,0:T(8,128)}, u32[]{:S(2)}) copy-start(s32[1,16,3,128]{3,1,2,0:T(8,128)} %param.23) | copy-start | bytes 73732
  21.1 142.2 %all-to-all-start.1 = ((bf16[16,3,64,2,512]{4,2,3,1,0:T(8,128)(2,1)}), bf16[16,3,64,2,512]{4,2,3,1,0:T(8,128)(2,1)}, u32[]{:S(2)}, u32[]{:S(2)}) async-start(bf16[16,3,64,2,512]{4,2,3,1,0:T(8,128)(2,1)} %broadcast_select_fusion), calls=%async_computation.1 | async-start | bytes 12582912 | tf_op jit(solution)/shard_map/all_to_all | solution.py:47
  27.6 209.0 %all-reduce.3.cloned.1.call-start = ((), (), s32[]{:S(2)}) async-start(), calls=%async_computation.4 | async-start | bytes 2097152 | tf_op jit(solution)/shard_map/psum | solution.py:86
  194.8 1.3 copy-start.9
  195.9 202.5 %all-reduce.5.cloned.1.call-start = ((), (), s32[]{:S(2)}) async-start(), calls=%async_computation.5 | async-start | bytes 1048576 | tf_op jit(solution)/shard_map/psum | solution.py:17
  196.2 45.3 %copy-start.1 = (bf16[1,512,1024]{2,1,0:T(8,128)(2,1)S(1)}, bf16[1,512,1024]{2,1,0:T(8,128)(2,1)}, u32[]{:S(2)}) copy-start(bf16[1,512,1024]{2,1,0:T(8,128)(2,1)} %param.24) | copy-start | bytes 3145732
  196.2 45.2 %copy-start.7 = (f32[1,512]{1,0:T(1,128)S(1)}, f32[1,512]{1,0:T(1,128)}, u32[]{:S(2)}) copy-start(f32[1,512]{1,0:T(1,128)} %param.26) | copy-start | bytes 6148
  196.2 45.2 %copy-start.8 = (s32[1,16,4]{1,2,0:T(4,128)S(1)}, s32[1,16,4]{1,2,0:T(4,128)}, u32[]{:S(2)}) copy-start(s32[1,16,4]{1,2,0:T(4,128)} %param.27) | copy-start | bytes 772
  236.6 3.0 copy-start.5
  241.4 130.4 %copy-start.13 = (s32[1,16,1]{1,2,0:T(1,128)S(1)}, s32[1,16,1]{1,2,0:T(1,128)}, u32[]{:S(2)}) copy-start(s32[1,16,1]{1,2,0:T(1,128)} %param.30) | copy-start | bytes 196
  245.6 11.2 %all-to-all-start = ((bf16[16,4,512]{2,1,0:T(4,128)(2,1)}), bf16[16,4,512]{2,1,0:T(4,128)(2,1)S(1)}, u32[]{:S(2)}, u32[]{:S(2)}) async-start(bf16[16,4,512]{2,1,0:T(4,128)(2,1)} %reshape.418), calls=%async_computation | async-start | bytes 131072 | tf_op jit(solution)/shard_map/while/body/eval_jaxpr/all_to_all | solution.py:100
  270.3 3.6 copy-start.3
  273.7 11.5 %copy-start.2 = (bf16[1,512,1024]{2,1,0:T(8,128)(2,1)S(1)}, bf16[1,512,1024]{2,1,0:T(8,128)(2,1)}, u32[]{:S(2)}) copy-start(bf16[1,512,1024]{2,1,0:T(8,128)(2,1)} %get-tuple-element.505) | copy-start | bytes 3145732 | tf_op jit(solution)/shard_map/while
  274.2 0.8 copy-start.4
  275.0 10.2 %collective-permute-start = (bf16[256,512]{1,0:T(8,128)(2,1)S(1)}, bf16[256,512]{1,0:T(8,128)(2,1)S(1)}, u32[]{:S(2)}, u32[]{:S(2)}) collective-permute-start(bf16[256,512]{1,0:T(8,128)(2,1)S(1)} %get-tuple-element.402), channel_id=1, source_target_pairs={{0,16},{1,17},{2,18},{3,19},{4,20},{5,21},{6,22},{7,23},{8,24},{9,... | collective-permute-start | bytes 786440 | tf_op jit(solution)/shard_map/while/body/eval_jaxpr/ppermute | solution.py:12
  289.3 9.8 %all-to-all-start = ((bf16[16,4,512]{2,1,0:T(4,128)(2,1)}), bf16[16,4,512]{2,1,0:T(4,128)(2,1)S(1)}, u32[]{:S(2)}, u32[]{:S(2)}) async-start(bf16[16,4,512]{2,1,0:T(4,128)(2,1)} %reshape.418), calls=%async_computation | async-start | bytes 131072 | tf_op jit(solution)/shard_map/while/body/eval_jaxpr/all_to_all | solution.py:100
  312.7 3.6 copy-start.3
  316.0 11.5 %copy-start.2 = (bf16[1,512,1024]{2,1,0:T(8,128)(2,1)S(1)}, bf16[1,512,1024]{2,1,0:T(8,128)(2,1)}, u32[]{:S(2)}) copy-start(bf16[1,512,1024]{2,1,0:T(8,128)(2,1)} %get-tuple-element.505) | copy-start | bytes 3145732 | tf_op jit(solution)/shard_map/while
  316.5 0.8 copy-start.4
  317.3 10.2 %collective-permute-start = (bf16[256,512]{1,0:T(8,128)(2,1)S(1)}, bf16[256,512]{1,0:T(8,128)(2,1)S(1)}, u32[]{:S(2)}, u32[]{:S(2)}) collective-permute-start(bf16[256,512]{1,0:T(8,128)(2,1)S(1)} %get-tuple-element.402), channel_id=1, source_target_pairs={{0,16},{1,17},{2,18},{3,19},{4,20},{5,21},{6,22},{7,23},{8,24},{9,... | collective-permute-start | bytes 786440 | tf_op jit(solution)/shard_map/while/body/eval_jaxpr/ppermute | solution.py:12
  331.7 9.8 %all-to-all-start = ((bf16[16,4,512]{2,1,0:T(4,128)(2,1)}), bf16[16,4,512]{2,1,0:T(4,128)(2,1)S(1)}, u32[]{:S(2)}, u32[]{:S(2)}) async-start(bf16[16,4,512]{2,1,0:T(4,128)(2,1)} %reshape.418), calls=%async_computation | async-start | bytes 131072 | tf_op jit(solution)/shard_map/while/body/eval_jaxpr/all_to_all | solution.py:100
  355.0 3.6 copy-start.3
  358.4 11.5 %copy-start.2 = (bf16[1,512,1024]{2,1,0:T(8,128)(2,1)S(1)}, bf16[1,512,1024]{2,1,0:T(8,128)(2,1)}, u32[]{:S(2)}) copy-start(bf16[1,512,1024]{2,1,0:T(8,128)(2,1)} %get-tuple-element.505) | copy-start | bytes 3145732 | tf_op jit(solution)/shard_map/while
  358.9 0.8 copy-start.4
  359.7 10.2 %collective-permute-start = (bf16[256,512]{1,0:T(8,128)(2,1)S(1)}, bf16[256,512]{1,0:T(8,128)(2,1)S(1)}, u32[]{:S(2)}, u32[]{:S(2)}) collective-permute-start(bf16[256,512]{1,0:T(8,128)(2,1)S(1)} %get-tuple-element.402), channel_id=1, source_target_pairs={{0,16},{1,17},{2,18},{3,19},{4,20},{5,21},{6,22},{7,23},{8,24},{9,... | collective-permute-start | bytes 786440 | tf_op jit(solution)/shard_map/while/body/eval_jaxpr/ppermute | solution.py:12
  401.8 6.5 %copy-start.11 = (s32[3,1024]{1,0:T(4,128)S(1)}, s32[3,1024]{1,0:T(4,128)}, u32[]{:S(2)}) copy-start(s32[3,1024]{1,0:T(4,128)} %param.31) | copy-start | bytes 36868
  401.8 52.1 %all-to-all-start.2 = ((bf16[16,1,128,2,256]{4,2,3,1,0:T(8,128)(2,1)}), bf16[16,1,128,2,256]{4,2,3,1,0:T(8,128)(2,1)S(1)}, u32[]{:S(2)}, u32[]{:S(2)}) async-start(bf16[16,1,128,2,256]{4,2,3,1,0:T(8,128)(2,1)} %bitcast.146), calls=%async_computation.2 | async-start | bytes 4194304 | tf_op jit(solution)/shard_map/all_to_all | solution.py:145
  408.0 121.3 %reduce-scatter.2.cloned.1.call-start = ((), (), s32[]{:S(2)}) async-start(), calls=%async_computation.6 | async-start | bytes 3145728 | tf_op jit(solution)/shard_map/reduce_scatter | solution.py:158
  475.3 17.0 %copy-start.12 = (bf16[256,227]{0,1:T(8,128)(2,1)S(1)}, bf16[256,227]{0,1:T(8,128)(2,1)}, u32[]{:S(2)}) copy-start(bf16[256,227]{0,1:T(8,128)(2,1)} %param.32) | copy-start | bytes 348676
  495.0 34.3 %copy-start.6 = (bf16[512,227]{0,1:T(8,128)(2,1)S(1)}, bf16[512,227]{0,1:T(8,128)(2,1)}, u32[]{:S(2)}) copy-start(bf16[512,227]{0,1:T(8,128)(2,1)} %param.33) | copy-start | bytes 697348
Sparse Core Ops, SparseCore 0:
  196.0 40.5 all-reduce.2
  371.9 26.3 all-reduce.4
  497.0 32.2 reduce-scatter.1
where the time goes:
time: 542 us; the launch traced here: 538 us
  waiting for transfers between devices  314 us (58%)
  local copies, waits for them, and re-layouts  123 us (23%)
  matrix products  34.4 us (6%)
  starting transfers between devices  32.4 us (6%)
  other arithmetic  17.8 us (3%)
  between operations  13.4 us (2%)
    all_to_all x1, waiting for transfers between devices, encode_sums(): lax.all_to_all(picked, 'shard', split_axis=0, concat_axis=0, tiled=True)  135 us
    all_to_all x1, waiting for transfers between devices, on_device(): lax.all_to_all(outgoing, 'shard', split_axis=0, concat_axis=0, tiled=True)  45.5 us
    gather x24, local copies, waits for them, and re-layouts, process(): gathered = lookup_table[safe_index[:, slot_index]].astype(jnp.float32)  40.4 us
    psum x1, waiting for transfers between devices, on_device(): encoded = lax.psum(partial_sums, 'phase')  40.4 us
    reduce_scatter x1, waiting for transfers between devices, on_device(): lax.psum_scatter(output_terms, 'phase', scatter_dimension=2, tiled=True)  32.4 us
    ppermute x3, waiting for transfers between devices, from_behind(): return lax.ppermute(value, axis, pairs)  26.8 us
    psum x1, waiting for transfers between devices, broadcast(): return lax.psum(block, axis)  26.5 us
    all_to_all x3, starting transfers between devices, process(): lax.all_to_all(source_part[send_nodes], 'shard', split_axis=0, concat_axi...  15.4 us
  transfers between devices with their start and end apart: 11, of which 11 were waited for; matrix products, arithmetic and copies ran while one was open for 1% of the time, Pallas kernels for 0%

commit v1 on v0

--- a/solution.py
+++ b/solution.py
@@ -53,7 +53,7 @@
     return jnp.transpose(summed.reshape(node_count, batches, columns), (1, 0, 2))
 
 
-def on_device(
+def on_device_sections(
     grid_fields,
     encode_weight,
     encode_send,
@@ -159,6 +159,140 @@
     return shared + skipped
 
 
+def swap(value):
+    return lax.ppermute(value, "phase", [(0, 1), (1, 0)])
+
+
+def sum_to_owners(partial_sums):
+    return lax.psum_scatter(partial_sums, "shard", scatter_dimension=0, tiled=True)[0]
+
+
+def gather_nodes(mapped):
+    return lax.all_gather(mapped, "shard", axis=0, tiled=False)
+
+
+def one_hot(indices, count, live):
+    hot = (indices[..., None] == jnp.arange(count, dtype=jnp.int32)) & live[..., None]
+    return hot.astype(jnp.bfloat16)
+
+
+def on_device_batches(
+    grid_fields,
+    encode_weight,
+    encode_send,
+    encode_count,
+    encode_target,
+    edge_weight,
+    node_weight,
+    node_gain,
+    mesh_send,
+    mesh_neighbour,
+    decode_weight,
+    decode_send,
+    decode_source,
+    output_weight,
+    skip_weight,
+):
+    phase_index = lax.axis_index("phase")
+    owners = lax.axis_size("shard")
+    batches, blocks, part_rows, features = grid_fields.shape
+    node_count, slot_count = mesh_neighbour.shape
+    block_size = encode_target.shape[3]
+    send_blocks = encode_send[0]
+    capacity = send_blocks.shape[1]
+
+    messages = jax.nn.silu(
+        jnp.einsum("mgrd,dc->mgrc", grid_fields, encode_weight, preferred_element_type=jnp.float32)
+    ).astype(jnp.bfloat16)
+    own = lax.dynamic_index_in_dim(messages, phase_index, 0, keepdims=False)
+    away = lax.dynamic_index_in_dim(messages, 1 - phase_index, 0, keepdims=False)
+    came = swap(away)
+    rows = jnp.concatenate([own, came], axis=1)
+
+    tables = jnp.concatenate(
+        [encode_target[0].reshape(owners, -1), decode_send[0].reshape(owners, -1)], axis=1
+    )
+    tables = lax.all_to_all(tables, "shard", split_axis=0, concat_axis=0, tiled=True)
+    targets = tables[:, : capacity * block_size].reshape(owners, capacity, 2, part_rows)
+    decode_block = tables[:, capacity * block_size :]
+    targets = jnp.where(phase_index == 0, targets, targets[:, :, ::-1])
+    targets = targets.reshape(owners, capacity * block_size)
+    slot_live = jnp.arange(capacity, dtype=jnp.int32)[None, :] < encode_count[0][:, None]
+    live = jnp.repeat(slot_live, block_size, axis=1)
+    targets = jnp.where(live, targets, -1)
+    hot = targets[:, None, :] == jnp.arange(node_count, dtype=jnp.int32)[None, :, None]
+    picked = rows[send_blocks].reshape(owners, capacity * block_size, features)
+    partial_sums = jnp.einsum(
+        "onr,orc->onc", hot.astype(jnp.bfloat16), picked, preferred_element_type=jnp.float32
+    ).astype(jnp.bfloat16)
+    encoded = sum_to_owners(partial_sums).astype(jnp.float32)
+    states = layer_norm(encoded).astype(jnp.bfloat16)
+
+    other_edge, other_node, other_gain = swap(edge_weight[0]), swap(node_weight[0]), swap(node_gain[0])
+    decode_all = jnp.concatenate([decode_weight, swap(decode_weight)], axis=1)
+    output_all = jnp.concatenate([output_weight, swap(output_weight)], axis=0)
+
+    edge_live = mesh_neighbour.T >= 0
+    remote = owners * mesh_send.shape[2]
+    source_hot = one_hot(mesh_neighbour.T, node_count + remote, edge_live)
+    send_nodes = mesh_send[0].reshape(-1)
+    send_hot = one_hot(send_nodes, node_count, send_nodes >= 0)
+    for layer in range(2):
+        mine = phase_index == layer
+        edge = jnp.where(mine, edge_weight[0], other_edge)
+        node = jnp.where(mine, node_weight[0], other_node)
+        gain = jnp.where(mine, node_gain[0], other_gain)
+        both_parts = jnp.dot(states, edge, preferred_element_type=jnp.float32)
+        source_part = both_parts[:, :features].astype(jnp.bfloat16)
+        dest_part = both_parts[:, features:]
+        outgoing = jnp.dot(send_hot, source_part, preferred_element_type=jnp.float32)
+        outgoing = outgoing.astype(jnp.bfloat16).reshape(owners, -1, features)
+        incoming = lax.all_to_all(outgoing, "shard", split_axis=0, concat_axis=0, tiled=True)
+        table = jnp.concatenate([source_part, incoming.reshape(-1, features)], axis=0)
+        running = jnp.zeros((node_count, features), jnp.float32)
+        for slot_index in range(slot_count):
+            gathered = jnp.dot(source_hot[slot_index], table, preferred_element_type=jnp.float32)
+            running = running + jnp.where(
+                edge_live[slot_index][:, None], jax.nn.silu(gathered + dest_part), 0.0
+            )
+        summary = running.astype(jnp.bfloat16)
+        mixed = jnp.dot(states, node[:features], preferred_element_type=jnp.float32)
+        mixed = mixed + jnp.dot(summary, node[features:], preferred_element_type=jnp.float32)
+        states = (states.astype(jnp.float32) + gain * layer_norm(jax.nn.silu(mixed))).astype(
+            jnp.bfloat16
+        )
+    mapped = jnp.dot(states, decode_all, preferred_element_type=jnp.float32).astype(jnp.bfloat16)
+
+    gathered = gather_nodes(mapped).reshape(owners, node_count // block_size, block_size, features)
+    chosen = gathered[jnp.arange(owners), decode_block[:, 0]].reshape(owners * block_size, features)
+    cells = decode_source.reshape(3, blocks, 2, part_rows)
+
+    def outputs(half):
+        indices = lax.dynamic_index_in_dim(cells, half, 2, keepdims=False).reshape(3, -1)
+        ids = jnp.arange(owners * block_size, dtype=jnp.int32)[None, :]
+        counts = sum((indices[e][:, None] == ids).astype(jnp.float32) for e in range(3))
+        summed = jnp.dot(counts.astype(jnp.bfloat16), chosen, preferred_element_type=jnp.float32)
+        hidden = jax.nn.silu(summed).astype(jnp.bfloat16)
+        return jnp.dot(hidden, output_all, preferred_element_type=jnp.float32)
+
+    leaving = outputs(1 - phase_index).astype(jnp.bfloat16)
+    arriving = swap(leaving).astype(jnp.float32)
+    kept = outputs(phase_index)
+    skipped = jnp.einsum(
+        "mgrd,do->mgro", grid_fields, skip_weight, preferred_element_type=jnp.float32
+    )
+    here = (jnp.arange(2) == phase_index)[:, None, None, None]
+    shape = (1, blocks, part_rows, kept.shape[1])
+    return jnp.where(here, kept.reshape(shape), arriving.reshape(shape)) + skipped
+
+
+def on_device(grid_fields, *others):
+    phases, batches = lax.axis_size("phase"), grid_fields.shape[0]
+    if phases == batches == 2 and others[10].shape[2] == 1:
+        return on_device_batches(grid_fields, *others)
+    return on_device_sections(grid_fields, *others)
+
+
 def solution(mesh):
     return jax.shard_map(
         on_device,

time: 542 us -> 242 us (0.45)
  waiting for transfers between devices: 314 us -> 129 us
  local copies, waits for them, and re-layouts: 123 us -> 14.7 us
  matrix products: 34.4 us -> 51.6 us
  other arithmetic: 17.8 us -> 7.01 us
  starting transfers between devices: 32.4 us -> 24 us
    all_to_all x5 -> x3, waiting for transfers between devices: 188 us -> 9.98 us  [the longest x2 5.27 us: on_device_batches(): lax.all_to_all(outgoing, 'shard', split_axis=0, concat_axis=0, tiled=True)]
    gather x35 -> x2, local copies, waits for them, and re-layouts: 76.9 us -> 7.85 us  [the longest x1 4.94 us: on_device_batches(): picked = rows[send_blocks].reshape(owners, capacity * block_size, features)]
    psum x2 -> x0, waiting for transfers between devices: 66.9 us -> none  [the longest x1 40.4 us: on_device(): encoded = lax.psum(partial_sums, 'phase')]
    all_gather x0 -> x1, waiting for transfers between devices: none -> 44.1 us  [gather_nodes(): return lax.all_gather(mapped, 'shard', axis=0, tiled=False)]
    ppermute x3 -> x7, waiting for transfers between devices: 26.8 us -> 49.9 us  [swap(): return lax.ppermute(value, 'phase', [(0, 1), (1, 0)])]
    dot_general x16 -> x28, matrix products: 34.4 us -> 51.6 us  [the longest x14 15.6 us: on_device_batches(): jnp.dot(source_hot[slot_index], table, preferred_element_type=jnp.float32)]
    reshape x7, local copies, waits for them, and re-layouts: 15.8 us -> 1.63 us  [the longest x2 1.3 us: on_device_batches(): outgoing = outgoing.astype(jnp.bfloat16).reshape(owners, -1, features)]
    all_to_all x2 -> x1, local copies, waits for them, and re-layouts: 12.8 us -> 0.65 us  [on_device_batches(): lax.all_to_all(tables, 'shard', split_axis=0, concat_axis=0, tiled=True)]
  transfers between devices with their start and end apart: 11 -> 12, of which waited for: 11 -> 9; matrix products, arithmetic and copies ran while one was open for 1% -> 13% of each run, Pallas kernels for 0% -> 0%
where the time goes in v1:
time: 242 us; the launch traced here: 240 us
  waiting for transfers between devices  129 us (53%)
  matrix products  51.6 us (21%)
  starting transfers between devices  24 us (10%)
  local copies, waits for them, and re-layouts  14.7 us (6%)
  between operations  13.8 us (6%)
  other arithmetic  7.01 us (3%)
    ppermute x7, waiting for transfers between devices, swap(): return lax.ppermute(value, 'phase', [(0, 1), (1, 0)])  49.9 us
    all_gather x1, waiting for transfers between devices, gather_nodes(): return lax.all_gather(mapped, 'shard', axis=0, tiled=False)  44.1 us
    reduce_scatter x1, waiting for transfers between devices, sum_to_owners(): lax.psum_scatter(partial_sums, 'shard', scatter_dimension=0, tiled=True)[0]  24.6 us
    dot_general x14, matrix products, on_device_batches(): jnp.dot(source_hot[slot_index], table, preferred_element_type=jnp.float32)  15.6 us
    all_to_all x2, starting transfers between devices, on_device_batches(): lax.all_to_all(outgoing, 'shard', split_axis=0, concat_axis=0, tiled=True)  10.1 us
    dot_general x2, matrix products, on_device_batches(): jnp.dot(summary, node[features:], preferred_element_type=jnp.float32)  8.86 us
    ppermute x7, starting transfers between devices, swap(): return lax.ppermute(value, 'phase', [(0, 1), (1, 0)])  7.38 us
    dot_general x1, matrix products, on_device_batches(): jnp.einsum('onr,orc->onc', hot.astype(jnp.bfloat16), picked, preferred_el...  7.16 us
  transfers between devices with their start and end apart: 12, of which 9 were waited for; matrix products, arithmetic and copies ran while one was open for 13% of the time, Pallas kernels for 0%

profile of v1, /device:TPU:10, one launch (start us, length us, event | category | flops | bytes accessed | tf_op | source)
XLA Modules:
  0.0 239.7 jit_solution(2774071081673878128)
XLA Ops:
  6.5 1.2 copy-done
  7.8 2.1 multiply_convert_fusion
  10.0 0.6 collective-permute-start
  10.7 0.6 copy.35
  11.3 6.3 %all-to-all-start = ((s32[16,1,385]{2,1,0:T(1,128)}), s32[16,1,385]{2,1,0:T(1,128)S(1)}, u32[]{:S(2)}, u32[]{:S(2)}) async-start(s32[16,1,385]{2,1,0:T(1,128)} %copy.35), calls=%async_computation | async-start | bytes 65536 | tf_op jit(solution)/shard_map/all_to_all | solution.py:215
  18.0 4.7 %all-to-all-done = s32[16,1,385]{2,1,0:T(1,128)S(1)} async-done(((s32[16,1,385]{2,1,0:T(1,128)}), s32[16,1,385]{2,1,0:T(1,128)S(1)}, u32[]{:S(2)}, u32[]{:S(2)}) %all-to-all-start) | async-done | bytes 24672 | tf_op jit(solution)/shard_map/all_to_all | solution.py:215
  23.2 0.5 collective-permute-done
  23.8 4.9 %gather_fusion = bf16[48,128,512]{2,1,0:T(8,128)(2,1)} fusion(bf16[8,128,512]{2,1,0:T(8,128)(2,1)S(1)} %pad_maximum_fusion, s32[1024]{0:T(1024)S(1)} %pad_clamp_fusion), kind=kCustom, calls=%fused_computation | custom fusion | bytes 12583104 | tf_op jit(solution)/shard_map/gather | solution.py:224
  28.7 7.2 %fusion.3 = bf16[16,256,512]{2,1,0:T(8,128)(2,1)} fusion(bf16[16,384,512]{2,1,0:T(8,128)(2,1)} %bitcast.116, s32[16,384]{1,0:T(8,128)S(1)} %bitcast_select_fusion), kind=kOutput, calls=%fused_computation.15 | convolution fusion | flops 1614282752 | bytes 10510336 | tf_op jit(solution)/shard_map/onr,orc->onc/dot_general | solution.py:225
  35.9 1.2 copy-done.1
  37.1 1.0 collective-permute-start.3
  38.1 1.0 collective-permute-start.2
  39.1 1.0 collective-permute-start.1
  40.3 0.7 fusion.2
  41.1 0.6 slice_reduce_fusion.7
  41.7 42.7 %collective-permute-done.1 = f32[512]{0:T(512)S(1)} collective-permute-done((f32[512]{0:T(512)S(1)}, f32[512]{0:T(512)S(1)}, u32[]{:S(2)}, u32[]{:S(2)}) %collective-permute-start.1) | collective-permute-done | bytes 2080 | tf_op jit(solution)/shard_map/ppermute | solution.py:163
  84.4 24.6 %reduce-scatter.2.cloned.1.call-done = bf16[1,256,512]{2,1,0:T(8,128)(2,1)} async-done(((bf16[16,256,512]{2,1,0:T(8,128)(2,1)}), bf16[1,256,512]{2,1,0:T(8,128)(2,1)}) %reduce-scatter.2.cloned.1.call-update) | async-done | bytes 262160 | tf_op jit(solution)/shard_map/reduce_scatter | solution.py:167
  109.0 1.1 convert_reduce_fusion
  110.1 1.2 fusion.22
  111.2 2.1 fusion.15
  113.4 0.2 convolution_convert_fusion.3
  113.6 0.7 reshape.163
  114.2 4.9 %all-to-all-start.1 = ((bf16[16,4,512]{2,1,0:T(4,128)(2,1)}), bf16[16,4,512]{2,1,0:T(4,128)(2,1)S(1)}, u32[]{:S(2)}, u32[]{:S(2)}) async-start(bf16[16,4,512]{2,1,0:T(4,128)(2,1)} %reshape.163), calls=%async_computation.2 | async-start | bytes 131072 | tf_op jit(solution)/shard_map/all_to_all | solution.py:250
  119.1 3.1 %broadcast_select_fusion = (bf16[1024,512]{1,0:T(8,128)(2,1)}, bf16[1024,512]{1,0:T(8,128)(2,1)}) fusion(bf16[1024,512]{1,0:T(8,128)(2,1)} %collective-permute-done.2, pred[]{:T(512)S(6)} %eq.173, bf16[1,1024,512]{2,1,0:T(8,128)(2,1)} %param.21, pred[]{:T(512)S(6)} %eq.162), kind=kLoop, calls=%fused_computation.57 | loop fusion | flops 1048576 | bytes 4194306 | tf_op jit(solution)/shard_map/jit(_where)/select_n | solution.py:243
  122.2 2.0 all-to-all-done.1
  124.2 1.1 convolution_add_fusion.15
  125.3 1.1 convolution_add_fusion.14
  126.4 1.1 convolution_add_fusion.13
  127.6 1.1 convolution_add_fusion.12
  128.7 1.1 convolution_add_fusion.11
  129.8 1.1 convolution_add_fusion.10
  130.9 1.1 convolution_add_fusion.9
  132.0 4.4 %fusion.27 = f32[256,512]{1,0:T(8,128)} fusion(bf16[1024,512]{1,0:T(8,128)(2,1)} %get-tuple-element.20, f32[256,512]{1,0:T(8,128)} %convolution_add_fusion.9, f32[256,512]{1,0:T(8,128)} %convolution_add_fusion.10, f32[256,512]{1,0:T(8,128)} %convolution_add_fusion.11, f32[256,512]{1,0:T(8,128)} %convolution_add_fusion.12, ...), kind=kOutput, calls=%fused_computation.71 | convolution fusion | flops 225181696 | bytes 5672960 | tf_op jit(solution)/shard_map/dot_general | solution.py:260
  136.4 1.8 fusion.187
  138.2 0.2 multiply_reduce_fusion.1
  138.5 0.2 add_convert_fusion.14
  138.7 0.5 fusion.13
  139.2 0.2 convolution_convert_fusion.2
  139.4 0.7 reshape.165
  140.0 5.2 %all-to-all-start.2 = ((bf16[16,4,512]{2,1,0:T(4,128)(2,1)}), bf16[16,4,512]{2,1,0:T(4,128)(2,1)S(1)}, u32[]{:S(2)}, u32[]{:S(2)}) async-start(bf16[16,4,512]{2,1,0:T(4,128)(2,1)} %reshape.165), calls=%async_computation.3 | async-start | bytes 131072 | tf_op jit(solution)/shard_map/all_to_all | solution.py:250
  145.2 0.2 all-gather.3.cloned.1.call-start
  145.5 1.6 collective-permute-start.4
  147.1 3.3 %all-to-all-done.2 = bf16[16,4,512]{2,1,0:T(4,128)(2,1)S(1)} async-done(((bf16[16,4,512]{2,1,0:T(4,128)(2,1)}), bf16[16,4,512]{2,1,0:T(4,128)(2,1)S(1)}, u32[]{:S(2)}, u32[]{:S(2)}) %all-to-all-start.2) | async-done | bytes 65568 | tf_op jit(solution)/shard_map/all_to_all | solution.py:250
  150.4 1.1 convolution_add_fusion.7
  151.5 1.1 convolution_add_fusion.6
  152.6 1.1 convolution_add_fusion.5
  153.7 1.1 convolution_add_fusion.4
  154.9 1.1 convolution_add_fusion.3
  156.0 1.1 convolution_add_fusion.2
  157.1 1.1 convolution_add_fusion.1
  158.2 4.4 %fusion.24 = f32[256,512]{1,0:T(8,128)} fusion(bf16[1024,512]{1,0:T(8,128)(2,1)} %get-tuple-element.19, f32[256,512]{1,0:T(8,128)} %convolution_add_fusion.1, f32[256,512]{1,0:T(8,128)} %convolution_add_fusion.2, f32[256,512]{1,0:T(8,128)} %convolution_add_fusion.3, f32[256,512]{1,0:T(8,128)} %convolution_add_fusion.4, ...), kind=kOutput, calls=%fused_computation.67 | convolution fusion | flops 225181696 | bytes 5672960 | tf_op jit(solution)/shard_map/dot_general | solution.py:260
  162.7 1.7 fusion.188
  164.4 0.2 multiply_reduce_fusion
  164.6 2.1 convolution_convert_fusion
  166.7 1.6 collective-permute-start.5
  169.1 2.9 %collective-permute-done.5 = bf16[256,227]{0,1:T(8,128)(2,1)S(1)} collective-permute-done((bf16[256,227]{0,1:T(8,128)(2,1)S(1)}, bf16[256,227]{0,1:T(8,128)(2,1)S(1)}, u32[]{:S(2)}, u32[]{:S(2)}) %collective-permute-start.5) | collective-permute-done | bytes 116256 | tf_op jit(solution)/shard_map/ppermute | solution.py:163
  172.1 44.1 %all-gather.3.cloned.1.call-done = bf16[4096,512]{1,0:T(8,128)(2,1)} async-done(((bf16[256,512]{1,0:T(8,128)(2,1)}), bf16[4096,512]{1,0:T(8,128)(2,1)}) %all-gather.3.cloned.1.call-update) | async-done | bytes 4194320 | tf_op jit(solution)/shard_map/all_gather | solution.py:171
  216.2 2.9 %gather_fusion.1 = bf16[16,128,512]{2,1,0:T(8,128)(2,1)S(1)} fusion(bf16[16,2,128,512]{3,2,1,0:T(8,128)(2,1)} %bitcast.122, s32[16]{0:T(128)S(1)} %fusion.175), kind=kCustom, calls=%fused_computation.1 | custom fusion | bytes 4194432 | tf_op jit(solution)/shard_map/gather | solution.py:267
  219.1 2.9 %convolution_convert_fusion.1 = bf16[512,227]{0,1:T(8,128)(2,1)} fusion(bf16[512,227]{0,1:T(8,128)(2,1)S(1)} %copy-done.8, bf16[2048,512]{1,0:T(8,128)(2,1)S(1)} %bitcast.118, s32[512]{0:T(512)S(1)} %eq.182, s32[512]{0:T(512)S(1)} %eq.178, s32[512]{0:T(512)S(1)} %eq.174), kind=kOutput, calls=%fused_computation.44 | convolution fusion | flops 1203619328 | bytes 2568192 | tf_op jit(solution)/shard_map/dot_general | solution.py:276
  222.0 0.6 collective-permute-start.6
  222.5 3.9 %fusion.12 = f32[512,227]{1,0:T(8,128)} fusion(bf16[512,227]{0,1:T(8,128)(2,1)} %copy-done.7, bf16[2048,512]{1,0:T(8,128)(2,1)S(1)} %bitcast.119, s32[512]{0:T(512)S(1)} %eq.158, s32[512]{0:T(512)S(1)} %eq.154, s32[512]{0:T(512)S(1)} %eq.150), kind=kOutput, calls=%fused_computation.51 | convolution fusion | flops 1203503104 | bytes 2800640 | tf_op jit(solution)/shard_map/dot_general | solution.py:276
  226.4 3.7 %collective-permute-done.6 = bf16[512,227]{0,1:T(8,128)(2,1)S(1)} collective-permute-done((bf16[512,227]{0,1:T(8,128)(2,1)}, bf16[512,227]{0,1:T(8,128)(2,1)S(1)}, u32[]{:S(2)}, u32[]{:S(2)}) %collective-permute-start.6) | collective-permute-done | bytes 232480 | tf_op jit(solution)/shard_map/ppermute | solution.py:163
  230.1 0.1 copy.39
  230.3 2.6 %select_add_fusion = f32[2,8,64,227]{3,2,1,0:T(8,128)} fusion(f32[8,64,227]{2,1,0:T(8,128)S(1)} %bitcast.120, f32[8,64,227]{2,1,0:T(8,128)} %bitcast.123, pred[2]{0:T(512)(128)(4,1)S(1)} %iota_compare_fusion.13, bf16[2,8,64,512]{3,2,1,0:T(8,128)(2,1)S(1)} %copy-done, bf16[512,227]{0,1:T(8,128)(2,1)} %param.29), kind=kOutput, calls=%fused_computation.48 | convolution fusion | flops 238491648 | bytes 3140610 | tf_op jit(solution)/shard_map/mgrd,do->mgro/dot_general | solution.py:281
  (88 shorter events, 2.2 us)
Async XLA Ops:
  6.5 1.2 copy-start
  7.8 2.8 %copy-start.10 = (s32[1,16,3,128]{3,1,2,0:T(8,128)S(1)}, s32[1,16,3,128]{3,1,2,0:T(8,128)}, u32[]{:S(2)}) copy-start(s32[1,16,3,128]{3,1,2,0:T(8,128)} %param.19) | copy-start | bytes 73732
  7.8 2.8 %copy-start.15 = (s32[1,16,1]{1,2,0:T(1,128)S(1)}, s32[1,16,1]{1,2,0:T(1,128)}, u32[]{:S(2)}) copy-start(s32[1,16,1]{1,2,0:T(1,128)} %param.26) | copy-start | bytes 196
  7.8 9.9 %copy-start.14 = (s32[1,16,3]{1,0,2:T(1,128)S(1)}, s32[1,16,3]{1,0,2:T(1,128)}, u32[]{:S(2)}) copy-start(s32[1,16,3]{1,0,2:T(1,128)} %param.17) | copy-start | bytes 580
  7.8 10.1 %copy-start.16 = (s32[1,16]{1,0:T(1,128)S(1)}, s32[1,16]{1,0:T(1,128)}, u32[]{:S(2)}) copy-start(s32[1,16]{1,0:T(1,128)} %param.18) | copy-start | bytes 196
  10.0 13.7 %collective-permute-start = (bf16[8,64,512]{2,1,0:T(8,128)(2,1)S(1)}, bf16[8,64,512]{2,1,0:T(8,128)(2,1)S(1)}, u32[]{:S(2)}, u32[]{:S(2)}) collective-permute-start(bf16[8,64,512]{2,1,0:T(8,128)(2,1)S(1)} %get-tuple-element.22), channel_id=1, source_target_pairs={{0,16},{16,0},{1,17},{17,1},{2,18},{18,2},{3,19},{19,3},{4,20},{20... | collective-permute-start | bytes 1572872 | tf_op jit(solution)/shard_map/ppermute | solution.py:163
  11.3 11.3 %all-to-all-start = ((s32[16,1,385]{2,1,0:T(1,128)}), s32[16,1,385]{2,1,0:T(1,128)S(1)}, u32[]{:S(2)}, u32[]{:S(2)}) async-start(s32[16,1,385]{2,1,0:T(1,128)} %copy.35), calls=%async_computation | async-start | bytes 65536 | tf_op jit(solution)/shard_map/all_to_all | solution.py:215
  17.6 91.3 %reduce-scatter.2.cloned.1.call-start = ((), (), s32[]{:S(2)}) async-start(), calls=%async_computation.4 | async-start | bytes 4456448 | tf_op jit(solution)/shard_map/reduce_scatter | solution.py:167
  35.9 1.2 copy-start.1
  35.9 3.3 %copy-start.13 = (f32[1,512]{1,0:T(1,128)S(1)}, f32[1,512]{1,0:T(1,128)}, u32[]{:S(2)}) copy-start(f32[1,512]{1,0:T(1,128)} %param.22) | copy-start | bytes 6148
  35.9 4.2 %copy-start.12 = (s32[1,16,4]{1,2,0:T(4,128)S(1)}, s32[1,16,4]{1,2,0:T(4,128)}, u32[]{:S(2)}) copy-start(s32[1,16,4]{1,2,0:T(4,128)} %param.23) | copy-start | bytes 772
  35.9 4.4 %copy-start.9 = (s32[256,8]{0,1:T(8,128)S(1)}, s32[256,8]{0,1:T(8,128)}, u32[]{:S(2)}) copy-start(s32[256,8]{0,1:T(8,128)} %param.24) | copy-start | bytes 24580
  37.1 74.1 %collective-permute-start.3 = (bf16[512,1024]{1,0:T(8,128)(2,1)S(1)}, bf16[512,1024]{1,0:T(8,128)(2,1)}, u32[]{:S(2)}, u32[]{:S(2)}) collective-permute-start(bf16[512,1024]{1,0:T(8,128)(2,1)S(1)} %bitcast.117), channel_id=1, source_target_pairs={{0,16},{16,0},{1,17},{17,1},{2,18},{18,2},{3,19},{19,3},{4,20},{20... | collective-permute-start | bytes 3145736 | tf_op jit(solution)/shard_map/ppermute | solution.py:163
  38.1 81.0 %collective-permute-start.2 = (bf16[1024,512]{1,0:T(8,128)(2,1)}, bf16[1024,512]{1,0:T(8,128)(2,1)}, u32[]{:S(2)}, u32[]{:S(2)}) collective-permute-start(bf16[1024,512]{1,0:T(8,128)(2,1)} %bitcast.121), channel_id=1, source_target_pairs={{0,16},{16,0},{1,17},{17,1},{2,18},{18,2},{3,19},{19,3},{4,20},{20... | collective-permute-start | bytes 3145736 | tf_op jit(solution)/shard_map/ppermute | solution.py:163
  39.1 45.2 %collective-permute-start.1 = (f32[512]{0:T(512)S(1)}, f32[512]{0:T(512)S(1)}, u32[]{:S(2)}, u32[]{:S(2)}) collective-permute-start(f32[512]{0:T(512)S(1)} %bitcast.130), channel_id=1, source_target_pairs={{0,16},{16,0},{1,17},{17,1},{2,18},{18,2},{3,19},{19,3},{4,20},{20... | collective-permute-start | bytes 6152 | tf_op jit(solution)/shard_map/ppermute | solution.py:163
  114.2 10.0 %all-to-all-start.1 = ((bf16[16,4,512]{2,1,0:T(4,128)(2,1)}), bf16[16,4,512]{2,1,0:T(4,128)(2,1)S(1)}, u32[]{:S(2)}, u32[]{:S(2)}) async-start(bf16[16,4,512]{2,1,0:T(4,128)(2,1)} %reshape.163), calls=%async_computation.2 | async-start | bytes 131072 | tf_op jit(solution)/shard_map/all_to_all | solution.py:250
  132.0 4.4 %copy-start.3 = (bf16[1,256,512]{2,1,0:T(8,128)(2,1)S(1)}, bf16[1,256,512]{2,1,0:T(8,128)(2,1)}, u32[]{:S(2)}) copy-start(bf16[1,256,512]{2,1,0:T(8,128)(2,1)} %reduce-scatter.2.cloned.1.call-done) | copy-start | bytes 786436
  136.4 2.2 copy-start.2
  138.7 6.8 %copy-start.4 = (bf16[256,512]{1,0:T(8,128)(2,1)}, bf16[256,512]{1,0:T(8,128)(2,1)S(1)}, u32[]{:S(2)}) copy-start(bf16[256,512]{1,0:T(8,128)(2,1)S(1)} %add_convert_fusion.14) | copy-start | bytes 786436
  140.0 10.4 %all-to-all-start.2 = ((bf16[16,4,512]{2,1,0:T(4,128)(2,1)}), bf16[16,4,512]{2,1,0:T(4,128)(2,1)S(1)}, u32[]{:S(2)}, u32[]{:S(2)}) async-start(bf16[16,4,512]{2,1,0:T(4,128)(2,1)} %reshape.165), calls=%async_computation.3 | async-start | bytes 131072 | tf_op jit(solution)/shard_map/all_to_all | solution.py:250
  145.2 70.9 %all-gather.3.cloned.1.call-start = ((), (), s32[]{:S(2)}) async-start(), calls=%async_computation.5 | async-start | bytes 4456448 | tf_op jit(solution)/shard_map/all_gather | solution.py:171
  145.5 19.1 %collective-permute-start.4 = (bf16[512,256]{1,0:T(8,128)(2,1)}, bf16[512,256]{1,0:T(8,128)(2,1)}, u32[]{:S(2)}, u32[]{:S(2)}) collective-permute-start(bf16[512,256]{1,0:T(8,128)(2,1)} %param.25), channel_id=1, source_target_pairs={{0,16},{16,0},{1,17},{17,1},{2,18},{18,2},{3,19},{19,3},{4,20},{20... | collective-permute-start | bytes 786440 | tf_op jit(solution)/shard_map/ppermute | solution.py:163
  151.5 6.7 %copy-start.17 = (pred[256]{0:T(512)(128)(4,1)S(1)}, pred[256]{0:T(512)(128)(4,1)}, u32[]{:S(2)}) copy-start(pred[256]{0:T(512)(128)(4,1)} %get-tuple-element.17) | copy-start | bytes 772
  151.5 6.7 %copy-start.18 = (pred[256]{0:T(512)(128)(4,1)S(1)}, pred[256]{0:T(512)(128)(4,1)}, u32[]{:S(2)}) copy-start(pred[256]{0:T(512)(128)(4,1)} %get-tuple-element.18) | copy-start | bytes 772
  158.2 4.4 %copy-start.5 = (bf16[256,512]{1,0:T(8,128)(2,1)S(1)}, bf16[256,512]{1,0:T(8,128)(2,1)}, u32[]{:S(2)}) copy-start(bf16[256,512]{1,0:T(8,128)(2,1)} %copy-done.4) | copy-start | bytes 786436
  162.7 4.1 %copy-start.6 = (bf16[256,227]{0,1:T(8,128)(2,1)S(1)}, bf16[256,227]{0,1:T(8,128)(2,1)}, u32[]{:S(2)}) copy-start(bf16[256,227]{0,1:T(8,128)(2,1)} %param.28) | copy-start | bytes 348676
  162.7 5.7 %copy-start.11 = (s32[3,1024]{1,0:T(4,128)S(1)}, s32[3,1024]{1,0:T(4,128)}, u32[]{:S(2)}) copy-start(s32[3,1024]{1,0:T(4,128)} %param.27) | copy-start | bytes 36868
  166.7 5.3 %collective-permute-start.5 = (bf16[256,227]{0,1:T(8,128)(2,1)S(1)}, bf16[256,227]{0,1:T(8,128)(2,1)S(1)}, u32[]{:S(2)}, u32[]{:S(2)}) collective-permute-start(bf16[256,227]{0,1:T(8,128)(2,1)S(1)} %copy-done.6), channel_id=1, source_target_pairs={{0,16},{16,0},{1,17},{17,1},{2,18},{18,2},{3,19},{19,3},{4,20},{20... | collective-permute-start | bytes 348680 | tf_op jit(solution)/shard_map/ppermute | solution.py:163
  172.1 44.1 %copy-start.7 = (bf16[512,227]{0,1:T(8,128)(2,1)}, bf16[512,227]{0,1:T(8,128)(2,1)S(1)}, u32[]{:S(2)}) copy-start(bf16[512,227]{0,1:T(8,128)(2,1)S(1)} %constant_dynamic-update-slice_fusion) | copy-start | bytes 697348
  216.2 2.9 %copy-start.8 = (bf16[512,227]{0,1:T(8,128)(2,1)S(1)}, bf16[512,227]{0,1:T(8,128)(2,1)}, u32[]{:S(2)}) copy-start(bf16[512,227]{0,1:T(8,128)(2,1)} %copy-done.7) | copy-start | bytes 697348
  222.0 8.2 %collective-permute-start.6 = (bf16[512,227]{0,1:T(8,128)(2,1)}, bf16[512,227]{0,1:T(8,128)(2,1)S(1)}, u32[]{:S(2)}, u32[]{:S(2)}) collective-permute-start(bf16[512,227]{0,1:T(8,128)(2,1)} %convolution_convert_fusion.1), channel_id=1, source_target_pairs={{0,16},{16,0},{1,17},{17,1},{2,18},{18,2},{3,19},{19,3},{4,20},{20... | collective-permute-start | bytes 697352 | tf_op jit(solution)/shard_map/ppermute | solution.py:163
Sparse Core Ops, SparseCore 0:
  36.0 72.9 reduce-scatter.1
  166.8 49.2 all-gather.2

commit v2 on v1

--- a/solution.py
+++ b/solution.py
@@ -3,6 +3,8 @@
 import jax
 import jax.numpy as jnp
 from jax import lax
+from jax.experimental import pallas as pl
+from jax.experimental.pallas import tpu as pltpu
 from jax.sharding import PartitionSpec as P
 
 
@@ -163,12 +165,203 @@
     return lax.ppermute(value, "phase", [(0, 1), (1, 0)])
 
 
-def sum_to_owners(partial_sums):
-    return lax.psum_scatter(partial_sums, "shard", scatter_dimension=0, tiled=True)[0]
+MESH_ID = pl.DeviceIdType.MESH
+DEPTH, ROWS, CORES = 4, 2, 2
+
+
+def greet(peers):
+    barrier = pltpu.get_barrier_semaphore()
+    for peer in peers:
+        pl.semaphore_signal(barrier, inc=1, device_id=peer, device_id_type=MESH_ID)
+    pl.semaphore_wait(barrier, len(peers))
+
+
+def send(source, target, sems, at, peer):
+    copy = pltpu.make_async_remote_copy(
+        src_ref=source,
+        dst_ref=target,
+        send_sem=sems.at[0, at],
+        recv_sem=sems.at[1, at],
+        device_id=peer,
+        device_id_type=MESH_ID,
+    )
+    copy.start()
+    return copy
+
+
+def places():
+    phase, me = lax.axis_index("phase"), lax.axis_index("shard")
+    z, y, c = me // 4, (me // 2) % 2, me % 2
+
+    def at(z, y, c):
+        return (phase, z * 4 + y * 2 + c)
+
+    across = at(z, y, 1 - c)
+    beside = at(z, 1 - y, c)
+    line = [at((z + k) % DEPTH, y, c) for k in range(1, DEPTH)]
+    return phase, me, z, y, c, across, beside, line
+
+
+def owner_kernel(
+    part, edge, node, states, edges, nodes,
+    core_in, y_out, y_in, z_out, z_in, total, core_sems, y_sems, z_sems, weight_sems,
+):
+    phase, me, z, y, c, across, beside, line = places()
+    partner = (1 - phase, me)
+    greet([across, beside, partner] + line)
+    step = 32
+    tiles = part.shape[3] // step
+    order = (2, 1, 3, 0)
+    spots = [(z + k) % DEPTH for k in range(DEPTH)]
+    core_copies = {}
+    for k in order:
+        core_copies[k] = send(
+            part.at[spots[k], :, 1 - c], core_in.at[spots[k]], core_sems, k, across
+        )
+    weight_copies = [
+        send(edge, edges.at[c], weight_sems, 0, partner),
+        send(node, nodes.at[c], weight_sems, 1, partner),
+    ]
+
+    def over_tiles(body):
+        def run(t, carry):
+            body(pl.ds(pl.multiple_of(t * step, step), step))
+            return carry
+
+        lax.fori_loop(0, tiles, run, 0)
+
+    def pair(spot, row, at):
+        return part[spot, row, c, at, :].astype(jnp.float32) + core_in[spot, row, at, :].astype(
+            jnp.float32
+        )
+
+    y_copies = {}
+    for k in order:
+        core_copies[k].wait()
+        spot = spots[k]
+
+        def to_beside(at):
+            y_out[k, at, :] = pair(spot, 1 - y, at).astype(jnp.bfloat16)
+
+        over_tiles(to_beside)
+        y_copies[k] = send(y_out.at[k], y_in.at[k], y_sems, k, beside)
+    z_copies = []
+    for k in order:
+        y_copies[k].wait()
+        spot = spots[k]
+
+        def add_up(at):
+            value = pair(spot, y, at) + y_in[k, at, :].astype(jnp.float32)
+            if k == 0:
+                total[at, :] = value
+            else:
+                z_out[k - 1, at, :] = value.astype(jnp.bfloat16)
+
+        over_tiles(add_up)
+        if k:
+            z_copies.append(send(z_out.at[k - 1], z_in.at[k - 1], z_sems, k - 1, line[k - 1]))
+    for copy in weight_copies:
+        copy.wait()
+    weight_copies = [
+        send(edges.at[c], edges.at[c], weight_sems, 2, across),
+        send(nodes.at[c], nodes.at[c], weight_sems, 3, across),
+    ]
+    for copy in z_copies:
+        copy.wait()
+
+    def finish(at):
+        value = total[at, :]
+        for k in range(DEPTH - 1):
+            value = value + z_in[k, at, :].astype(jnp.float32)
+        states[at, :] = layer_norm(value).astype(jnp.bfloat16)
+
+    over_tiles(finish)
+    for copy in weight_copies:
+        copy.wait()
+
+
+def states_and_weights(partial_sums, edge, node):
+    owners, nodes, features = partial_sums.shape
+    part = partial_sums.reshape(DEPTH, ROWS, CORES, nodes, features)
+    core = lax.axis_index("shard") % 2
+    edge_half = lax.dynamic_index_in_dim(
+        edge.reshape(2, edge.shape[0] // 2, edge.shape[1]), core, 0, keepdims=False
+    )
+    node_half = lax.dynamic_index_in_dim(
+        node.reshape(2, node.shape[0] // 2, node.shape[1]), core, 0, keepdims=False
+    )
+    kind = jnp.bfloat16
+    states, edges, node_weights = pl.pallas_call(
+        owner_kernel,
+        out_shape=(
+            jax.ShapeDtypeStruct((nodes, features), kind),
+            jax.ShapeDtypeStruct((2,) + edge_half.shape, kind),
+            jax.ShapeDtypeStruct((2,) + node_half.shape, kind),
+        ),
+        in_specs=[pl.BlockSpec(memory_space=pltpu.VMEM)] * 3,
+        out_specs=[pl.BlockSpec(memory_space=pltpu.VMEM)] * 3,
+        scratch_shapes=[
+            pltpu.VMEM((DEPTH, ROWS, nodes, features), kind),
+            pltpu.VMEM((DEPTH, nodes, features), kind),
+            pltpu.VMEM((DEPTH, nodes, features), kind),
+            pltpu.VMEM((DEPTH - 1, nodes, features), kind),
+            pltpu.VMEM((DEPTH - 1, nodes, features), kind),
+            pltpu.VMEM((nodes, features), jnp.float32),
+            pltpu.SemaphoreType.DMA((2, DEPTH)),
+            pltpu.SemaphoreType.DMA((2, DEPTH)),
+            pltpu.SemaphoreType.DMA((2, DEPTH - 1)),
+            pltpu.SemaphoreType.DMA((2, 4)),
+        ],
+        compiler_params=pltpu.CompilerParams(
+            collective_id=0, has_side_effects=True, vmem_limit_bytes=40 * 2**20
+        ),
+        name="sum_to_owners",
+    )(part, edge_half, node_half)
+    return states, edges.reshape(edge.shape), node_weights.reshape(node.shape)
+
+
+def gather_kernel(mine, everyone, own_sem, z_sems, y_sems, core_sems):
+    phase, me, z, y, c, across, beside, line = places()
+    greet([across, beside] + line)
+    here = everyone.at[z, y, c]
+    z_copies = {}
+    for k in (1, 3, 2):
+        z_copies[k] = send(mine, here, z_sems, k - 1, line[k - 1])
+    y_copies = {0: send(mine, here, y_sems, 0, beside)}
+    core_copies = [send(mine, here, core_sems, 0, across)]
+    keep = pltpu.make_async_copy(mine, here, own_sem.at[0])
+    keep.start()
+    for k in (1, 3, 2):
+        z_copies[k].wait()
+        block = everyone.at[(z + DEPTH - k) % DEPTH, y, c]
+        y_copies[k] = send(block, block, y_sems, k, beside)
+        core_copies.append(send(block, block, core_sems, k, across))
+    for k in (0, 1, 3, 2):
+        y_copies[k].wait()
+        block = everyone.at[(z + DEPTH - k) % DEPTH, 1 - y, c]
+        core_copies.append(send(block, block, core_sems, DEPTH + k, across))
+    keep.wait()
+    for copy in core_copies:
+        copy.wait()
 
 
 def gather_nodes(mapped):
-    return lax.all_gather(mapped, "shard", axis=0, tiled=False)
+    return pl.pallas_call(
+        gather_kernel,
+        out_shape=jax.ShapeDtypeStruct((DEPTH, ROWS, CORES) + mapped.shape, mapped.dtype),
+        in_specs=[pl.BlockSpec(memory_space=pltpu.VMEM)],
+        out_specs=pl.BlockSpec(memory_space=pltpu.VMEM),
+        scratch_shapes=[
+            pltpu.SemaphoreType.DMA((1,)),
+            pltpu.SemaphoreType.DMA((2, DEPTH - 1)),
+            pltpu.SemaphoreType.DMA((2, DEPTH)),
+            pltpu.SemaphoreType.DMA((2, 2 * DEPTH)),
+        ],
+        compiler_params=pltpu.CompilerParams(
+            collective_id=1, has_side_effects=True, vmem_limit_bytes=24 * 2**20
+        ),
+        name="gather_nodes",
+    )(mapped)
 
 
 def one_hot(indices, count, live):
@@ -225,10 +418,10 @@
     partial_sums = jnp.einsum(
         "onr,orc->onc", hot.astype(jnp.bfloat16), picked, preferred_element_type=jnp.float32
     ).astype(jnp.bfloat16)
-    encoded = sum_to_owners(partial_sums).astype(jnp.float32)
-    states = layer_norm(encoded).astype(jnp.bfloat16)
-
-    other_edge, other_node, other_gain = swap(edge_weight[0]), swap(node_weight[0]), swap(node_gain[0])
+    states, other_edge, other_node = states_and_weights(
+        partial_sums, edge_weight[0], node_weight[0]
+    )
+    other_gain = swap(node_gain[0])
     decode_all = jnp.concatenate([decode_weight, swap(decode_weight)], axis=1)
     output_all = jnp.concatenate([output_weight, swap(output_weight)], axis=0)
 
@@ -288,7 +481,8 @@
 
 def on_device(grid_fields, *others):
     phases, batches = lax.axis_size("phase"), grid_fields.shape[0]
-    if phases == batches == 2 and others[10].shape[2] == 1:
+    owners = lax.axis_size("shard")
+    if phases == batches == 2 and owners == DEPTH * ROWS * CORES and others[10].shape[2] == 1:
         return on_device_batches(grid_fields, *others)
     return on_device_sections(grid_fields, *others)
 

time: 242 us -> 188 us (0.78)
  waiting for transfers between devices: 129 us -> 9.83 us
  Pallas kernels: 0 us -> 71.6 us
  between operations: 13.8 us -> 0.66 us
  local copies, waits for them, and re-layouts: 14.7 us -> 21.2 us
  other arithmetic: 7.01 us -> 10.6 us
  starting transfers between devices: 24 us -> 21.1 us
    pallas_call x0 -> x2, Pallas kernels: none -> 71.6 us  [the longest x1 38 us: states_and_weights(): pl.pallas_call(owner_kernel, out_shape=(jax.ShapeDtypeStruct((nodes, feat...]
    ppermute x7 -> x5, waiting for transfers between devices: 49.9 us -> 3.86 us  [swap(): return lax.ppermute(value, 'phase', [(0, 1), (1, 0)])]
    all_gather x1 -> x0, waiting for transfers between devices: 44.1 us -> none  [gather_nodes(): return lax.all_gather(mapped, 'shard', axis=0, tiled=False)]
    reduce_scatter x1 -> x0, waiting for transfers between devices: 24.6 us -> none  [sum_to_owners(): lax.psum_scatter(partial_sums, 'shard', scatter_dimension=0, tiled=True)[0]]
    all_to_all x1, waiting for transfers between devices: 4.71 us -> 0.01 us  [on_device_batches(): lax.all_to_all(tables, 'shard', split_axis=0, concat_axis=0, tiled=True)]
    eq x6, local copies, waits for them, and re-layouts: 0.45 us -> 3.92 us  [outputs(): indices[e][:, None] == ids]
    ppermute x7 -> x5, starting transfers between devices: 7.38 us -> 4.67 us  [swap(): return lax.ppermute(value, 'phase', [(0, 1), (1, 0)])]
  transfers between devices with their start and end apart: 12 -> 8, of which waited for: 9 -> 3; matrix products, arithmetic and copies ran while one was open for 13% -> 38% of each run, Pallas kernels for 0% -> 21%
where the time goes in v2:
time: 188 us; the launch traced here: 185 us
  Pallas kernels  71.6 us (38%)
  matrix products  49.7 us (26%)
  local copies, waits for them, and re-layouts  21.2 us (11%)
  starting transfers between devices  21.1 us (11%)
  other arithmetic  10.6 us (6%)
  waiting for transfers between devices  9.83 us (5%)
    pallas_call x1, Pallas kernels, states_and_weights(): pl.pallas_call(owner_kernel, out_shape=(jax.ShapeDtypeStruct((nodes, feat...  38 us
    pallas_call x1, Pallas kernels, gather_nodes(): pl.pallas_call(gather_kernel, out_shape=jax.ShapeDtypeStruct((DEPTH, ROWS...  33.6 us
    dot_general x14, matrix products, on_device_batches(): jnp.dot(source_hot[slot_index], table, preferred_element_type=jnp.float32)  15.5 us
    all_to_all x2, starting transfers between devices, on_device_batches(): lax.all_to_all(outgoing, 'shard', split_axis=0, concat_axis=0, tiled=True)  10.1 us
    dot_general x2, matrix products, on_device_batches(): jnp.dot(summary, node[features:], preferred_element_type=jnp.float32)  9.27 us
    dot_general x2, matrix products, outputs(): return jnp.dot(hidden, output_all, preferred_element_type=jnp.float32)  6.74 us
    all_to_all x1, starting transfers between devices, on_device_batches(): lax.all_to_all(tables, 'shard', split_axis=0, concat_axis=0, tiled=True)  6.29 us
    all_to_all x2, waiting for transfers between devices, on_device_batches(): lax.all_to_all(outgoing, 'shard', split_axis=0, concat_axis=0, tiled=True)  5.97 us
  transfers between devices with their start and end apart: 8, of which 3 were waited for; matrix products, arithmetic and copies ran while one was open for 38% of the time, Pallas kernels for 21%

profile of v2, /device:TPU:10, one launch (start us, length us, event | category | flops | bytes accessed | tf_op | source)
XLA Modules:
  0.0 184.6 jit_solution(5109356062508125103)
XLA Ops:
  0.0 0.5 collective-permute-start.3
  0.5 1.5 collective-permute-start.2
  2.1 2.1 %multiply_convert_fusion = bf16[2,8,64,512]{3,2,1,0:T(8,128)(2,1)S(1)} fusion(bf16[2,8,64,512]{3,2,1,0:T(8,128)(2,1)S(1)} %copy-done, bf16[512,512]{1,0:T(8,128)(2,1)} %param.16), kind=kOutput, calls=%fused_computation.21 | convolution fusion | flops 539492352 | bytes 2621440 | tf_op jit(solution)/shard_map/mgrd,dc->mgrc/dot_general | solution.py:398
  4.3 1.1 dynamic-slice_bitcast_fusion.3
  5.3 0.5 collective-permute-start
  6.0 0.6 copy.35
  6.6 6.3 %all-to-all-start = ((s32[16,1,385]{2,1,0:T(1,128)}), s32[16,1,385]{2,1,0:T(1,128)S(1)}, u32[]{:S(2)}, u32[]{:S(2)}) async-start(s32[16,1,385]{2,1,0:T(1,128)} %copy.35), calls=%async_computation | async-start | bytes 65536 | tf_op jit(solution)/shard_map/all_to_all | solution.py:408
  12.9 1.6 collective-permute-start.1
  14.5 0.7 constant_dynamic-update-slice_fusion.1
  15.2 0.5 iota_compare_fusion.13
  16.0 1.1 dynamic-slice_bitcast_fusion.1.edge
  17.1 0.6 slice_reduce_fusion.7
  17.8 1.5 fusion.2
  19.6 0.6 eq.184
  20.3 0.6 eq.180
  20.9 0.6 eq.176
  21.5 0.7 eq.160
  22.2 0.7 eq.156
  22.9 0.7 eq.152
  23.5 0.6 broadcast_select_fusion.1
  24.7 0.7 constant_dynamic-update-slice_fusion
  25.4 1.3 pad_maximum_fusion
  26.7 4.9 %gather_fusion = bf16[48,128,512]{2,1,0:T(8,128)(2,1)} fusion(bf16[8,128,512]{2,1,0:T(8,128)(2,1)S(1)} %pad_maximum_fusion, s32[1024]{0:T(1024)S(1)} %pad_clamp_fusion), kind=kCustom, calls=%fused_computation | custom fusion | bytes 12583104 | tf_op jit(solution)/shard_map/gather | solution.py:417
  31.6 5.1 %fusion.3 = bf16[16,256,512]{2,1,0:T(8,128)(2,1)S(1)} fusion(bf16[16,384,512]{2,1,0:T(8,128)(2,1)} %bitcast.115, s32[16,384]{1,0:T(8,128)S(1)} %bitcast_select_fusion.4), kind=kOutput, calls=%fused_computation.15 | convolution fusion | flops 1614282752 | bytes 10510336 | tf_op jit(solution)/shard_map/onr,orc->onc/dot_general | solution.py:418
  36.8 38.0 %sum_to_owners.1 = (bf16[256,512]{1,0:T(8,128)(2,1)S(1)}, bf16[2,256,1024]{2,1,0:T(8,128)(2,1)S(1)}, bf16[2,512,512]{2,1,0:T(8,128)(2,1)S(1)}) custom-call(bf16[4,2,2,256,512]{4,3,2,1,0:T(8,128)(2,1)S(1)} %bitcast.114, bf16[256,1024]{1,0:T(8,128)(2,1)S(1)} %dynamic-slice_bitcast_fusion.1.edge, bf16[512,512]{1,0:T(8,128)(2,1)S(1)} %dynamic-slice_bitcast_fusion.node), custom_call_target="tpu_custom_call" | custom-call | tf_op jit(solution)/shard_map/sum_to_owners/pallas_call | solution.py:294
  74.8 1.6 bitcast_select_fusion.2
  76.4 1.2 bitcast_select_fusion
  78.2 0.6 reshape.162
  78.9 4.7 %all-to-all-start.1 = ((bf16[16,4,512]{2,1,0:T(4,128)(2,1)}), bf16[16,4,512]{2,1,0:T(4,128)(2,1)S(1)}, u32[]{:S(2)}, u32[]{:S(2)}) async-start(bf16[16,4,512]{2,1,0:T(4,128)(2,1)} %reshape.162), calls=%async_computation.1 | async-start | bytes 131072 | tf_op jit(solution)/shard_map/all_to_all | solution.py:443
  83.6 2.1 %fusion.17 = f32[256,512]{1,0:T(8,128)} fusion(bf16[256,512]{1,0:T(8,128)(2,1)S(1)} %get-tuple-element.8, bf16[1024,512]{1,0:T(8,128)(2,1)} %get-tuple-element.28), kind=kOutput, calls=%fused_computation.62 | convolution fusion | flops 134217728 | bytes 1310720 | tf_op jit(solution)/shard_map/dot_general | solution.py:452
  85.7 3.0 %all-to-all-done.1 = bf16[16,4,512]{2,1,0:T(4,128)(2,1)S(1)} async-done(((bf16[16,4,512]{2,1,0:T(4,128)(2,1)}), bf16[16,4,512]{2,1,0:T(4,128)(2,1)S(1)}, u32[]{:S(2)}, u32[]{:S(2)}) %all-to-all-start.1) | async-done | bytes 65568 | tf_op jit(solution)/shard_map/all_to_all | solution.py:443
  88.8 1.1 convolution_add_fusion.9
  89.9 1.1 convolution_add_fusion.10
  91.0 1.1 convolution_add_fusion.11
  92.1 1.1 convolution_add_fusion.12
  93.2 1.1 convolution_add_fusion.13
  94.4 1.1 convolution_add_fusion.14
  95.5 1.1 convolution_add_fusion.15
  96.6 4.6 %fusion.172 = (f32[256]{0:T(256)S(1)}, f32[256,512]{1,0:T(8,128)}) fusion(f32[256,512]{1,0:T(8,128)} %fusion.17, bf16[1024,512]{1,0:T(8,128)(2,1)} %get-tuple-element.28, f32[256,512]{1,0:T(8,128)} %convolution_add_fusion.9, f32[256,512]{1,0:T(8,128)} %convolution_add_fusion.10, f32[256,512]{1,0:T(8,128)} %convolution_add_fusion.11, ...), kind=kOutput, calls=%fused_computation.266 | convolution fusion | flops 225967872 | bytes 6198272 | tf_op jit(solution)/shard_map/dot_general | solution.py:453
  101.3 1.2 multiply_reduce_fusion.1
  102.5 1.2 add_convert_fusion.14
  103.8 1.7 fusion.177
  105.6 0.7 reshape.164
  106.3 5.4 %all-to-all-start.2 = ((bf16[16,4,512]{2,1,0:T(4,128)(2,1)}), bf16[16,4,512]{2,1,0:T(4,128)(2,1)S(1)}, u32[]{:S(2)}, u32[]{:S(2)}) async-start(bf16[16,4,512]{2,1,0:T(4,128)(2,1)} %reshape.164), calls=%async_computation.2 | async-start | bytes 131072 | tf_op jit(solution)/shard_map/all_to_all | solution.py:443
  111.7 2.1 %fusion.14 = f32[256,512]{1,0:T(8,128)} fusion(bf16[256,512]{1,0:T(8,128)(2,1)S(1)} %add_convert_fusion.14, bf16[1024,512]{1,0:T(8,128)(2,1)} %get-tuple-element.27), kind=kOutput, calls=%fused_computation.58 | convolution fusion | flops 134217728 | bytes 1310720 | tf_op jit(solution)/shard_map/dot_general | solution.py:452
  113.8 3.0 %all-to-all-done.2 = bf16[16,4,512]{2,1,0:T(4,128)(2,1)S(1)} async-done(((bf16[16,4,512]{2,1,0:T(4,128)(2,1)}), bf16[16,4,512]{2,1,0:T(4,128)(2,1)S(1)}, u32[]{:S(2)}, u32[]{:S(2)}) %all-to-all-start.2) | async-done | bytes 65568 | tf_op jit(solution)/shard_map/all_to_all | solution.py:443
  116.9 1.1 convolution_add_fusion.1
  118.0 1.1 convolution_add_fusion.2
  119.1 1.1 convolution_add_fusion.3
  120.2 1.1 convolution_add_fusion.4
  121.3 1.1 convolution_add_fusion.5
  122.4 1.1 convolution_add_fusion.6
  123.5 1.1 convolution_add_fusion.7
  124.7 4.6 %fusion.173 = (f32[256]{0:T(256)S(1)}, f32[256,512]{1,0:T(8,128)}) fusion(f32[256,512]{1,0:T(8,128)} %fusion.14, bf16[1024,512]{1,0:T(8,128)(2,1)} %get-tuple-element.27, f32[256,512]{1,0:T(8,128)} %convolution_add_fusion.1, f32[256,512]{1,0:T(8,128)} %convolution_add_fusion.2, f32[256,512]{1,0:T(8,128)} %convolution_add_fusion.3, ...), kind=kOutput, calls=%fused_computation.267 | convolution fusion | flops 225967872 | bytes 6198272 | tf_op jit(solution)/shard_map/dot_general | solution.py:453
  129.3 1.2 multiply_reduce_fusion
  130.6 1.5 convolution_convert_fusion.mine
  132.2 33.6 %gather_nodes.1 = bf16[4,2,2,256,512]{4,3,2,1,0:T(8,128)(2,1)S(1)} custom-call(bf16[256,512]{1,0:T(8,128)(2,1)S(1)} %convolution_convert_fusion.mine), custom_call_target="tpu_custom_call" | custom-call | tf_op jit(solution)/shard_map/gather_nodes/pallas_call | solution.py:349
  165.8 1.9 %copy-done.1 = bf16[4,2,2,256,512]{4,3,2,1,0:T(8,128)(2,1)} copy-done((bf16[4,2,2,256,512]{4,3,2,1,0:T(8,128)(2,1)}, bf16[4,2,2,256,512]{4,3,2,1,0:T(8,128)(2,1)S(1)}, u32[]{:S(2)}) %copy-start.1) | copy-done | bytes 4194328
  167.7 2.9 %gather_fusion.1 = bf16[16,128,512]{2,1,0:T(8,128)(2,1)S(1)} fusion(bf16[16,2,128,512]{3,2,1,0:T(8,128)(2,1)} %bitcast.113, s32[16]{0:T(128)S(1)} %fusion.164), kind=kCustom, calls=%fused_computation.1 | custom fusion | bytes 4194432 | tf_op jit(solution)/shard_map/gather | solution.py:460
  170.7 2.9 %convolution_convert_fusion.1 = bf16[512,227]{0,1:T(8,128)(2,1)} fusion(bf16[512,227]{0,1:T(8,128)(2,1)S(1)} %copy-done.7, bf16[2048,512]{1,0:T(8,128)(2,1)S(1)} %bitcast.118, s32[512]{0:T(512)S(1)} %copy-done.14, s32[512]{0:T(512)S(1)} %copy-done.15, s32[512]{0:T(512)S(1)} %copy-done.17), kind=kOutput, calls=%fused_computation.44 | convolution fusion | flops 1203619328 | bytes 2568192 | tf_op jit(solution)/shard_map/dot_general | solution.py:469
  173.6 0.6 collective-permute-start.4
  174.1 3.9 %fusion.12 = f32[512,227]{1,0:T(8,128)} fusion(bf16[512,227]{0,1:T(8,128)(2,1)} %constant_dynamic-update-slice_fusion, bf16[2048,512]{1,0:T(8,128)(2,1)S(1)} %bitcast.119, s32[512]{0:T(512)S(1)} %copy-done.12, s32[512]{0:T(512)S(1)} %copy-done.13, s32[512]{0:T(512)S(1)} %copy-done.16), kind=kOutput, calls=%fused_computation.55 | convolution fusion | flops 1203503104 | bytes 2800640 | tf_op jit(solution)/shard_map/dot_general | solution.py:469
  178.0 3.9 %collective-permute-done.4 = bf16[512,227]{0,1:T(8,128)(2,1)S(1)} collective-permute-done((bf16[512,227]{0,1:T(8,128)(2,1)}, bf16[512,227]{0,1:T(8,128)(2,1)S(1)}, u32[]{:S(2)}, u32[]{:S(2)}) %collective-permute-start.4) | collective-permute-done | bytes 232480 | tf_op jit(solution)/shard_map/ppermute | solution.py:165
  182.0 2.6 %select_add_fusion = f32[2,8,64,227]{3,2,1,0:T(8,128)} fusion(f32[8,64,227]{2,1,0:T(8,128)S(1)} %bitcast.120, f32[8,64,227]{2,1,0:T(8,128)} %bitcast.121, pred[2]{0:T(512)(128)(4,1)S(1)} %copy-done.39, bf16[2,8,64,512]{3,2,1,0:T(8,128)(2,1)S(1)} %copy-done, bf16[512,227]{0,1:T(8,128)(2,1)} %param.29), kind=kOutput, calls=%fused_computation.52 | convolution fusion | flops 238491648 | bytes 3140610 | tf_op jit(solution)/shard_map/mgrd,do->mgro/dot_general | solution.py:474
  (121 shorter events, 2.6 us)
Async XLA Ops:
  0.0 2.0 %copy-start = (bf16[2,8,64,512]{3,2,1,0:T(8,128)(2,1)S(1)}, bf16[2,8,64,512]{3,2,1,0:T(8,128)(2,1)}, u32[]{:S(2)}) copy-start(bf16[2,8,64,512]{3,2,1,0:T(8,128)(2,1)} %param.15) | copy-start | bytes 3145732
  0.0 24.7 %collective-permute-start.3 = (bf16[256,227]{0,1:T(8,128)(2,1)}, bf16[256,227]{0,1:T(8,128)(2,1)S(1)}, u32[]{:S(2)}, u32[]{:S(2)}) collective-permute-start(bf16[256,227]{0,1:T(8,128)(2,1)} %param.28), channel_id=1, source_target_pairs={{0,16},{16,0},{1,17},{17,1},{2,18},{18,2},{3,19},{19,3},{4,20},{20... | collective-permute-start | bytes 348680 | tf_op jit(solution)/shard_map/ppermute | solution.py:165
  0.5 130.1 %collective-permute-start.2 = (bf16[512,256]{1,0:T(8,128)(2,1)}, bf16[512,256]{1,0:T(8,128)(2,1)}, u32[]{:S(2)}, u32[]{:S(2)}) collective-permute-start(bf16[512,256]{1,0:T(8,128)(2,1)} %param.25), channel_id=1, source_target_pairs={{0,16},{16,0},{1,17},{17,1},{2,18},{18,2},{3,19},{19,3},{4,20},{20... | collective-permute-start | bytes 786440 | tf_op jit(solution)/shard_map/ppermute | solution.py:165
  2.0 3.8 %copy-start.21 = (s32[1,16,1]{1,2,0:T(1,128)S(1)}, s32[1,16,1]{1,2,0:T(1,128)}, u32[]{:S(2)}) copy-start(s32[1,16,1]{1,2,0:T(1,128)} %param.26) | copy-start | bytes 196
  2.0 3.9 %copy-start.9 = (s32[1,16,3,128]{3,1,2,0:T(8,128)S(1)}, s32[1,16,3,128]{3,1,2,0:T(8,128)}, u32[]{:S(2)}) copy-start(s32[1,16,3,128]{3,1,2,0:T(8,128)} %param.19) | copy-start | bytes 73732
  2.0 10.9 %copy-start.18 = (f32[1,512]{1,0:T(1,128)S(1)}, f32[1,512]{1,0:T(1,128)}, u32[]{:S(2)}) copy-start(f32[1,512]{1,0:T(1,128)} %param.22) | copy-start | bytes 6148
  2.0 12.5 %copy-start.6 = (bf16[256,227]{0,1:T(8,128)(2,1)S(1)}, bf16[256,227]{0,1:T(8,128)(2,1)}, u32[]{:S(2)}) copy-start(bf16[256,227]{0,1:T(8,128)(2,1)} %param.28) | copy-start | bytes 348676
  2.1 13.7 %copy-start.20 = (s32[1,16,3]{1,0,2:T(1,128)S(1)}, s32[1,16,3]{1,0,2:T(1,128)}, u32[]{:S(2)}) copy-start(s32[1,16,3]{1,0,2:T(1,128)} %param.17) | copy-start | bytes 580
  2.1 13.8 %copy-start.22 = (s32[1,16]{1,0:T(1,128)S(1)}, s32[1,16]{1,0:T(1,128)}, u32[]{:S(2)}) copy-start(s32[1,16]{1,0:T(1,128)} %param.18) | copy-start | bytes 196
  2.1 15.0 %copy-start.3 = (bf16[1,1024,512]{2,1,0:T(8,128)(2,1)S(1)}, bf16[1,1024,512]{2,1,0:T(8,128)(2,1)}, u32[]{:S(2)}) copy-start(bf16[1,1024,512]{2,1,0:T(8,128)(2,1)} %param.21) | copy-start | bytes 3145732
  4.2 12.9 %copy-start.8 = (s32[256,8]{0,1:T(8,128)S(1)}, s32[256,8]{0,1:T(8,128)}, u32[]{:S(2)}) copy-start(s32[256,8]{0,1:T(8,128)} %param.24) | copy-start | bytes 24580
  4.2 15.0 %copy-start.11 = (s32[1,16,4]{1,2,0:T(4,128)S(1)}, s32[1,16,4]{1,2,0:T(4,128)}, u32[]{:S(2)}) copy-start(s32[1,16,4]{1,2,0:T(4,128)} %param.23) | copy-start | bytes 772
  4.2 15.2 %copy-start.10 = (s32[3,1024]{1,0:T(4,128)S(1)}, s32[3,1024]{1,0:T(4,128)}, u32[]{:S(2)}) copy-start(s32[3,1024]{1,0:T(4,128)} %param.27) | copy-start | bytes 36868
  5.3 20.1 %collective-permute-start = (bf16[8,64,512]{2,1,0:T(8,128)(2,1)}, bf16[8,64,512]{2,1,0:T(8,128)(2,1)}, u32[]{:S(2)}, u32[]{:S(2)}) collective-permute-start(bf16[8,64,512]{2,1,0:T(8,128)(2,1)} %get-tuple-element.30), channel_id=1, source_target_pairs={{0,16},{16,0},{1,17},{17,1},{2,18},{18,2},{3,19},{19,3},{4,20},{20... | collective-permute-start | bytes 1572872 | tf_op jit(solution)/shard_map/ppermute | solution.py:165
  6.6 17.5 %all-to-all-start = ((s32[16,1,385]{2,1,0:T(1,128)}), s32[16,1,385]{2,1,0:T(1,128)S(1)}, u32[]{:S(2)}, u32[]{:S(2)}) async-start(s32[16,1,385]{2,1,0:T(1,128)} %copy.35), calls=%async_computation | async-start | bytes 65536 | tf_op jit(solution)/shard_map/all_to_all | solution.py:408
  12.9 10.6 %collective-permute-start.1 = (f32[512]{0:T(512)S(1)}, f32[512]{0:T(512)S(1)}, u32[]{:S(2)}, u32[]{:S(2)}) collective-permute-start(f32[512]{0:T(512)S(1)} %bitcast.128), channel_id=1, source_target_pairs={{0,16},{16,0},{1,17},{17,1},{2,18},{18,2},{3,19},{19,3},{4,20},{20... | collective-permute-start | bytes 6152 | tf_op jit(solution)/shard_map/ppermute | solution.py:165
  36.8 38.0 %copy-start.4 = (bf16[1,1024,512]{2,1,0:T(8,128)(2,1)S(1)}, bf16[1,1024,512]{2,1,0:T(8,128)(2,1)}, u32[]{:S(2)}) copy-start(bf16[1,1024,512]{2,1,0:T(8,128)(2,1)} %param.21) | copy-start | bytes 3145732
  36.8 39.6 %copy-start.5 = (bf16[1,512,1024]{2,1,0:T(8,128)(2,1)S(1)}, bf16[1,512,1024]{2,1,0:T(8,128)(2,1)}, u32[]{:S(2)}) copy-start(bf16[1,512,1024]{2,1,0:T(8,128)(2,1)} %param.20) | copy-start | bytes 3145732
  76.4 12.4 %copy-start.2 = (pred[8,256,320]{2,1,0:T(32,128)(4,1)S(1)}, pred[8,256,320]{2,1,0:T(32,128)(4,1)}, u32[]{:S(2)}) copy-start(pred[8,256,320]{2,1,0:T(32,128)(4,1)} %fusion.2) | copy-start | bytes 1966084
  78.9 9.9 %all-to-all-start.1 = ((bf16[16,4,512]{2,1,0:T(4,128)(2,1)}), bf16[16,4,512]{2,1,0:T(4,128)(2,1)S(1)}, u32[]{:S(2)}, u32[]{:S(2)}) async-start(bf16[16,4,512]{2,1,0:T(4,128)(2,1)} %reshape.162), calls=%async_computation.1 | async-start | bytes 131072 | tf_op jit(solution)/shard_map/all_to_all | solution.py:443
  89.9 6.7 %copy-start.23 = (pred[256]{0:T(512)(128)(4,1)S(1)}, pred[256]{0:T(512)(128)(4,1)}, u32[]{:S(2)}) copy-start(pred[256]{0:T(512)(128)(4,1)} %get-tuple-element.17) | copy-start | bytes 772
  89.9 6.7 %copy-start.25 = (pred[256]{0:T(512)(128)(4,1)S(1)}, pred[256]{0:T(512)(128)(4,1)}, u32[]{:S(2)}) copy-start(pred[256]{0:T(512)(128)(4,1)} %get-tuple-element.18) | copy-start | bytes 772
  89.9 6.7 %copy-start.27 = (pred[256]{0:T(512)(128)(4,1)S(1)}, pred[256]{0:T(512)(128)(4,1)}, u32[]{:S(2)}) copy-start(pred[256]{0:T(512)(128)(4,1)} %get-tuple-element.19) | copy-start | bytes 772
  89.9 6.7 %copy-start.29 = (pred[256]{0:T(512)(128)(4,1)S(1)}, pred[256]{0:T(512)(128)(4,1)}, u32[]{:S(2)}) copy-start(pred[256]{0:T(512)(128)(4,1)} %get-tuple-element.20) | copy-start | bytes 772
  89.9 6.7 %copy-start.31 = (pred[256]{0:T(512)(128)(4,1)S(1)}, pred[256]{0:T(512)(128)(4,1)}, u32[]{:S(2)}) copy-start(pred[256]{0:T(512)(128)(4,1)} %get-tuple-element.21) | copy-start | bytes 772
  89.9 6.7 %copy-start.33 = (pred[256]{0:T(512)(128)(4,1)S(1)}, pred[256]{0:T(512)(128)(4,1)}, u32[]{:S(2)}) copy-start(pred[256]{0:T(512)(128)(4,1)} %get-tuple-element.22) | copy-start | bytes 772
  89.9 6.7 %copy-start.35 = (pred[256]{0:T(512)(128)(4,1)S(1)}, pred[256]{0:T(512)(128)(4,1)}, u32[]{:S(2)}) copy-start(pred[256]{0:T(512)(128)(4,1)} %get-tuple-element.23) | copy-start | bytes 772
  89.9 6.7 %copy-start.37 = (pred[256]{0:T(512)(128)(4,1)S(1)}, pred[256]{0:T(512)(128)(4,1)}, u32[]{:S(2)}) copy-start(pred[256]{0:T(512)(128)(4,1)} %get-tuple-element.24) | copy-start | bytes 772
  106.3 10.5 %all-to-all-start.2 = ((bf16[16,4,512]{2,1,0:T(4,128)(2,1)}), bf16[16,4,512]{2,1,0:T(4,128)(2,1)S(1)}, u32[]{:S(2)}, u32[]{:S(2)}) async-start(bf16[16,4,512]{2,1,0:T(4,128)(2,1)} %reshape.164), calls=%async_computation.2 | async-start | bytes 131072 | tf_op jit(solution)/shard_map/all_to_all | solution.py:443
  117.9 6.7 %copy-start.24 = (pred[256]{0:T(512)(128)(4,1)S(1)}, pred[256]{0:T(512)(128)(4,1)}, u32[]{:S(2)}) copy-start(pred[256]{0:T(512)(128)(4,1)} %get-tuple-element.17) | copy-start | bytes 772
  117.9 6.7 %copy-start.26 = (pred[256]{0:T(512)(128)(4,1)S(1)}, pred[256]{0:T(512)(128)(4,1)}, u32[]{:S(2)}) copy-start(pred[256]{0:T(512)(128)(4,1)} %get-tuple-element.18) | copy-start | bytes 772
  118.0 6.7 %copy-start.28 = (pred[256]{0:T(512)(128)(4,1)S(1)}, pred[256]{0:T(512)(128)(4,1)}, u32[]{:S(2)}) copy-start(pred[256]{0:T(512)(128)(4,1)} %get-tuple-element.19) | copy-start | bytes 772
  118.0 6.7 %copy-start.30 = (pred[256]{0:T(512)(128)(4,1)S(1)}, pred[256]{0:T(512)(128)(4,1)}, u32[]{:S(2)}) copy-start(pred[256]{0:T(512)(128)(4,1)} %get-tuple-element.20) | copy-start | bytes 772
  118.0 6.7 %copy-start.32 = (pred[256]{0:T(512)(128)(4,1)S(1)}, pred[256]{0:T(512)(128)(4,1)}, u32[]{:S(2)}) copy-start(pred[256]{0:T(512)(128)(4,1)} %get-tuple-element.21) | copy-start | bytes 772
  118.0 6.7 %copy-start.34 = (pred[256]{0:T(512)(128)(4,1)S(1)}, pred[256]{0:T(512)(128)(4,1)}, u32[]{:S(2)}) copy-start(pred[256]{0:T(512)(128)(4,1)} %get-tuple-element.22) | copy-start | bytes 772
  118.0 6.7 %copy-start.36 = (pred[256]{0:T(512)(128)(4,1)S(1)}, pred[256]{0:T(512)(128)(4,1)}, u32[]{:S(2)}) copy-start(pred[256]{0:T(512)(128)(4,1)} %get-tuple-element.23) | copy-start | bytes 772
  118.0 6.7 %copy-start.38 = (pred[256]{0:T(512)(128)(4,1)S(1)}, pred[256]{0:T(512)(128)(4,1)}, u32[]{:S(2)}) copy-start(pred[256]{0:T(512)(128)(4,1)} %get-tuple-element.24) | copy-start | bytes 772
  124.7 5.9 %copy-start.19 = (f32[512]{0:T(512)S(1)}, f32[512]{0:T(512)}, u32[]{:S(2)}) copy-start(f32[512]{0:T(512)} %get-tuple-element.31) | copy-start | bytes 6148
  132.2 38.5 %copy-start.7 = (bf16[512,227]{0,1:T(8,128)(2,1)S(1)}, bf16[512,227]{0,1:T(8,128)(2,1)}, u32[]{:S(2)}) copy-start(bf16[512,227]{0,1:T(8,128)(2,1)} %constant_dynamic-update-slice_fusion) | copy-start | bytes 697348
  132.2 38.5 %copy-start.14 = (s32[512]{0:T(512)S(1)}, s32[512]{0:T(512)}, u32[]{:S(2)}) copy-start(s32[512]{0:T(512)} %eq.184) | copy-start | bytes 6148
  132.2 38.5 %copy-start.15 = (s32[512]{0:T(512)S(1)}, s32[512]{0:T(512)}, u32[]{:S(2)}) copy-start(s32[512]{0:T(512)} %eq.180) | copy-start | bytes 6148
  132.2 38.5 %copy-start.17 = (s32[512]{0:T(512)S(1)}, s32[512]{0:T(512)}, u32[]{:S(2)}) copy-start(s32[512]{0:T(512)} %eq.176) | copy-start | bytes 6148
  165.8 1.9 %copy-start.1 = (bf16[4,2,2,256,512]{4,3,2,1,0:T(8,128)(2,1)}, bf16[4,2,2,256,512]{4,3,2,1,0:T(8,128)(2,1)S(1)}, u32[]{:S(2)}) copy-start(bf16[4,2,2,256,512]{4,3,2,1,0:T(8,128)(2,1)S(1)} %gather_nodes.1) | copy-start | bytes 12582916
  170.6 3.5 %copy-start.12 = (s32[512]{0:T(512)S(1)}, s32[512]{0:T(512)}, u32[]{:S(2)}) copy-start(s32[512]{0:T(512)} %eq.160) | copy-start | bytes 6148
  170.7 3.5 %copy-start.13 = (s32[512]{0:T(512)S(1)}, s32[512]{0:T(512)}, u32[]{:S(2)}) copy-start(s32[512]{0:T(512)} %eq.156) | copy-start | bytes 6148
  170.7 3.5 %copy-start.16 = (s32[512]{0:T(512)S(1)}, s32[512]{0:T(512)}, u32[]{:S(2)}) copy-start(s32[512]{0:T(512)} %eq.152) | copy-start | bytes 6148
  173.6 8.4 %copy-start.39 = (pred[2]{0:T(512)(128)(4,1)S(1)}, pred[2]{0:T(512)(128)(4,1)}, u32[]{:S(2)}) copy-start(pred[2]{0:T(512)(128)(4,1)} %iota_compare_fusion.13) | copy-start | bytes 10
  173.6 8.3 %collective-permute-start.4 = (bf16[512,227]{0,1:T(8,128)(2,1)}, bf16[512,227]{0,1:T(8,128)(2,1)S(1)}, u32[]{:S(2)}, u32[]{:S(2)}) collective-permute-start(bf16[512,227]{0,1:T(8,128)(2,1)} %convolution_convert_fusion.1), channel_id=1, source_target_pairs={{0,16},{16,0},{1,17},{17,1},{2,18},{18,2},{3,19},{19,3},{4,20},{20... | collective-permute-start | bytes 697352 | tf_op jit(solution)/shard_map/ppermute | solution.py:165

commit v3 on v2

--- a/solution.py
+++ b/solution.py
@@ -166,6 +166,7 @@
 
 
 MESH_ID = pl.DeviceIdType.MESH
+PIECE = 128
 DEPTH, ROWS, CORES = 4, 2, 2
 
 
@@ -208,6 +209,12 @@
 ):
     phase, me, z, y, c, across, beside, line = places()
     partner = (1 - phase, me)
+    keeps = [
+        pltpu.make_async_copy(edge, edges.at[phase], weight_sems.at[0, 4]),
+        pltpu.make_async_copy(node, nodes.at[phase], weight_sems.at[1, 4]),
+    ]
+    for keep in keeps:
+        keep.start()
     greet([across, beside, partner] + line)
     step = 32
     tiles = part.shape[3] // step
@@ -219,8 +226,8 @@
             part.at[spots[k], :, 1 - c], core_in.at[spots[k]], core_sems, k, across
         )
     weight_copies = [
-        send(edge, edges.at[c], weight_sems, 0, partner),
-        send(node, nodes.at[c], weight_sems, 1, partner),
+        send(edge.at[c], edges.at[phase, c], weight_sems, 0, partner),
+        send(node.at[c], nodes.at[phase, c], weight_sems, 1, partner),
     ]
 
     def over_tiles(body):
@@ -263,8 +270,8 @@
     for copy in weight_copies:
         copy.wait()
     weight_copies = [
-        send(edges.at[c], edges.at[c], weight_sems, 2, across),
-        send(nodes.at[c], nodes.at[c], weight_sems, 3, across),
+        send(edges.at[1 - phase, c], edges.at[1 - phase, c], weight_sems, 2, across),
+        send(nodes.at[1 - phase, c], nodes.at[1 - phase, c], weight_sems, 3, across),
     ]
     for copy in z_copies:
         copy.wait()
@@ -276,20 +283,15 @@
         states[at, :] = layer_norm(value).astype(jnp.bfloat16)
 
     over_tiles(finish)
-    for copy in weight_copies:
+    for copy in weight_copies + keeps:
         copy.wait()
 
 
 def states_and_weights(partial_sums, edge, node):
     owners, nodes, features = partial_sums.shape
     part = partial_sums.reshape(DEPTH, ROWS, CORES, nodes, features)
-    core = lax.axis_index("shard") % 2
-    edge_half = lax.dynamic_index_in_dim(
-        edge.reshape(2, edge.shape[0] // 2, edge.shape[1]), core, 0, keepdims=False
-    )
-    node_half = lax.dynamic_index_in_dim(
-        node.reshape(2, node.shape[0] // 2, node.shape[1]), core, 0, keepdims=False
-    )
+    edge_half = edge.reshape(2, edge.shape[0] // 2, edge.shape[1])
+    node_half = node.reshape(2, node.shape[0] // 2, node.shape[1])
     kind = jnp.bfloat16
     states, edges, node_weights = pl.pallas_call(
         owner_kernel,
@@ -310,42 +312,49 @@
             pltpu.SemaphoreType.DMA((2, DEPTH)),
             pltpu.SemaphoreType.DMA((2, DEPTH)),
             pltpu.SemaphoreType.DMA((2, DEPTH - 1)),
-            pltpu.SemaphoreType.DMA((2, 4)),
+            pltpu.SemaphoreType.DMA((2, 5)),
         ],
         compiler_params=pltpu.CompilerParams(
             collective_id=0, has_side_effects=True, vmem_limit_bytes=40 * 2**20
         ),
         name="sum_to_owners",
     )(part, edge_half, node_half)
-    return states, edges.reshape(edge.shape), node_weights.reshape(node.shape)
+    return states, edges.reshape((2,) + edge.shape), node_weights.reshape((2,) + node.shape)
 
 
 def gather_kernel(mine, everyone, own_sem, z_sems, y_sems, core_sems):
     phase, me, z, y, c, across, beside, line = places()
     greet([across, beside] + line)
-    here = everyone.at[z, y, c]
-    z_copies = {}
-    for k in (1, 3, 2):
-        z_copies[k] = send(mine, here, z_sems, k - 1, line[k - 1])
-    y_copies = {0: send(mine, here, y_sems, 0, beside)}
-    core_copies = [send(mine, here, core_sems, 0, across)]
-    keep = pltpu.make_async_copy(mine, here, own_sem.at[0])
+    pieces = mine.shape[0] // PIECE
+    whole = everyone.at[z, y, c]
+    spans = [pl.ds(p * PIECE, PIECE) for p in range(pieces)]
+    keep = pltpu.make_async_copy(mine, whole, own_sem.at[0])
+    z_copies, y_copies, core_copies = {}, {}, []
+    for p, span in enumerate(spans):
+        own, here = mine.at[span], everyone.at[z, y, c, span]
+        for k in (2, 1, 3):
+            z_copies[p, k] = send(own, here, z_sems, p * 4 + k, line[k - 1])
+        y_copies[p, 0] = send(own, here, y_sems, p * 4, beside)
+        core_copies.append(send(own, here, core_sems, p * 8, across))
     keep.start()
-    for k in (1, 3, 2):
-        z_copies[k].wait()
-        block = everyone.at[(z + DEPTH - k) % DEPTH, y, c]
-        y_copies[k] = send(block, block, y_sems, k, beside)
-        core_copies.append(send(block, block, core_sems, k, across))
-    for k in (0, 1, 3, 2):
-        y_copies[k].wait()
-        block = everyone.at[(z + DEPTH - k) % DEPTH, 1 - y, c]
-        core_copies.append(send(block, block, core_sems, DEPTH + k, across))
+    for p, span in enumerate(spans):
+        for k in (1, 3, 2):
+            z_copies[p, k].wait()
+            block = everyone.at[(z + DEPTH - k) % DEPTH, y, c, span]
+            y_copies[p, k] = send(block, block, y_sems, p * 4 + k, beside)
+            core_copies.append(send(block, block, core_sems, p * 8 + k, across))
+    for p, span in enumerate(spans):
+        for k in (0, 1, 3, 2):
+            y_copies[p, k].wait()
+            block = everyone.at[(z + DEPTH - k) % DEPTH, 1 - y, c, span]
+            core_copies.append(send(block, block, core_sems, p * 8 + 4 + k, across))
     keep.wait()
     for copy in core_copies:
         copy.wait()
 
 
 def gather_nodes(mapped):
+    pieces = mapped.shape[0] // PIECE
     return pl.pallas_call(
         gather_kernel,
         out_shape=jax.ShapeDtypeStruct((DEPTH, ROWS, CORES) + mapped.shape, mapped.dtype),
@@ -353,9 +362,9 @@
         out_specs=pl.BlockSpec(memory_space=pltpu.VMEM),
         scratch_shapes=[
             pltpu.SemaphoreType.DMA((1,)),
-            pltpu.SemaphoreType.DMA((2, DEPTH - 1)),
-            pltpu.SemaphoreType.DMA((2, DEPTH)),
-            pltpu.SemaphoreType.DMA((2, 2 * DEPTH)),
+            pltpu.SemaphoreType.DMA((2, 4 * pieces)),
+            pltpu.SemaphoreType.DMA((2, 4 * pieces)),
+            pltpu.SemaphoreType.DMA((2, 8 * pieces)),
         ],
         compiler_params=pltpu.CompilerParams(
             collective_id=1, has_side_effects=True, vmem_limit_bytes=24 * 2**20
@@ -364,9 +373,97 @@
     )(mapped)
 
 
-def one_hot(indices, count, live):
-    hot = (indices[..., None] == jnp.arange(count, dtype=jnp.int32)) & live[..., None]
-    return hot.astype(jnp.bfloat16)
+def silu(values):
+    half = 0.5 * values
+    return half + half * jnp.tanh(half)
+
+
+def sections_kernel(
+    first, edges, nodes, gains, source_hot, live, send_hot, decode, mapped,
+    states, outgoing, incoming, table, dest, mixed, running, send_sems, recv_sems,
+):
+    phase, me = lax.axis_index("phase"), lax.axis_index("shard")
+    owners, lanes = incoming.shape[1], incoming.shape[3]
+    node_count, features = first.shape
+    slots = source_hot.shape[0]
+    peers = [lax.rem(me + k, owners) for k in range(1, owners)]
+    greet([(phase, peer) for peer in peers])
+    packed = owners * 16
+    chunk_of_row = (lax.broadcasted_iota(jnp.int32, (packed, lanes), 0) // 4) % 4
+    states[...] = first[...]
+
+    def dot(left, right):
+        return jnp.dot(left, right, preferred_element_type=jnp.float32)
+
+    for layer in range(2):
+        source = dot(states[...], edges[layer, :, :features]).astype(jnp.bfloat16)
+        table[:node_count, :] = source
+        chosen = dot(send_hot[...], source)
+        payload = jnp.zeros((packed, lanes), jnp.float32)
+        for j in range(4):
+            payload = jnp.where(chunk_of_row == j, chosen[:, j * lanes : (j + 1) * lanes], payload)
+        outgoing[layer] = payload.astype(jnp.bfloat16).reshape(owners, 16, lanes)
+        copies = []
+        for k, peer in enumerate(peers):
+            copy = pltpu.make_async_remote_copy(
+                src_ref=outgoing.at[layer, peer],
+                dst_ref=incoming.at[layer, me],
+                send_sem=send_sems.at[layer, k],
+                recv_sem=recv_sems.at[layer, k],
+                device_id=(phase, peer),
+                device_id_type=MESH_ID,
+            )
+            copy.start()
+            copies.append(copy)
+        incoming[layer, me] = outgoing[layer, me]
+        dest[...] = dot(states[...], edges[layer, :, features:])
+        mixed[...] = dot(states[...], nodes[layer, :features, :])
+        running[...] = jnp.zeros_like(running)
+        for copy in copies:
+            copy.wait()
+        arrived = incoming[layer].reshape(packed, lanes).astype(jnp.float32)
+        for j in range(4):
+            table[node_count:, j * lanes : (j + 1) * lanes] = jnp.where(
+                chunk_of_row == j, arrived, 0.0
+            ).astype(jnp.bfloat16)
+
+        def one_slot(slot, carry):
+            gathered = dot(source_hot[slot], table[...])
+            running[...] += silu(gathered + dest[...]) * live[slot]
+            return carry
+
+        lax.fori_loop(0, slots, one_slot, 0)
+        value = mixed[...] + dot(running[...].astype(jnp.bfloat16), nodes[layer, features:, :])
+        value = gains[layer] * layer_norm(silu(value))
+        states[...] = (states[...].astype(jnp.float32) + value).astype(jnp.bfloat16)
+    mapped[...] = dot(states[...], decode[...]).astype(jnp.bfloat16)
+
+
+def run_sections(states, edges, nodes, gains, source_hot, live, send_hot, decode, owners):
+    node_count, features = states.shape
+    lanes = features // 4
+    kind = jnp.bfloat16
+    return pl.pallas_call(
+        sections_kernel,
+        out_shape=jax.ShapeDtypeStruct((node_count, features), kind),
+        in_specs=[pl.BlockSpec(memory_space=pltpu.VMEM)] * 8,
+        out_specs=pl.BlockSpec(memory_space=pltpu.VMEM),
+        scratch_shapes=[
+            pltpu.VMEM((node_count, features), kind),
+            pltpu.VMEM((2, owners, 16, lanes), kind),
+            pltpu.VMEM((2, owners, 16, lanes), kind),
+            pltpu.VMEM((node_count + owners * 16, features), kind),
+            pltpu.VMEM((node_count, features), jnp.float32),
+            pltpu.VMEM((node_count, features), jnp.float32),
+            pltpu.VMEM((node_count, features), jnp.float32),
+            pltpu.SemaphoreType.DMA((2, owners - 1)),
+            pltpu.SemaphoreType.DMA((2, owners - 1)),
+        ],
+        compiler_params=pltpu.CompilerParams(
+            collective_id=2, has_side_effects=True, vmem_limit_bytes=40 * 2**20
+        ),
+        name="run_sections",
+    )(states, edges, nodes, gains, source_hot, live, send_hot, decode)
 
 
 def on_device_batches(
@@ -418,43 +515,27 @@
     partial_sums = jnp.einsum(
         "onr,orc->onc", hot.astype(jnp.bfloat16), picked, preferred_element_type=jnp.float32
     ).astype(jnp.bfloat16)
-    states, other_edge, other_node = states_and_weights(
-        partial_sums, edge_weight[0], node_weight[0]
-    )
+    states, edges, nodes = states_and_weights(partial_sums, edge_weight[0], node_weight[0])
     other_gain = swap(node_gain[0])
+    first = phase_index == 0
+    gains = jnp.stack(
+        [jnp.where(first, node_gain[0], other_gain), jnp.where(first, other_gain, node_gain[0])]
+    )[:, None, :]
     decode_all = jnp.concatenate([decode_weight, swap(decode_weight)], axis=1)
     output_all = jnp.concatenate([output_weight, swap(output_weight)], axis=0)
 
-    edge_live = mesh_neighbour.T >= 0
-    remote = owners * mesh_send.shape[2]
-    source_hot = one_hot(mesh_neighbour.T, node_count + remote, edge_live)
-    send_nodes = mesh_send[0].reshape(-1)
-    send_hot = one_hot(send_nodes, node_count, send_nodes >= 0)
-    for layer in range(2):
-        mine = phase_index == layer
-        edge = jnp.where(mine, edge_weight[0], other_edge)
-        node = jnp.where(mine, node_weight[0], other_node)
-        gain = jnp.where(mine, node_gain[0], other_gain)
-        both_parts = jnp.dot(states, edge, preferred_element_type=jnp.float32)
-        source_part = both_parts[:, :features].astype(jnp.bfloat16)
-        dest_part = both_parts[:, features:]
-        outgoing = jnp.dot(send_hot, source_part, preferred_element_type=jnp.float32)
-        outgoing = outgoing.astype(jnp.bfloat16).reshape(owners, -1, features)
-        incoming = lax.all_to_all(outgoing, "shard", split_axis=0, concat_axis=0, tiled=True)
-        table = jnp.concatenate([source_part, incoming.reshape(-1, features)], axis=0)
-        running = jnp.zeros((node_count, features), jnp.float32)
-        for slot_index in range(slot_count):
-            gathered = jnp.dot(source_hot[slot_index], table, preferred_element_type=jnp.float32)
-            running = running + jnp.where(
-                edge_live[slot_index][:, None], jax.nn.silu(gathered + dest_part), 0.0
-            )
-        summary = running.astype(jnp.bfloat16)
-        mixed = jnp.dot(states, node[:features], preferred_element_type=jnp.float32)
-        mixed = mixed + jnp.dot(summary, node[features:], preferred_element_type=jnp.float32)
-        states = (states.astype(jnp.float32) + gain * layer_norm(jax.nn.silu(mixed))).astype(
-            jnp.bfloat16
-        )
-    mapped = jnp.dot(states, decode_all, preferred_element_type=jnp.float32).astype(jnp.bfloat16)
+    neighbour = mesh_neighbour.T
+    packed = jnp.arange(owners * 16, dtype=jnp.int32)
+    columns = jnp.concatenate(
+        [jnp.arange(node_count, dtype=jnp.int32), node_count + packed // 16 * 4 + packed % 4]
+    )
+    source_hot = (neighbour[:, :, None] == columns).astype(jnp.bfloat16)
+    live = (neighbour >= 0).astype(jnp.float32)[:, :, None]
+    send_nodes = jnp.tile(mesh_send[0][:, None, :], (1, 4, 1)).reshape(-1)
+    send_hot = send_nodes[:, None] == jnp.arange(node_count, dtype=jnp.int32)
+    mapped = run_sections(
+        states, edges, nodes, gains, source_hot, live, send_hot.astype(jnp.bfloat16), decode_all, owners
+    )
 
     gathered = gather_nodes(mapped).reshape(owners, node_count // block_size, block_size, features)
     chosen = gathered[jnp.arange(owners), decode_block[:, 0]].reshape(owners * block_size, features)
@@ -482,7 +563,7 @@
 def on_device(grid_fields, *others):
     phases, batches = lax.axis_size("phase"), grid_fields.shape[0]
     owners = lax.axis_size("shard")
-    if phases == batches == 2 and owners == DEPTH * ROWS * CORES and others[10].shape[2] == 1:
+    if phases == batches == 2 and owners == DEPTH * ROWS * CORES and others[7].shape[2] == 4 and others[10].shape[2] == 1:
         return on_device_batches(grid_fields, *others)
     return on_device_sections(grid_fields, *others)
 

time: 188 us -> 158 us (0.84); the launches traced: 185 us -> 158 us
  matrix products: 49.7 us -> 16.7 us
  Pallas kernels: 71.6 us -> 95.2 us
  starting transfers between devices: 21.1 us -> 11 us
  other arithmetic: 10.6 us -> 4.98 us
    dot_general x23 -> x0, matrix products: 33.1 us -> none  [the longest x14 15.5 us: on_device_batches(): jnp.dot(source_hot[slot_index], table, preferred_element_type=jnp.float32)]
    pallas_call x0 -> x1, Pallas kernels: none -> 19.1 us  [run_sections(): pl.pallas_call(sections_kernel, out_shape=jax.ShapeDtypeStruct((node_coun...]
    all_to_all x2 -> x0, starting transfers between devices: 10.1 us -> none  [on_device_batches(): lax.all_to_all(outgoing, 'shard', split_axis=0, concat_axis=0, tiled=True)]
    all_to_all x2 -> x0, waiting for transfers between devices: 5.97 us -> none  [on_device_batches(): lax.all_to_all(outgoing, 'shard', split_axis=0, concat_axis=0, tiled=True)]
    ppermute x5, waiting for transfers between devices: 3.86 us -> 9.42 us  [swap(): return lax.ppermute(value, 'phase', [(0, 1), (1, 0)])]
    pallas_call x1, Pallas kernels: 33.6 us -> 37.6 us  [gather_nodes(): pl.pallas_call(gather_kernel, out_shape=jax.ShapeDtypeStruct((DEPTH, ROWS...]
    eq x6, local copies, waits for them, and re-layouts: 3.92 us -> 0.45 us  [outputs(): indices[e][:, None] == ids]
    select_n x3 -> x1, other arithmetic: 3.31 us -> 0.01 us  [on_device_batches(): jnp.where(first, node_gain[0], other_gain)]
  transfers between devices with their start and end apart: 8 -> 6, of which waited for: 3 -> 2; matrix products, arithmetic and copies ran while one was open for 38% -> 8% of each run, Pallas kernels for 21% -> 0%
where the time goes in v3:
time: 158 us
  Pallas kernels  95.2 us (60%)
  local copies, waits for them, and re-layouts  20.1 us (13%)
  matrix products  16.7 us (11%)
  starting transfers between devices  11 us (7%)
  waiting for transfers between devices  9.42 us (6%)
  other arithmetic  4.98 us (3%)
    pallas_call x1, Pallas kernels, states_and_weights(): pl.pallas_call(owner_kernel, out_shape=(jax.ShapeDtypeStruct((nodes, feat...  38.5 us
    pallas_call x1, Pallas kernels, gather_nodes(): pl.pallas_call(gather_kernel, out_shape=jax.ShapeDtypeStruct((DEPTH, ROWS...  37.6 us
    pallas_call x1, Pallas kernels, run_sections(): pl.pallas_call(sections_kernel, out_shape=jax.ShapeDtypeStruct((node_coun...  19.1 us
    ppermute x5, waiting for transfers between devices, swap(): return lax.ppermute(value, 'phase', [(0, 1), (1, 0)])  9.42 us
    dot_general x2, matrix products, outputs(): return jnp.dot(hidden, output_all, preferred_element_type=jnp.float32)  6.74 us
    all_to_all x1, starting transfers between devices, on_device_batches(): lax.all_to_all(tables, 'shard', split_axis=0, concat_axis=0, tiled=True)  6.3 us
    gather x1, local copies, waits for them, and re-layouts, on_device_batches(): picked = rows[send_blocks].reshape(owners, capacity * block_size, features)  6.14 us
    dot_general x1, matrix products, on_device_batches(): jnp.einsum('onr,orc->onc', hot.astype(jnp.bfloat16), picked, preferred_el...  5.26 us
  transfers between devices with their start and end apart: 6, of which 2 were waited for; matrix products, arithmetic and copies ran while one was open for 8% of the time, Pallas kernels for 0%

profile of v3, /device:TPU:10, one launch (start us, length us, event | category | flops | bytes accessed | tf_op | source)
XLA Modules:
  0.0 157.7 jit_solution(15387622128401142380)
XLA Ops:
  0.0 0.0 copy-start
  0.0 1.2 copy-done
  1.2 0.0 copy-start.14
  1.2 0.0 copy-start.7
  1.3 0.0 copy-start.10
  1.3 2.1 %multiply_convert_fusion = bf16[2,8,64,512]{3,2,1,0:T(8,128)(2,1)S(1)} fusion(bf16[2,8,64,512]{3,2,1,0:T(8,128)(2,1)S(1)} %copy-done, bf16[512,512]{1,0:T(8,128)(2,1)} %param.16), kind=kOutput, calls=%fused_computation.20 | convolution fusion | flops 539492352 | bytes 2621440 | tf_op jit(solution)/shard_map/mgrd,dc->mgrc/dot_general | solution.py:495
  3.4 1.1 dynamic-slice_bitcast_fusion.1
  4.5 0.5 collective-permute-start
  5.0 0.1 copy.36
  5.1 0.6 copy.37
  5.8 6.3 %all-to-all-start = ((s32[16,1,385]{2,1,0:T(1,128)}), s32[16,1,385]{2,1,0:T(1,128)S(1)}, u32[]{:S(2)}, u32[]{:S(2)}) async-start(s32[16,1,385]{2,1,0:T(1,128)} %copy.37), calls=%async_computation | async-start | bytes 65536 | tf_op jit(solution)/shard_map/all_to_all | solution.py:505
  12.1 1.6 collective-permute-start.1
  13.6 0.5 collective-permute-start.2
  14.2 1.5 collective-permute-start.3
  15.7 1.6 %constant_dynamic-update-slice_fusion.1 = bf16[512,227]{0,1:T(8,128)(2,1)} fusion(bf16[256,227]{0,1:T(8,128)(2,1)} %param.28), kind=kLoop, calls=%fused_computation.62 | loop fusion | bytes 235008
  17.3 0.1 copy.38
  17.4 0.1 reshape.122
  17.5 0.1 iota_compare_fusion.11
  17.6 0.0 copy-done.7
  17.6 1.4 copy.40.live
  18.9 0.0 copy-done.10
  18.9 0.1 copy.39
  19.0 0.1 tile.11
  19.1 0.1 fusion.15.send_hot
  19.3 0.1 reshape.108
  19.4 0.5 compare_convert_fusion.source_hot
  19.9 0.1 dynamic-slice_reduce_fusion.5
  20.0 0.1 eq.147
  20.1 0.1 eq.151
  20.2 0.1 eq.155
  20.2 0.1 eq.169
  20.3 0.1 eq.173
  20.4 0.1 eq.177
  20.5 0.0 collective-permute-done.1
  20.5 0.0 all-to-all-done
  20.5 0.1 reshape.110
  20.6 0.1 rev.3
  20.8 0.1 reshape.111
  20.9 0.1 broadcast_in_dim.59
  21.0 0.1 fusion.23
  21.1 5.6 %collective-permute-done.3 = bf16[256,227]{0,1:T(8,128)(2,1)} collective-permute-done((bf16[256,227]{0,1:T(8,128)(2,1)}, bf16[256,227]{0,1:T(8,128)(2,1)}, u32[]{:S(2)}, u32[]{:S(2)}) %collective-permute-start.3) | collective-permute-done | bytes 116256 | tf_op jit(solution)/shard_map/ppermute | solution.py:165
  26.7 1.6 constant_dynamic-update-slice_fusion
  28.2 0.0 collective-permute-done.2
  28.2 1.8 %pad_maximum_fusion.1.decode = bf16[512,512]{1,0:T(8,128)(2,1)} fusion(bf16[512,256]{1,0:T(8,128)(2,1)} %collective-permute-done.2, bf16[512,256]{1,0:T(8,128)(2,1)} %param.25), kind=kLoop, calls=%fused_computation.30 | loop fusion | flops 1048576 | bytes 1048576 | tf_op jit(solution)/shard_map/concatenate | solution.py:524
  30.1 0.0 collective-permute-done
  30.1 2.2 %pad_maximum_fusion = bf16[8,128,512]{2,1,0:T(8,128)(2,1)} fusion(bf16[8,64,512]{2,1,0:T(8,128)(2,1)} %collective-permute-done, bf16[8,64,512]{2,1,0:T(8,128)(2,1)} %get-tuple-element.17), kind=kLoop, calls=%fused_computation.25 | loop fusion | flops 2097152 | bytes 2097152 | tf_op jit(solution)/shard_map/concatenate | solution.py:500
  32.3 6.1 %gather_fusion = bf16[48,128,512]{2,1,0:T(8,128)(2,1)} fusion(bf16[8,128,512]{2,1,0:T(8,128)(2,1)} %pad_maximum_fusion, s32[1024]{0:T(1024)S(1)} %pad_clamp_fusion), kind=kCustom, calls=%fused_computation | custom fusion | bytes 12583104 | tf_op jit(solution)/shard_map/gather | solution.py:514
  38.4 5.3 %fusion.2 = bf16[16,256,512]{2,1,0:T(8,128)(2,1)S(1)} fusion(bf16[16,384,512]{2,1,0:T(8,128)(2,1)} %bitcast.68, s32[16,384]{1,0:T(8,128)S(1)} %bitcast_select_fusion), kind=kOutput, calls=%fused_computation.14 | convolution fusion | flops 1614282752 | bytes 10510336 | tf_op jit(solution)/shard_map/onr,orc->onc/dot_general | solution.py:515
  43.7 0.0 copy-start.2
  43.7 0.0 copy-start.3
  43.7 0.0 copy-done.4
  43.7 0.0 copy-done.5
  43.8 38.5 %sum_to_owners.1 = (bf16[256,512]{1,0:T(8,128)(2,1)S(1)}, bf16[2,2,256,1024]{3,2,1,0:T(8,128)(2,1)S(1)}, bf16[2,2,512,512]{3,2,1,0:T(8,128)(2,1)S(1)}) custom-call(bf16[4,2,2,256,512]{4,3,2,1,0:T(8,128)(2,1)S(1)} %bitcast.63, bf16[2,256,1024]{2,1,0:T(8,128)(2,1)S(1)} %bitcast.66, bf16[2,512,512]{2,1,0:T(8,128)(2,1)S(1)} %bitcast.67), custom_call_target="tpu_custom_call" | custom-call | tf_op jit(solution)/shard_map/sum_to_owners/pallas_call | solution.py:296
  82.2 19.1 %run_sections.1.mine = bf16[256,512]{1,0:T(8,128)(2,1)S(1)} custom-call(bf16[256,512]{1,0:T(8,128)(2,1)S(1)} %get-tuple-element.8.first, bf16[2,512,1024]{2,1,0:T(8,128)(2,1)S(1)} %bitcast.64, bf16[2,1024,512]{2,1,0:T(8,128)(2,1)S(1)} %bitcast.65, f32[2,1,512]{2,1,0:T(1,128)S(1)} %broadcast_in_dim.61.gains, ...), custom_call_target="tpu_custom_call" | custom-call | tf_op jit(solution)/shard_map/run_sections/pallas_call | solution.py:446
  101.3 0.0 copy-start.6
  101.4 37.6 %gather_nodes.1 = bf16[4,2,2,256,512]{4,3,2,1,0:T(8,128)(2,1)S(1)} custom-call(bf16[256,512]{1,0:T(8,128)(2,1)S(1)} %run_sections.1.mine), custom_call_target="tpu_custom_call" | custom-call | tf_op jit(solution)/shard_map/gather_nodes/pallas_call | solution.py:358
  139.0 1.9 %copy-done.1 = bf16[4,2,2,256,512]{4,3,2,1,0:T(8,128)(2,1)} copy-done((bf16[4,2,2,256,512]{4,3,2,1,0:T(8,128)(2,1)}, bf16[4,2,2,256,512]{4,3,2,1,0:T(8,128)(2,1)S(1)}, u32[]{:S(2)}) %copy-start.1) | copy-done | bytes 4194328
  140.9 2.9 %gather_fusion.1 = bf16[16,128,512]{2,1,0:T(8,128)(2,1)S(1)} fusion(bf16[16,2,128,512]{3,2,1,0:T(8,128)(2,1)} %bitcast.62, s32[16]{0:T(128)S(1)} %fusion.23), kind=kCustom, calls=%fused_computation.1 | custom fusion | bytes 4194432 | tf_op jit(solution)/shard_map/gather | solution.py:541
  143.8 2.9 %convolution_convert_fusion = bf16[512,227]{0,1:T(8,128)(2,1)} fusion(bf16[512,227]{0,1:T(8,128)(2,1)S(1)} %copy-done.6, bf16[2048,512]{1,0:T(8,128)(2,1)S(1)} %bitcast.69, s32[512]{0:T(512)S(1)} %eq.177, s32[512]{0:T(512)S(1)} %eq.173, s32[512]{0:T(512)S(1)} %eq.169), kind=kOutput, calls=%fused_computation.24 | convolution fusion | flops 1203619328 | bytes 2568192 | tf_op jit(solution)/shard_map/dot_general | solution.py:550
  146.7 0.5 collective-permute-start.4
  147.3 3.9 %fusion.11 = f32[512,227]{1,0:T(8,128)} fusion(bf16[512,227]{0,1:T(8,128)(2,1)} %constant_dynamic-update-slice_fusion, bf16[2048,512]{1,0:T(8,128)(2,1)S(1)} %bitcast.70, s32[512]{0:T(512)S(1)} %eq.155, s32[512]{0:T(512)S(1)} %eq.151, s32[512]{0:T(512)S(1)} %eq.147), kind=kOutput, calls=%fused_computation.29 | convolution fusion | flops 1203503104 | bytes 2800640 | tf_op jit(solution)/shard_map/dot_general | solution.py:550
  151.1 3.9 %collective-permute-done.4 = bf16[512,227]{0,1:T(8,128)(2,1)S(1)} collective-permute-done((bf16[512,227]{0,1:T(8,128)(2,1)}, bf16[512,227]{0,1:T(8,128)(2,1)S(1)}, u32[]{:S(2)}, u32[]{:S(2)}) %collective-permute-start.4) | collective-permute-done | bytes 232480 | tf_op jit(solution)/shard_map/ppermute | solution.py:165
  155.0 0.1 copy.42
  155.1 2.6 %select_add_fusion = f32[2,8,64,227]{3,2,1,0:T(8,128)} fusion(f32[8,64,227]{2,1,0:T(8,128)S(1)} %bitcast.71, f32[8,64,227]{2,1,0:T(8,128)} %bitcast.72, pred[2]{0:T(512)(128)(4,1)S(1)} %iota_compare_fusion.12, bf16[2,8,64,512]{3,2,1,0:T(8,128)(2,1)S(1)} %copy-done, bf16[512,227]{0,1:T(8,128)(2,1)} %param.29), kind=kOutput, calls=%fused_computation.26 | convolution fusion | flops 238491648 | bytes 3140610 | tf_op jit(solution)/shard_map/mgrd,do->mgro/dot_general | solution.py:555
  (35 shorter events, 0.2 us)
Async XLA Ops:
  0.0 1.2 copy-start
  1.2 3.8 %copy-start.8 = (s32[1,16,3,128]{3,1,2,0:T(8,128)S(1)}, s32[1,16,3,128]{3,1,2,0:T(8,128)}, u32[]{:S(2)}) copy-start(s32[1,16,3,128]{3,1,2,0:T(8,128)} %param.19) | copy-start | bytes 73732
  1.2 3.8 %copy-start.13 = (s32[1,16,1]{1,2,0:T(1,128)S(1)}, s32[1,16,1]{1,2,0:T(1,128)}, u32[]{:S(2)}) copy-start(s32[1,16,1]{1,2,0:T(1,128)} %param.26) | copy-start | bytes 196
  1.2 10.8 %copy-start.11 = (f32[1,512]{1,0:T(1,128)S(1)}, f32[1,512]{1,0:T(1,128)}, u32[]{:S(2)}) copy-start(f32[1,512]{1,0:T(1,128)} %param.22) | copy-start | bytes 6148
  1.2 16.0 %copy-start.12 = (s32[1,16,3]{1,0,2:T(1,128)S(1)}, s32[1,16,3]{1,0,2:T(1,128)}, u32[]{:S(2)}) copy-start(s32[1,16,3]{1,0,2:T(1,128)} %param.17) | copy-start | bytes 580
  1.2 16.2 %copy-start.14 = (s32[1,16]{1,0:T(1,128)S(1)}, s32[1,16]{1,0:T(1,128)}, u32[]{:S(2)}) copy-start(s32[1,16]{1,0:T(1,128)} %param.18) | copy-start | bytes 196
  1.2 16.3 %copy-start.7 = (s32[256,8]{0,1:T(8,128)S(1)}, s32[256,8]{0,1:T(8,128)}, u32[]{:S(2)}) copy-start(s32[256,8]{0,1:T(8,128)} %param.24) | copy-start | bytes 24580
  1.3 17.7 %copy-start.10 = (s32[1,16,4]{1,2,0:T(4,128)S(1)}, s32[1,16,4]{1,2,0:T(4,128)}, u32[]{:S(2)}) copy-start(s32[1,16,4]{1,2,0:T(4,128)} %param.23) | copy-start | bytes 772
  1.3 18.0 %copy-start.9 = (s32[3,1024]{1,0:T(4,128)S(1)}, s32[3,1024]{1,0:T(4,128)}, u32[]{:S(2)}) copy-start(s32[3,1024]{1,0:T(4,128)} %param.27) | copy-start | bytes 36868
  4.5 25.6 %collective-permute-start = (bf16[8,64,512]{2,1,0:T(8,128)(2,1)}, bf16[8,64,512]{2,1,0:T(8,128)(2,1)}, u32[]{:S(2)}, u32[]{:S(2)}) collective-permute-start(bf16[8,64,512]{2,1,0:T(8,128)(2,1)} %get-tuple-element.18), channel_id=1, source_target_pairs={{0,16},{16,0},{1,17},{17,1},{2,18},{18,2},{3,19},{19,3},{4,20},{20... | collective-permute-start | bytes 1572872 | tf_op jit(solution)/shard_map/ppermute | solution.py:165
  5.8 14.7 %all-to-all-start = ((s32[16,1,385]{2,1,0:T(1,128)}), s32[16,1,385]{2,1,0:T(1,128)S(1)}, u32[]{:S(2)}, u32[]{:S(2)}) async-start(s32[16,1,385]{2,1,0:T(1,128)} %copy.37), calls=%async_computation | async-start | bytes 65536 | tf_op jit(solution)/shard_map/all_to_all | solution.py:505
  12.1 8.4 %collective-permute-start.1 = (f32[512]{0:T(512)S(1)}, f32[512]{0:T(512)S(1)}, u32[]{:S(2)}, u32[]{:S(2)}) collective-permute-start(f32[512]{0:T(512)S(1)} %bitcast.82), channel_id=1, source_target_pairs={{0,16},{16,0},{1,17},{17,1},{2,18},{18,2},{3,19},{19,3},{4,20},{20... | collective-permute-start | bytes 6152 | tf_op jit(solution)/shard_map/ppermute | solution.py:165
  13.6 14.6 %collective-permute-start.2 = (bf16[512,256]{1,0:T(8,128)(2,1)}, bf16[512,256]{1,0:T(8,128)(2,1)}, u32[]{:S(2)}, u32[]{:S(2)}) collective-permute-start(bf16[512,256]{1,0:T(8,128)(2,1)} %param.25), channel_id=1, source_target_pairs={{0,16},{16,0},{1,17},{17,1},{2,18},{18,2},{3,19},{19,3},{4,20},{20... | collective-permute-start | bytes 786440 | tf_op jit(solution)/shard_map/ppermute | solution.py:165
  14.2 12.5 %collective-permute-start.3 = (bf16[256,227]{0,1:T(8,128)(2,1)}, bf16[256,227]{0,1:T(8,128)(2,1)}, u32[]{:S(2)}, u32[]{:S(2)}) collective-permute-start(bf16[256,227]{0,1:T(8,128)(2,1)} %param.28), channel_id=1, source_target_pairs={{0,16},{16,0},{1,17},{17,1},{2,18},{18,2},{3,19},{19,3},{4,20},{20... | collective-permute-start | bytes 348680 | tf_op jit(solution)/shard_map/ppermute | solution.py:165
  38.4 5.3 %copy-start.4 = (bf16[1,512,1024]{2,1,0:T(8,128)(2,1)S(1)}, bf16[1,512,1024]{2,1,0:T(8,128)(2,1)}, u32[]{:S(2)}) copy-start(bf16[1,512,1024]{2,1,0:T(8,128)(2,1)} %param.20) | copy-start | bytes 3145732
  38.4 5.3 %copy-start.5 = (bf16[1,1024,512]{2,1,0:T(8,128)(2,1)S(1)}, bf16[1,1024,512]{2,1,0:T(8,128)(2,1)}, u32[]{:S(2)}) copy-start(bf16[1,1024,512]{2,1,0:T(8,128)(2,1)} %param.21) | copy-start | bytes 3145732
  43.7 38.5 %copy-start.2 = (f32[8,256,1]{2,1,0:T(8,128)S(1)}, f32[8,256,1]{2,1,0:T(8,128)}, u32[]{:S(2)}) copy-start(f32[8,256,1]{2,1,0:T(8,128)} %copy.40.live) | copy-start | bytes 24580
  43.7 38.5 %copy-start.3 = (bf16[512,512]{1,0:T(8,128)(2,1)S(1)}, bf16[512,512]{1,0:T(8,128)(2,1)}, u32[]{:S(2)}) copy-start(bf16[512,512]{1,0:T(8,128)(2,1)} %pad_maximum_fusion.1.decode) | copy-start | bytes 1572868
  101.3 42.5 %copy-start.6 = (bf16[512,227]{0,1:T(8,128)(2,1)S(1)}, bf16[512,227]{0,1:T(8,128)(2,1)}, u32[]{:S(2)}) copy-start(bf16[512,227]{0,1:T(8,128)(2,1)} %constant_dynamic-update-slice_fusion) | copy-start | bytes 697348
  139.0 1.9 %copy-start.1 = (bf16[4,2,2,256,512]{4,3,2,1,0:T(8,128)(2,1)}, bf16[4,2,2,256,512]{4,3,2,1,0:T(8,128)(2,1)S(1)}, u32[]{:S(2)}) copy-start(bf16[4,2,2,256,512]{4,3,2,1,0:T(8,128)(2,1)S(1)} %gather_nodes.1) | copy-start | bytes 12582916
  146.7 8.3 %collective-permute-start.4 = (bf16[512,227]{0,1:T(8,128)(2,1)}, bf16[512,227]{0,1:T(8,128)(2,1)S(1)}, u32[]{:S(2)}, u32[]{:S(2)}) collective-permute-start(bf16[512,227]{0,1:T(8,128)(2,1)} %convolution_convert_fusion), channel_id=1, source_target_pairs={{0,16},{16,0},{1,17},{17,1},{2,18},{18,2},{3,19},{19,3},{4,20},{20... | collective-permute-start | bytes 697352 | tf_op jit(solution)/shard_map/ppermute | solution.py:165

commit v4 on v3

--- a/solution.py
+++ b/solution.py
@@ -204,7 +204,7 @@
 
 
 def owner_kernel(
-    part, edge, node, states, edges, nodes,
+    part, edge, node, decode, gain, states, edges, nodes, decode_other, gains,
     core_in, y_out, y_in, z_out, z_in, total, core_sems, y_sems, z_sems, weight_sems,
 ):
     phase, me, z, y, c, across, beside, line = places()
@@ -212,6 +212,7 @@
     keeps = [
         pltpu.make_async_copy(edge, edges.at[phase], weight_sems.at[0, 4]),
         pltpu.make_async_copy(node, nodes.at[phase], weight_sems.at[1, 4]),
+        pltpu.make_async_copy(gain, gains.at[phase], weight_sems.at[0, 7]),
     ]
     for keep in keeps:
         keep.start()
@@ -228,6 +229,8 @@
     weight_copies = [
         send(edge.at[c], edges.at[phase, c], weight_sems, 0, partner),
         send(node.at[c], nodes.at[phase, c], weight_sems, 1, partner),
+        send(decode, decode_other, weight_sems, 5, partner),
+        send(gain, gains.at[phase], weight_sems, 6, partner),
     ]
 
     def over_tiles(body):
@@ -287,21 +290,23 @@
         copy.wait()
 
 
-def states_and_weights(partial_sums, edge, node):
+def states_and_weights(partial_sums, edge, node, decode, gain):
     owners, nodes, features = partial_sums.shape
     part = partial_sums.reshape(DEPTH, ROWS, CORES, nodes, features)
     edge_half = edge.reshape(2, edge.shape[0] // 2, edge.shape[1])
     node_half = node.reshape(2, node.shape[0] // 2, node.shape[1])
     kind = jnp.bfloat16
-    states, edges, node_weights = pl.pallas_call(
+    states, edges, node_weights, decode_other, gains = pl.pallas_call(
         owner_kernel,
         out_shape=(
             jax.ShapeDtypeStruct((nodes, features), kind),
             jax.ShapeDtypeStruct((2,) + edge_half.shape, kind),
             jax.ShapeDtypeStruct((2,) + node_half.shape, kind),
+            jax.ShapeDtypeStruct(decode.shape, kind),
+            jax.ShapeDtypeStruct((2,) + gain.shape, gain.dtype),
         ),
-        in_specs=[pl.BlockSpec(memory_space=pltpu.VMEM)] * 3,
-        out_specs=[pl.BlockSpec(memory_space=pltpu.VMEM)] * 3,
+        in_specs=[pl.BlockSpec(memory_space=pltpu.VMEM)] * 5,
+        out_specs=[pl.BlockSpec(memory_space=pltpu.VMEM)] * 5,
         scratch_shapes=[
             pltpu.VMEM((DEPTH, ROWS, nodes, features), kind),
             pltpu.VMEM((DEPTH, nodes, features), kind),
@@ -312,14 +317,15 @@
             pltpu.SemaphoreType.DMA((2, DEPTH)),
             pltpu.SemaphoreType.DMA((2, DEPTH)),
             pltpu.SemaphoreType.DMA((2, DEPTH - 1)),
-            pltpu.SemaphoreType.DMA((2, 5)),
+            pltpu.SemaphoreType.DMA((2, 8)),
         ],
         compiler_params=pltpu.CompilerParams(
             collective_id=0, has_side_effects=True, vmem_limit_bytes=40 * 2**20
         ),
         name="sum_to_owners",
-    )(part, edge_half, node_half)
-    return states, edges.reshape((2,) + edge.shape), node_weights.reshape((2,) + node.shape)
+    )(part, edge_half, node_half, decode, gain)
+    edges, node_weights = edges.reshape((2,) + edge.shape), node_weights.reshape((2,) + node.shape)
+    return states, edges, node_weights, decode_other, gains
 
 
 def gather_kernel(mine, everyone, own_sem, z_sems, y_sems, core_sems):
@@ -373,13 +379,46 @@
     )(mapped)
 
 
+def sum_rows_kernel(send_blocks, rows, targets, sums):
+    owner = pl.program_id(0)
+    block_size = rows.shape[1]
+    nodes = lax.broadcasted_iota(jnp.int32, (sums.shape[1], block_size), 0)
+    total = jnp.zeros(sums.shape[1:], jnp.float32)
+    for slot in range(targets.shape[2] // block_size):
+        wanted = targets[0, :, slot * block_size : (slot + 1) * block_size]
+        hot = (nodes == wanted).astype(jnp.float32).astype(jnp.bfloat16)
+        block = rows[send_blocks[owner, slot]]
+        total = total + jnp.dot(hot, block, preferred_element_type=jnp.float32)
+    sums[0] = total.astype(jnp.bfloat16)
+
+
+def sum_rows(rows, send_blocks, targets, node_count):
+    owners, width = targets.shape
+    features = rows.shape[2]
+    return pl.pallas_call(
+        sum_rows_kernel,
+        out_shape=jax.ShapeDtypeStruct((owners, node_count, features), jnp.bfloat16),
+        grid_spec=pltpu.PrefetchScalarGridSpec(
+            num_scalar_prefetch=1,
+            grid=(owners,),
+            in_specs=[
+                pl.BlockSpec(rows.shape, lambda o, blocks: (0, 0, 0)),
+                pl.BlockSpec((1, 1, width), lambda o, blocks: (o, 0, 0)),
+            ],
+            out_specs=pl.BlockSpec((1, node_count, features), lambda o, blocks: (o, 0, 0)),
+        ),
+        compiler_params=pltpu.CompilerParams(vmem_limit_bytes=24 * 2**20),
+        name="sum_rows",
+    )(send_blocks, rows, targets[:, None, :])
+
+
 def silu(values):
     half = 0.5 * values
     return half + half * jnp.tanh(half)
 
 
 def sections_kernel(
-    first, edges, nodes, gains, source_hot, live, send_hot, decode, mapped,
+    first, edges, nodes, gains, source_hot, live, send_hot, decode, decode_other, mapped,
     states, outgoing, incoming, table, dest, mixed, running, send_sems, recv_sems,
 ):
     phase, me = lax.axis_index("phase"), lax.axis_index("shard")
@@ -436,17 +475,21 @@
         value = mixed[...] + dot(running[...].astype(jnp.bfloat16), nodes[layer, features:, :])
         value = gains[layer] * layer_norm(silu(value))
         states[...] = (states[...].astype(jnp.float32) + value).astype(jnp.bfloat16)
-    mapped[...] = dot(states[...], decode[...]).astype(jnp.bfloat16)
-
-
-def run_sections(states, edges, nodes, gains, source_hot, live, send_hot, decode, owners):
+    width = decode.shape[1]
+    mapped[:, :width] = dot(states[...], decode[...]).astype(jnp.bfloat16)
+    mapped[:, width:] = dot(states[...], decode_other[...]).astype(jnp.bfloat16)
+
+
+def run_sections(
+    states, edges, nodes, gains, source_hot, live, send_hot, decode, decode_other, owners
+):
     node_count, features = states.shape
     lanes = features // 4
     kind = jnp.bfloat16
     return pl.pallas_call(
         sections_kernel,
         out_shape=jax.ShapeDtypeStruct((node_count, features), kind),
-        in_specs=[pl.BlockSpec(memory_space=pltpu.VMEM)] * 8,
+        in_specs=[pl.BlockSpec(memory_space=pltpu.VMEM)] * 9,
         out_specs=pl.BlockSpec(memory_space=pltpu.VMEM),
         scratch_shapes=[
             pltpu.VMEM((node_count, features), kind),
@@ -463,7 +506,7 @@
             collective_id=2, has_side_effects=True, vmem_limit_bytes=40 * 2**20
         ),
         name="run_sections",
-    )(states, edges, nodes, gains, source_hot, live, send_hot, decode)
+    )(states, edges, nodes, gains, source_hot, live, send_hot, decode, decode_other)
 
 
 def on_device_batches(
@@ -510,18 +553,12 @@
     slot_live = jnp.arange(capacity, dtype=jnp.int32)[None, :] < encode_count[0][:, None]
     live = jnp.repeat(slot_live, block_size, axis=1)
     targets = jnp.where(live, targets, -1)
-    hot = targets[:, None, :] == jnp.arange(node_count, dtype=jnp.int32)[None, :, None]
-    picked = rows[send_blocks].reshape(owners, capacity * block_size, features)
-    partial_sums = jnp.einsum(
-        "onr,orc->onc", hot.astype(jnp.bfloat16), picked, preferred_element_type=jnp.float32
-    ).astype(jnp.bfloat16)
-    states, edges, nodes = states_and_weights(partial_sums, edge_weight[0], node_weight[0])
-    other_gain = swap(node_gain[0])
-    first = phase_index == 0
-    gains = jnp.stack(
-        [jnp.where(first, node_gain[0], other_gain), jnp.where(first, other_gain, node_gain[0])]
-    )[:, None, :]
-    decode_all = jnp.concatenate([decode_weight, swap(decode_weight)], axis=1)
+    partial_sums = sum_rows(rows, send_blocks, targets, node_count)
+
+    states, edges, nodes, decode_other, gains = states_and_weights(
+        partial_sums, edge_weight[0], node_weight[0], decode_weight, node_gain
+    )
+    states, output_weight = lax.optimization_barrier((states, output_weight))
     output_all = jnp.concatenate([output_weight, swap(output_weight)], axis=0)
 
     neighbour = mesh_neighbour.T
@@ -534,7 +571,16 @@
     send_nodes = jnp.tile(mesh_send[0][:, None, :], (1, 4, 1)).reshape(-1)
     send_hot = send_nodes[:, None] == jnp.arange(node_count, dtype=jnp.int32)
     mapped = run_sections(
-        states, edges, nodes, gains, source_hot, live, send_hot.astype(jnp.bfloat16), decode_all, owners
+        states,
+        edges,
+        nodes,
+        gains,
+        source_hot,
+        live,
+        send_hot.astype(jnp.bfloat16),
+        decode_weight,
+        decode_other,
+        owners,
     )
 
     gathered = gather_nodes(mapped).reshape(owners, node_count // block_size, block_size, features)

time: 158 us -> 145 us (0.918)
  local copies, waits for them, and re-layouts: 20.1 us -> 13 us
  Pallas kernels: 95.2 us -> 102 us
  matrix products: 16.7 us -> 12.3 us
  waiting for transfers between devices: 9.42 us -> 5.64 us
  other arithmetic: 4.98 us -> 2.18 us
  starting transfers between devices: 11 us -> 8.99 us
    pallas_call x0 -> x1, Pallas kernels: none -> 6.35 us  [sum_rows(): pl.pallas_call(sum_rows_kernel, out_shape=jax.ShapeDtypeStruct((owners, n...]
    gather x1 -> x0, local copies, waits for them, and re-layouts: 6.14 us -> none  [on_device_batches(): picked = rows[send_blocks].reshape(owners, capacity * block_size, features)]
    ppermute x5 -> x3, waiting for transfers between devices: 9.42 us -> 3.8 us  [swap(): return lax.ppermute(value, 'phase', [(0, 1), (1, 0)])]
    dot_general x1 -> x0, matrix products: 5.26 us -> none  [on_device_batches(): jnp.einsum('onr,orc->onc', hot.astype(jnp.bfloat16), picked, preferred_el...]
    ppermute x5 -> x3, starting transfers between devices: 4.67 us -> 2.7 us  [swap(): return lax.ppermute(value, 'phase', [(0, 1), (1, 0)])]
    all_to_all x1, waiting for transfers between devices: 0.01 us -> 1.84 us  [on_device_batches(): lax.all_to_all(tables, 'shard', split_axis=0, concat_axis=0, tiled=True)]
    concatenate x1 -> x0, other arithmetic: 1.84 us -> none  [on_device_batches(): decode_all = jnp.concatenate([decode_weight, swap(decode_weight)], axis=1)]
  transfers between devices with their start and end apart: 6 -> 4, of which waited for: 2 -> 3; matrix products, arithmetic and copies ran while one was open for 8% -> 8% of each run, Pallas kernels for 0% -> 39%
where the time goes in v4:
time: 145 us; the launch traced here: 144 us
  Pallas kernels  102 us (70%)
  local copies, waits for them, and re-layouts  13 us (9%)
  matrix products  12.3 us (8%)
  starting transfers between devices  8.99 us (6%)
  waiting for transfers between devices  5.64 us (4%)
  other arithmetic  2.18 us (2%)
    pallas_call x1, Pallas kernels, states_and_weights(): pl.pallas_call(owner_kernel, out_shape=(jax.ShapeDtypeStruct((nodes, feat...  38.5 us
    pallas_call x1, Pallas kernels, gather_nodes(): pl.pallas_call(gather_kernel, out_shape=jax.ShapeDtypeStruct((DEPTH, ROWS...  37.6 us
    pallas_call x1, Pallas kernels, run_sections(): pl.pallas_call(sections_kernel, out_shape=jax.ShapeDtypeStruct((node_coun...  19.1 us
    dot_general x2, matrix products, outputs(): return jnp.dot(hidden, output_all, preferred_element_type=jnp.float32)  7.65 us
    pallas_call x1, Pallas kernels, sum_rows(): pl.pallas_call(sum_rows_kernel, out_shape=jax.ShapeDtypeStruct((owners, n...  6.35 us
    all_to_all x1, starting transfers between devices, on_device_batches(): lax.all_to_all(tables, 'shard', split_axis=0, concat_axis=0, tiled=True)  6.29 us
    unnamed x34, local copies, waits for them, and re-layouts  3.91 us
    ppermute x3, waiting for transfers between devices, swap(): return lax.ppermute(value, 'phase', [(0, 1), (1, 0)])  3.8 us
  transfers between devices with their start and end apart: 4, of which 3 were waited for; matrix products, arithmetic and copies ran while one was open for 8% of the time, Pallas kernels for 39%

profile of v4, /device:TPU:10, one launch (start us, length us, event | category | flops | bytes accessed | tf_op | source)
XLA Modules:
  0.0 144.0 jit_solution(6565465396871367290)
XLA Ops:
  0.0 0.0 copy-start
  0.0 1.2 copy-done
  1.2 2.0 %multiply_convert_fusion = bf16[2,8,64,512]{3,2,1,0:T(8,128)(2,1)S(1)} fusion(bf16[2,8,64,512]{3,2,1,0:T(8,128)(2,1)S(1)} %copy-done, bf16[512,512]{1,0:T(8,128)(2,1)} %param.16), kind=kOutput, calls=%fused_computation.15 | convolution fusion | flops 539492352 | bytes 2621440 | tf_op jit(solution)/shard_map/mgrd,dc->mgrc/dot_general | solution.py:538
  3.3 0.0 copy-start.9
  3.3 0.0 copy-start.13
  3.3 0.0 copy-start.14
  3.3 0.0 copy-start.8
  3.3 0.0 copy-start.11
  3.3 0.0 copy-start.12
  3.3 1.1 dynamic-slice_bitcast_fusion.1
  4.4 0.5 collective-permute-start
  5.0 0.1 copy.39
  5.1 0.6 copy.40
  5.7 6.3 %all-to-all-start = ((s32[16,1,385]{2,1,0:T(1,128)}), s32[16,1,385]{2,1,0:T(1,128)S(1)}, u32[]{:S(2)}, u32[]{:S(2)}) async-start(s32[16,1,385]{2,1,0:T(1,128)} %copy.40), calls=%async_computation | async-start | bytes 65536 | tf_op jit(solution)/shard_map/all_to_all | solution.py:548
  12.0 0.1 iota_compare_fusion.7
  12.1 0.0 copy-done.8
  12.1 0.0 copy-done.11
  12.1 0.1 copy.43
  12.2 0.1 tile.11
  12.3 0.1 fusion.12.send_hot
  12.5 0.5 compare_convert_fusion.source_hot
  13.0 0.1 broadcast_in_dim.54
  13.1 0.0 copy-done.12
  13.1 0.1 copy.50
  13.2 1.3 copy.44.live
  14.6 0.0 copy-done.10
  14.6 0.1 reshape.85
  14.7 0.1 dynamic-slice_reduce_fusion.5
  14.8 0.1 eq.133
  14.8 0.1 eq.137
  14.9 0.1 eq.141
  15.0 0.1 eq.152
  15.1 0.1 eq.156
  15.2 0.1 eq.160
  15.2 1.8 %all-to-all-done = s32[16,1,385]{2,1,0:T(1,128)S(1)} async-done(((s32[16,1,385]{2,1,0:T(1,128)}), s32[16,1,385]{2,1,0:T(1,128)S(1)}, u32[]{:S(2)}, u32[]{:S(2)}) %all-to-all-start) | async-done | bytes 24672 | tf_op jit(solution)/shard_map/all_to_all | solution.py:548
  17.1 0.1 reshape.87
  17.2 0.1 rev.3
  17.3 0.1 reshape.88
  17.5 0.9 collective-permute-done
  18.4 1.3 pad_maximum_fusion.rows
  19.7 0.0 copy-start.3
  19.7 0.0 copy-start.4
  19.7 0.0 copy-start.5
  19.7 0.0 copy-start.6
  19.7 6.4 %sum_rows.1 = bf16[16,256,512]{2,1,0:T(8,128)(2,1)S(1)} custom-call(s32[16,3]{1,0:T(8,128)S(1)} %bitcast.57, bf16[8,128,512]{2,1,0:T(8,128)(2,1)S(1)} %pad_maximum_fusion.rows, s32[16,1,384]{2,1,0:T(1,128)S(1)} %broadcast_select_fusion.1.targets), custom_call_target="tpu_custom_call" | custom-call | tf_op jit(solution)/shard_map/sum_rows/pallas_call | solution.py:398
  26.1 0.0 copy-start.7
  26.1 0.0 copy-start.2
  26.1 38.5 %sum_to_owners.1 = (bf16[256,512]{1,0:T(8,128)(2,1)S(1)}, bf16[2,2,256,1024]{3,2,1,0:T(8,128)(2,1)S(1)}, bf16[2,2,512,512]{3,2,1,0:T(8,128)(2,1)S(1)}, bf16[512,256]{1,0:T(8,128)(2,1)S(1)}, f32[2,1,512]{2,1,0:T(1,128)S(1)}) custom-call(bf16[4,2,2,256,512]{4,3,2,1,0:T(8,128)(2,1)S(1)} %bitcast.51, bf16[2,256,1024]{2,1,0:T(8,128)(2,1)S(1)} %bitcast.55, ...), custom_call_target="tpu_custom_call" | custom-call | tf_op jit(solution)/shard_map/sum_to_owners/pallas_call | solution.py:299
  64.7 0.0 copy-done.7
  64.7 0.7 collective-permute-start.1
  65.3 0.1 fusion.20
  65.4 19.1 %run_sections.1.mine = bf16[256,512]{1,0:T(8,128)(2,1)S(1)} custom-call(bf16[256,512]{1,0:T(8,128)(2,1)S(1)} %get-tuple-element.13.first, bf16[2,512,1024]{2,1,0:T(8,128)(2,1)S(1)} %bitcast.53, bf16[2,1024,512]{2,1,0:T(8,128)(2,1)S(1)} %bitcast.54, f32[2,1,512]{2,1,0:T(1,128)S(1)} %get-tuple-element.16.gains, ...), custom_call_target="tpu_custom_call" | custom-call | tf_op jit(solution)/shard_map/run_sections/pallas_call | solution.py:489
  84.5 37.6 %gather_nodes.1 = bf16[4,2,2,256,512]{4,3,2,1,0:T(8,128)(2,1)S(1)} custom-call(bf16[256,512]{1,0:T(8,128)(2,1)S(1)} %run_sections.1.mine), custom_call_target="tpu_custom_call" | custom-call | tf_op jit(solution)/shard_map/gather_nodes/pallas_call | solution.py:364
  122.2 1.9 %copy-done.1 = bf16[4,2,2,256,512]{4,3,2,1,0:T(8,128)(2,1)} copy-done((bf16[4,2,2,256,512]{4,3,2,1,0:T(8,128)(2,1)}, bf16[4,2,2,256,512]{4,3,2,1,0:T(8,128)(2,1)S(1)}, u32[]{:S(2)}) %copy-start.1) | copy-done | bytes 4194328
  124.1 2.9 %gather_fusion = bf16[16,128,512]{2,1,0:T(8,128)(2,1)S(1)} fusion(bf16[16,2,128,512]{3,2,1,0:T(8,128)(2,1)} %bitcast.52, s32[16]{0:T(128)S(1)} %fusion.20), kind=kCustom, calls=%fused_computation | custom fusion | bytes 4194432 | tf_op jit(solution)/shard_map/gather | solution.py:587
  127.0 0.7 constant_dynamic-update-slice_fusion.1
  127.6 0.0 collective-permute-done.1
  127.6 1.6 %constant_dynamic-update-slice_fusion = bf16[512,227]{0,1:T(8,128)(2,1)} fusion(bf16[512,227]{0,1:T(8,128)(2,1)} %constant_dynamic-update-slice_fusion.1, bf16[256,227]{0,1:T(8,128)(2,1)} %collective-permute-done.1), kind=kLoop, calls=%fused_computation.46 | loop fusion | bytes 237568 | tf_op jit(solution)/shard_map/concatenate | solution.py:562
  129.2 3.8 %convolution_convert_fusion = bf16[512,227]{0,1:T(8,128)(2,1)} fusion(bf16[512,227]{0,1:T(8,128)(2,1)} %constant_dynamic-update-slice_fusion, bf16[2048,512]{1,0:T(8,128)(2,1)S(1)} %bitcast.58, s32[512]{0:T(512)S(1)} %eq.160, s32[512]{0:T(512)S(1)} %eq.156, s32[512]{0:T(512)S(1)} %eq.152), kind=kOutput, calls=%fused_computation.19 | convolution fusion | flops 1203619328 | bytes 2568192 | tf_op jit(solution)/shard_map/dot_general | solution.py:596
  133.0 1.5 %collective-permute-start.2 = (bf16[512,227]{0,1:T(8,128)(2,1)}, bf16[512,227]{0,1:T(8,128)(2,1)S(1)}, u32[]{:S(2)}, u32[]{:S(2)}) collective-permute-start(bf16[512,227]{0,1:T(8,128)(2,1)} %convolution_convert_fusion), channel_id=1, source_target_pairs={{0,16},{16,0},{1,17},{17,1},{2,18},{18,2},{3,19},{19,3},{4,20},{20... | collective-permute-start | bytes 697352 | tf_op jit(solution)/shard_map/ppermute | solution.py:165
  134.5 3.9 %fusion.8 = f32[512,227]{1,0:T(8,128)} fusion(bf16[512,227]{0,1:T(8,128)(2,1)} %constant_dynamic-update-slice_fusion, bf16[2048,512]{1,0:T(8,128)(2,1)S(1)} %bitcast.59, s32[512]{0:T(512)S(1)} %eq.141, s32[512]{0:T(512)S(1)} %eq.137, s32[512]{0:T(512)S(1)} %eq.133), kind=kOutput, calls=%fused_computation.24 | convolution fusion | flops 1203503104 | bytes 2800640 | tf_op jit(solution)/shard_map/dot_general | solution.py:596
  138.3 2.9 %collective-permute-done.2 = bf16[512,227]{0,1:T(8,128)(2,1)S(1)} collective-permute-done((bf16[512,227]{0,1:T(8,128)(2,1)}, bf16[512,227]{0,1:T(8,128)(2,1)S(1)}, u32[]{:S(2)}, u32[]{:S(2)}) %collective-permute-start.2) | collective-permute-done | bytes 232480 | tf_op jit(solution)/shard_map/ppermute | solution.py:165
  141.2 0.1 copy.46
  141.4 2.6 %select_add_fusion = f32[2,8,64,227]{3,2,1,0:T(8,128)} fusion(f32[8,64,227]{2,1,0:T(8,128)S(1)} %bitcast.60, f32[8,64,227]{2,1,0:T(8,128)} %bitcast.61, pred[2]{0:T(512)(128)(4,1)S(1)} %iota_compare_fusion.8, bf16[2,8,64,512]{3,2,1,0:T(8,128)(2,1)S(1)} %copy-done, bf16[512,227]{0,1:T(8,128)(2,1)} %param.29), kind=kOutput, calls=%fused_computation.21 | convolution fusion | flops 238491648 | bytes 3140610 | tf_op jit(solution)/shard_map/mgrd,do->mgro/dot_general | solution.py:601
  (24 shorter events, 0.2 us)
Async XLA Ops:
  0.0 1.2 copy-start
  3.3 1.7 %copy-start.9 = (s32[1,16,3,128]{3,1,2,0:T(8,128)S(1)}, s32[1,16,3,128]{3,1,2,0:T(8,128)}, u32[]{:S(2)}) copy-start(s32[1,16,3,128]{3,1,2,0:T(8,128)} %param.19) | copy-start | bytes 73732
  3.3 1.7 %copy-start.13 = (s32[1,16,1]{1,2,0:T(1,128)S(1)}, s32[1,16,1]{1,2,0:T(1,128)}, u32[]{:S(2)}) copy-start(s32[1,16,1]{1,2,0:T(1,128)} %param.26) | copy-start | bytes 196
  3.3 8.7 %copy-start.14 = (s32[1,16]{1,0:T(1,128)S(1)}, s32[1,16]{1,0:T(1,128)}, u32[]{:S(2)}) copy-start(s32[1,16]{1,0:T(1,128)} %param.18) | copy-start | bytes 196
  3.3 8.8 %copy-start.8 = (s32[256,8]{0,1:T(8,128)S(1)}, s32[256,8]{0,1:T(8,128)}, u32[]{:S(2)}) copy-start(s32[256,8]{0,1:T(8,128)} %param.24) | copy-start | bytes 24580
  3.3 8.8 %copy-start.11 = (s32[1,16,4]{1,2,0:T(4,128)S(1)}, s32[1,16,4]{1,2,0:T(4,128)}, u32[]{:S(2)}) copy-start(s32[1,16,4]{1,2,0:T(4,128)} %param.23) | copy-start | bytes 772
  3.3 9.8 %copy-start.12 = (s32[1,16,3]{1,0,2:T(1,128)S(1)}, s32[1,16,3]{1,0,2:T(1,128)}, u32[]{:S(2)}) copy-start(s32[1,16,3]{1,0,2:T(1,128)} %param.17) | copy-start | bytes 580
  4.4 10.2 %copy-start.10 = (s32[3,1024]{1,0:T(4,128)S(1)}, s32[3,1024]{1,0:T(4,128)}, u32[]{:S(2)}) copy-start(s32[3,1024]{1,0:T(4,128)} %param.27) | copy-start | bytes 36868
  4.4 14.0 %collective-permute-start = (bf16[8,64,512]{2,1,0:T(8,128)(2,1)}, bf16[8,64,512]{2,1,0:T(8,128)(2,1)}, u32[]{:S(2)}, u32[]{:S(2)}) collective-permute-start(bf16[8,64,512]{2,1,0:T(8,128)(2,1)} %get-tuple-element.26), channel_id=1, source_target_pairs={{0,16},{16,0},{1,17},{17,1},{2,18},{18,2},{3,19},{19,3},{4,20},{20... | collective-permute-start | bytes 1572872 | tf_op jit(solution)/shard_map/ppermute | solution.py:165
  5.7 11.3 %all-to-all-start = ((s32[16,1,385]{2,1,0:T(1,128)}), s32[16,1,385]{2,1,0:T(1,128)S(1)}, u32[]{:S(2)}, u32[]{:S(2)}) async-start(s32[16,1,385]{2,1,0:T(1,128)} %copy.40), calls=%async_computation | async-start | bytes 65536 | tf_op jit(solution)/shard_map/all_to_all | solution.py:548
  19.7 6.4 %copy-start.3 = (bf16[1,512,1024]{2,1,0:T(8,128)(2,1)S(1)}, bf16[1,512,1024]{2,1,0:T(8,128)(2,1)}, u32[]{:S(2)}) copy-start(bf16[1,512,1024]{2,1,0:T(8,128)(2,1)} %param.20) | copy-start | bytes 3145732
  19.7 6.4 %copy-start.4 = (bf16[1,1024,512]{2,1,0:T(8,128)(2,1)S(1)}, bf16[1,1024,512]{2,1,0:T(8,128)(2,1)}, u32[]{:S(2)}) copy-start(bf16[1,1024,512]{2,1,0:T(8,128)(2,1)} %param.21) | copy-start | bytes 3145732
  19.7 6.4 %copy-start.5 = (bf16[512,256]{1,0:T(8,128)(2,1)S(1)}, bf16[512,256]{1,0:T(8,128)(2,1)}, u32[]{:S(2)}) copy-start(bf16[512,256]{1,0:T(8,128)(2,1)} %decode.3) | copy-start | bytes 786436
  19.7 6.4 %copy-start.6 = (f32[1,512]{1,0:T(1,128)S(1)}, f32[1,512]{1,0:T(1,128)}, u32[]{:S(2)}) copy-start(f32[1,512]{1,0:T(1,128)} %gain.1) | copy-start | bytes 6148
  26.1 38.5 %copy-start.7 = (bf16[256,227]{0,1:T(8,128)(2,1)S(1)}, bf16[256,227]{0,1:T(8,128)(2,1)}, u32[]{:S(2)}) copy-start(bf16[256,227]{0,1:T(8,128)(2,1)} %param.28) | copy-start | bytes 348676
  26.1 39.3 %copy-start.2 = (f32[8,256,1]{2,1,0:T(8,128)S(1)}, f32[8,256,1]{2,1,0:T(8,128)}, u32[]{:S(2)}) copy-start(f32[8,256,1]{2,1,0:T(8,128)} %copy.44.live) | copy-start | bytes 24580
  64.7 62.9 %collective-permute-start.1 = (bf16[256,227]{0,1:T(8,128)(2,1)S(1)}, bf16[256,227]{0,1:T(8,128)(2,1)}, u32[]{:S(2)}, u32[]{:S(2)}) collective-permute-start(bf16[256,227]{0,1:T(8,128)(2,1)S(1)} %copy-done.7), channel_id=1, source_target_pairs={{0,16},{16,0},{1,17},{17,1},{2,18},{18,2},{3,19},{19,3},{4,20},{20... | collective-permute-start | bytes 348680 | tf_op jit(solution)/shard_map/ppermute | solution.py:165
  122.1 1.9 %copy-start.1 = (bf16[4,2,2,256,512]{4,3,2,1,0:T(8,128)(2,1)}, bf16[4,2,2,256,512]{4,3,2,1,0:T(8,128)(2,1)S(1)}, u32[]{:S(2)}) copy-start(bf16[4,2,2,256,512]{4,3,2,1,0:T(8,128)(2,1)S(1)} %gather_nodes.1) | copy-start | bytes 12582916
  133.0 8.3 %collective-permute-start.2 = (bf16[512,227]{0,1:T(8,128)(2,1)}, bf16[512,227]{0,1:T(8,128)(2,1)S(1)}, u32[]{:S(2)}, u32[]{:S(2)}) collective-permute-start(bf16[512,227]{0,1:T(8,128)(2,1)} %convolution_convert_fusion), channel_id=1, source_target_pairs={{0,16},{16,0},{1,17},{17,1},{2,18},{18,2},{3,19},{19,3},{4,20},{20... | collective-permute-start | bytes 697352 | tf_op jit(solution)/shard_map/ppermute | solution.py:165

commit v5 on v4

--- a/solution.py
+++ b/solution.py
@@ -166,7 +166,7 @@
 
 
 MESH_ID = pl.DeviceIdType.MESH
-PIECE = 128
+PIECE = 64
 DEPTH, ROWS, CORES = 4, 2, 2
 
 
@@ -559,7 +559,7 @@
         partial_sums, edge_weight[0], node_weight[0], decode_weight, node_gain
     )
     states, output_weight = lax.optimization_barrier((states, output_weight))
-    output_all = jnp.concatenate([output_weight, swap(output_weight)], axis=0)
+    output_other, width = swap(output_weight), output_weight.shape[0]
 
     neighbour = mesh_neighbour.T
     packed = jnp.arange(owners * 16, dtype=jnp.int32)
@@ -593,7 +593,10 @@
         counts = sum((indices[e][:, None] == ids).astype(jnp.float32) for e in range(3))
         summed = jnp.dot(counts.astype(jnp.bfloat16), chosen, preferred_element_type=jnp.float32)
         hidden = jax.nn.silu(summed).astype(jnp.bfloat16)
-        return jnp.dot(hidden, output_all, preferred_element_type=jnp.float32)
+        result = jnp.dot(hidden[:, :width], output_weight, preferred_element_type=jnp.float32)
+        return result + jnp.dot(
+            hidden[:, width:], output_other, preferred_element_type=jnp.float32
+        )
 
     leaving = outputs(1 - phase_index).astype(jnp.bfloat16)
     arriving = swap(leaving).astype(jnp.float32)

time: 145 us -> 141 us (0.972)
  matrix products: 12.3 us -> 9.1 us
  waiting for transfers between devices: 5.64 us -> 8.5 us
  Pallas kernels: 102 us -> 99.6 us
  local copies, waits for them, and re-layouts: 13 us -> 11 us
    ppermute x3, waiting for transfers between devices: 3.8 us -> 6.65 us  [swap(): return lax.ppermute(value, 'phase', [(0, 1), (1, 0)])]
    pallas_call x1, Pallas kernels: 37.6 us -> 35.6 us  [gather_nodes(): pl.pallas_call(gather_kernel, out_shape=jax.ShapeDtypeStruct((DEPTH, ROWS...]
    dot_general x2 -> x6, matrix products: 7.65 us -> 5.63 us  [the longest x2 4.61 us: outputs(): jnp.dot(counts.astype(jnp.bfloat16), chosen, preferred_element_type=jnp.f...]
    concatenate x1 -> x0, local copies, waits for them, and re-layouts: 1.56 us -> none  [on_device_batches(): output_all = jnp.concatenate([output_weight, swap(output_weight)], axis=0)]
    unnamed x34 -> x35, local copies, waits for them, and re-layouts: 3.91 us -> 3.27 us
  transfers between devices with their start and end apart: 4 -> 4, of which waited for: 3 -> 3; matrix products, arithmetic and copies ran while one was open for 8% -> 9% of each run, Pallas kernels for 39% -> 0%
where the time goes in v5:
time: 141 us; the launch traced here: 140 us
  Pallas kernels  99.6 us (71%)
  local copies, waits for them, and re-layouts  11 us (8%)
  matrix products  9.1 us (6%)
  starting transfers between devices  8.92 us (6%)
  waiting for transfers between devices  8.5 us (6%)
  other arithmetic  2.18 us (2%)
    pallas_call x1, Pallas kernels, states_and_weights(): pl.pallas_call(owner_kernel, out_shape=(jax.ShapeDtypeStruct((nodes, feat...  38.5 us
    pallas_call x1, Pallas kernels, gather_nodes(): pl.pallas_call(gather_kernel, out_shape=jax.ShapeDtypeStruct((DEPTH, ROWS...  35.6 us
    pallas_call x1, Pallas kernels, run_sections(): pl.pallas_call(sections_kernel, out_shape=jax.ShapeDtypeStruct((node_coun...  19.1 us
    ppermute x3, waiting for transfers between devices, swap(): return lax.ppermute(value, 'phase', [(0, 1), (1, 0)])  6.65 us
    pallas_call x1, Pallas kernels, sum_rows(): pl.pallas_call(sum_rows_kernel, out_shape=jax.ShapeDtypeStruct((owners, n...  6.35 us
    all_to_all x1, starting transfers between devices, on_device_batches(): lax.all_to_all(tables, 'shard', split_axis=0, concat_axis=0, tiled=True)  6.29 us
    dot_general x2, matrix products, outputs(): jnp.dot(counts.astype(jnp.bfloat16), chosen, preferred_element_type=jnp.f...  4.61 us
    unnamed x35, local copies, waits for them, and re-layouts  3.27 us
  transfers between devices with their start and end apart: 4, of which 3 were waited for; matrix products, arithmetic and copies ran while one was open for 9% of the time, Pallas kernels for 0%

profile of v5, /device:TPU:10, one launch (start us, length us, event | category | flops | bytes accessed | tf_op | source)
XLA Modules:
  0.0 139.6 jit_solution(9620931665640099495)
XLA Ops:
  0.0 0.0 copy-start
  0.0 1.2 copy-done
  1.2 2.0 %multiply_convert_fusion = bf16[2,8,64,512]{3,2,1,0:T(8,128)(2,1)S(1)} fusion(bf16[2,8,64,512]{3,2,1,0:T(8,128)(2,1)S(1)} %copy-done, bf16[512,512]{1,0:T(8,128)(2,1)} %param.16), kind=kOutput, calls=%fused_computation.15 | convolution fusion | flops 539492352 | bytes 2621440 | tf_op jit(solution)/shard_map/mgrd,dc->mgrc/dot_general | solution.py:538
  3.3 0.0 copy-start.10
  3.3 0.0 copy-start.14
  3.3 0.0 copy-start.15
  3.3 0.0 copy-start.9
  3.3 0.0 copy-start.12
  3.3 0.0 copy-start.13
  3.3 1.1 dynamic-slice_bitcast_fusion.1
  4.4 0.5 collective-permute-start
  5.0 0.1 copy.39
  5.1 0.6 copy.40
  5.7 6.3 %all-to-all-start = ((s32[16,1,385]{2,1,0:T(1,128)}), s32[16,1,385]{2,1,0:T(1,128)S(1)}, u32[]{:S(2)}, u32[]{:S(2)}) async-start(s32[16,1,385]{2,1,0:T(1,128)} %copy.40), calls=%async_computation | async-start | bytes 65536 | tf_op jit(solution)/shard_map/all_to_all | solution.py:548
  12.0 0.1 iota_compare_fusion.7
  12.1 0.0 copy-done.9
  12.1 0.1 copy.43
  12.2 0.1 tile.11
  12.3 0.1 fusion.16.send_hot
  12.5 0.5 compare_convert_fusion.source_hot
  13.0 0.1 broadcast_in_dim.54
  13.1 0.1 copy.49
  13.2 1.3 copy.44.live
  14.6 0.1 reshape.85
  14.7 0.1 dynamic-slice_reduce_fusion.5
  14.8 0.1 eq.133
  14.8 0.1 eq.137
  14.9 0.1 eq.141
  15.0 0.1 eq.152
  15.1 0.1 eq.156
  15.1 0.1 eq.160
  15.2 1.8 %all-to-all-done = s32[16,1,385]{2,1,0:T(1,128)S(1)} async-done(((s32[16,1,385]{2,1,0:T(1,128)}), s32[16,1,385]{2,1,0:T(1,128)S(1)}, u32[]{:S(2)}, u32[]{:S(2)}) %all-to-all-start) | async-done | bytes 24672 | tf_op jit(solution)/shard_map/all_to_all | solution.py:548
  17.1 0.1 reshape.87
  17.2 0.1 rev.3
  17.3 0.1 reshape.88
  17.4 0.1 fusion.24
  17.6 0.8 collective-permute-done
  18.4 1.3 pad_maximum_fusion.rows
  19.7 0.0 copy-start.3
  19.7 0.0 copy-start.4
  19.7 0.0 copy-start.5
  19.7 0.0 copy-start.6
  19.7 6.3 %sum_rows.1 = bf16[16,256,512]{2,1,0:T(8,128)(2,1)S(1)} custom-call(s32[16,3]{1,0:T(8,128)S(1)} %bitcast.59, bf16[8,128,512]{2,1,0:T(8,128)(2,1)S(1)} %pad_maximum_fusion.rows, s32[16,1,384]{2,1,0:T(1,128)S(1)} %broadcast_select_fusion.1.targets), custom_call_target="tpu_custom_call" | custom-call | tf_op jit(solution)/shard_map/sum_rows/pallas_call | solution.py:398
  26.1 0.0 copy-start.2
  26.1 38.5 %sum_to_owners.1 = (bf16[256,512]{1,0:T(8,128)(2,1)S(1)}, bf16[2,2,256,1024]{3,2,1,0:T(8,128)(2,1)S(1)}, bf16[2,2,512,512]{3,2,1,0:T(8,128)(2,1)S(1)}, bf16[512,256]{1,0:T(8,128)(2,1)S(1)}, f32[2,1,512]{2,1,0:T(1,128)S(1)}) custom-call(bf16[4,2,2,256,512]{4,3,2,1,0:T(8,128)(2,1)S(1)} %bitcast.53, bf16[2,256,1024]{2,1,0:T(8,128)(2,1)S(1)} %bitcast.57, ...), custom_call_target="tpu_custom_call" | custom-call | tf_op jit(solution)/shard_map/sum_to_owners/pallas_call | solution.py:299
  64.7 19.1 %run_sections.1.mine = bf16[256,512]{1,0:T(8,128)(2,1)S(1)} custom-call(bf16[256,512]{1,0:T(8,128)(2,1)S(1)} %get-tuple-element.13.first, bf16[2,512,1024]{2,1,0:T(8,128)(2,1)S(1)} %bitcast.55, bf16[2,1024,512]{2,1,0:T(8,128)(2,1)S(1)} %bitcast.56, f32[2,1,512]{2,1,0:T(1,128)S(1)} %get-tuple-element.16.gains, ...), custom_call_target="tpu_custom_call" | custom-call | tf_op jit(solution)/shard_map/run_sections/pallas_call | solution.py:489
  83.8 0.0 copy-start.7
  83.8 35.6 %gather_nodes.1 = bf16[4,2,2,256,512]{4,3,2,1,0:T(8,128)(2,1)S(1)} custom-call(bf16[256,512]{1,0:T(8,128)(2,1)S(1)} %run_sections.1.mine), custom_call_target="tpu_custom_call" | custom-call | tf_op jit(solution)/shard_map/gather_nodes/pallas_call | solution.py:364
  119.4 1.9 %copy-done.1 = bf16[4,2,2,256,512]{4,3,2,1,0:T(8,128)(2,1)} copy-done((bf16[4,2,2,256,512]{4,3,2,1,0:T(8,128)(2,1)}, bf16[4,2,2,256,512]{4,3,2,1,0:T(8,128)(2,1)S(1)}, u32[]{:S(2)}) %copy-start.1) | copy-done | bytes 4194328
  121.3 0.6 collective-permute-start.1
  121.9 2.9 %gather_fusion = bf16[16,128,512]{2,1,0:T(8,128)(2,1)S(1)} fusion(bf16[16,2,128,512]{3,2,1,0:T(8,128)(2,1)} %bitcast.54, s32[16]{0:T(128)S(1)} %fusion.24), kind=kCustom, calls=%fused_computation | custom fusion | bytes 4194432 | tf_op jit(solution)/shard_map/gather | solution.py:587
  124.8 2.3 %multiply_convert_fusion.2 = bf16[512,512]{1,0:T(8,128)(2,1)S(1)} fusion(bf16[2048,512]{1,0:T(8,128)(2,1)S(1)} %bitcast.60, s32[512]{0:T(512)S(1)} %eq.141, s32[512]{0:T(512)S(1)} %eq.137, s32[512]{0:T(512)S(1)} %eq.133), kind=kOutput, calls=%fused_computation.25 | convolution fusion | flops 1084489728 | bytes 2627584 | tf_op jit(solution)/shard_map/dot_general | solution.py:594
  127.1 0.3 fusion.14
  127.4 2.3 %multiply_convert_fusion.1 = bf16[512,512]{1,0:T(8,128)(2,1)S(1)} fusion(bf16[2048,512]{1,0:T(8,128)(2,1)S(1)} %bitcast.61, s32[512]{0:T(512)S(1)} %eq.160, s32[512]{0:T(512)S(1)} %eq.156, s32[512]{0:T(512)S(1)} %eq.152), kind=kOutput, calls=%fused_computation.24 | convolution fusion | flops 1084489728 | bytes 2627584 | tf_op jit(solution)/shard_map/dot_general | solution.py:594
  129.7 0.3 fusion.11
  129.9 0.0 copy-start.8
  129.9 0.0 collective-permute-done.1
  130.0 0.3 fusion.8
  130.2 1.5 %collective-permute-start.2 = (bf16[512,227]{0,1:T(8,128)(2,1)S(1)}, bf16[512,227]{0,1:T(8,128)(2,1)S(1)}, u32[]{:S(2)}, u32[]{:S(2)}) collective-permute-start(bf16[512,227]{0,1:T(8,128)(2,1)S(1)} %fusion.8), channel_id=1, source_target_pairs={{0,16},{16,0},{1,17},{17,1},{2,18},{18,2},{3,19},{19,3},{4,20},{20... | collective-permute-start | bytes 697352 | tf_op jit(solution)/shard_map/ppermute | solution.py:165
  131.7 0.3 convolution_add_fusion.1
  132.0 0.2 copy.45
  132.2 5.9 %collective-permute-done.2 = bf16[512,227]{0,1:T(8,128)(2,1)S(1)} collective-permute-done((bf16[512,227]{0,1:T(8,128)(2,1)S(1)}, bf16[512,227]{0,1:T(8,128)(2,1)S(1)}, u32[]{:S(2)}, u32[]{:S(2)}) %collective-permute-start.2) | collective-permute-done | bytes 232480 | tf_op jit(solution)/shard_map/ppermute | solution.py:165
  138.0 0.1 copy.46
  138.2 1.4 %select_add_fusion = f32[2,8,64,227]{3,2,1,0:T(8,128)} fusion(f32[8,64,227]{2,1,0:T(8,128)S(1)} %bitcast.63, f32[8,64,227]{2,1,0:T(8,128)S(1)} %bitcast.62, pred[2]{0:T(512)(128)(4,1)S(1)} %iota_compare_fusion.8, bf16[2,8,64,512]{3,2,1,0:T(8,128)(2,1)S(1)} %copy-done, bf16[512,227]{0,1:T(8,128)(2,1)S(1)} %copy-done.8), kind=kOutput, calls=%fused_computation.23 | convolution fusion | flops 238491648 | bytes 3140610 | tf_op jit(solution)/shard_map/mgrd,do->mgro/dot_general | solution.py:604
  (29 shorter events, 0.2 us)
Async XLA Ops:
  0.0 1.2 copy-start
  3.3 1.7 %copy-start.10 = (s32[1,16,3,128]{3,1,2,0:T(8,128)S(1)}, s32[1,16,3,128]{3,1,2,0:T(8,128)}, u32[]{:S(2)}) copy-start(s32[1,16,3,128]{3,1,2,0:T(8,128)} %param.19) | copy-start | bytes 73732
  3.3 1.7 %copy-start.14 = (s32[1,16,1]{1,2,0:T(1,128)S(1)}, s32[1,16,1]{1,2,0:T(1,128)}, u32[]{:S(2)}) copy-start(s32[1,16,1]{1,2,0:T(1,128)} %param.26) | copy-start | bytes 196
  3.3 8.7 %copy-start.15 = (s32[1,16]{1,0:T(1,128)S(1)}, s32[1,16]{1,0:T(1,128)}, u32[]{:S(2)}) copy-start(s32[1,16]{1,0:T(1,128)} %param.18) | copy-start | bytes 196
  3.3 8.8 %copy-start.9 = (s32[256,8]{0,1:T(8,128)S(1)}, s32[256,8]{0,1:T(8,128)}, u32[]{:S(2)}) copy-start(s32[256,8]{0,1:T(8,128)} %param.24) | copy-start | bytes 24580
  3.3 8.8 %copy-start.12 = (s32[1,16,4]{1,2,0:T(4,128)S(1)}, s32[1,16,4]{1,2,0:T(4,128)}, u32[]{:S(2)}) copy-start(s32[1,16,4]{1,2,0:T(4,128)} %param.23) | copy-start | bytes 772
  3.3 9.8 %copy-start.13 = (s32[1,16,3]{1,0,2:T(1,128)S(1)}, s32[1,16,3]{1,0,2:T(1,128)}, u32[]{:S(2)}) copy-start(s32[1,16,3]{1,0,2:T(1,128)} %param.17) | copy-start | bytes 580
  4.4 10.2 %copy-start.11 = (s32[3,1024]{1,0:T(4,128)S(1)}, s32[3,1024]{1,0:T(4,128)}, u32[]{:S(2)}) copy-start(s32[3,1024]{1,0:T(4,128)} %param.27) | copy-start | bytes 36868
  4.4 14.0 %collective-permute-start = (bf16[8,64,512]{2,1,0:T(8,128)(2,1)}, bf16[8,64,512]{2,1,0:T(8,128)(2,1)}, u32[]{:S(2)}, u32[]{:S(2)}) collective-permute-start(bf16[8,64,512]{2,1,0:T(8,128)(2,1)} %get-tuple-element.26), channel_id=1, source_target_pairs={{0,16},{16,0},{1,17},{17,1},{2,18},{18,2},{3,19},{19,3},{4,20},{20... | collective-permute-start | bytes 1572872 | tf_op jit(solution)/shard_map/ppermute | solution.py:165
  5.7 11.3 %all-to-all-start = ((s32[16,1,385]{2,1,0:T(1,128)}), s32[16,1,385]{2,1,0:T(1,128)S(1)}, u32[]{:S(2)}, u32[]{:S(2)}) async-start(s32[16,1,385]{2,1,0:T(1,128)} %copy.40), calls=%async_computation | async-start | bytes 65536 | tf_op jit(solution)/shard_map/all_to_all | solution.py:548
  19.7 6.4 %copy-start.3 = (bf16[1,512,1024]{2,1,0:T(8,128)(2,1)S(1)}, bf16[1,512,1024]{2,1,0:T(8,128)(2,1)}, u32[]{:S(2)}) copy-start(bf16[1,512,1024]{2,1,0:T(8,128)(2,1)} %param.20) | copy-start | bytes 3145732
  19.7 6.4 %copy-start.4 = (bf16[1,1024,512]{2,1,0:T(8,128)(2,1)S(1)}, bf16[1,1024,512]{2,1,0:T(8,128)(2,1)}, u32[]{:S(2)}) copy-start(bf16[1,1024,512]{2,1,0:T(8,128)(2,1)} %param.21) | copy-start | bytes 3145732
  19.7 6.4 %copy-start.5 = (bf16[512,256]{1,0:T(8,128)(2,1)S(1)}, bf16[512,256]{1,0:T(8,128)(2,1)}, u32[]{:S(2)}) copy-start(bf16[512,256]{1,0:T(8,128)(2,1)} %decode.3) | copy-start | bytes 786436
  19.7 6.4 %copy-start.6 = (f32[1,512]{1,0:T(1,128)S(1)}, f32[1,512]{1,0:T(1,128)}, u32[]{:S(2)}) copy-start(f32[1,512]{1,0:T(1,128)} %gain.1) | copy-start | bytes 6148
  26.1 38.5 %copy-start.2 = (f32[8,256,1]{2,1,0:T(8,128)S(1)}, f32[8,256,1]{2,1,0:T(8,128)}, u32[]{:S(2)}) copy-start(f32[8,256,1]{2,1,0:T(8,128)} %copy.44.live) | copy-start | bytes 24580
  83.8 37.5 %copy-start.7 = (bf16[256,227]{0,1:T(8,128)(2,1)S(1)}, bf16[256,227]{0,1:T(8,128)(2,1)}, u32[]{:S(2)}) copy-start(bf16[256,227]{0,1:T(8,128)(2,1)} %param.28) | copy-start | bytes 348676
  119.4 1.9 %copy-start.1 = (bf16[4,2,2,256,512]{4,3,2,1,0:T(8,128)(2,1)}, bf16[4,2,2,256,512]{4,3,2,1,0:T(8,128)(2,1)S(1)}, u32[]{:S(2)}) copy-start(bf16[4,2,2,256,512]{4,3,2,1,0:T(8,128)(2,1)S(1)} %gather_nodes.1) | copy-start | bytes 12582916
  121.3 8.6 %collective-permute-start.1 = (bf16[256,227]{0,1:T(8,128)(2,1)S(1)}, bf16[256,227]{0,1:T(8,128)(2,1)S(1)}, u32[]{:S(2)}, u32[]{:S(2)}) collective-permute-start(bf16[256,227]{0,1:T(8,128)(2,1)S(1)} %copy-done.7), channel_id=1, source_target_pairs={{0,16},{16,0},{1,17},{17,1},{2,18},{18,2},{3,19},{19,3},{4,20},{20... | collective-permute-start | bytes 348680 | tf_op jit(solution)/shard_map/ppermute | solution.py:165
  129.9 8.3 %copy-start.8 = (bf16[512,227]{0,1:T(8,128)(2,1)S(1)}, bf16[512,227]{0,1:T(8,128)(2,1)}, u32[]{:S(2)}) copy-start(bf16[512,227]{0,1:T(8,128)(2,1)} %param.29) | copy-start | bytes 697348
  130.2 7.8 %collective-permute-start.2 = (bf16[512,227]{0,1:T(8,128)(2,1)S(1)}, bf16[512,227]{0,1:T(8,128)(2,1)S(1)}, u32[]{:S(2)}, u32[]{:S(2)}) collective-permute-start(bf16[512,227]{0,1:T(8,128)(2,1)S(1)} %fusion.8), channel_id=1, source_target_pairs={{0,16},{16,0},{1,17},{17,1},{2,18},{18,2},{3,19},{19,3},{4,20},{20... | collective-permute-start | bytes 697352 | tf_op jit(solution)/shard_map/ppermute | solution.py:165
